TPU v7x, 256 devices: a whole 4x4x8 slice. The times are simulated.
256 devices in a mesh: grp: 8 (over y, core), clu: 32 (over z, x).
Axes of the slice: x: 4, y: 4, z: 8, core: 2. Of those that a mesh axis runs over, the one named last changes fastest.
Arguments:
- near_blocks: bfloat16 [2048, 6, 256, 256], P(('grp', 'clu')), may hold values from -6 to 6
- diag_blocks: bfloat16 [2048, 256, 256], P(('grp', 'clu')), may hold values from -6 to 6
- bases: bfloat16 [2048, 256, 256], P(('grp', 'clu')), may hold values from -0.375 to 0.375
- diag_inverses: float32 [2048, 128, 128], P(('grp', 'clu')), may hold values from -0.5 to 0.5
- col_device: int32 [2048, 6], P(('grp', 'clu')), may hold values from 0 to 31, all different within a row; in each aligned block of 8 rows (0 to 7, 8 to 15, ...) at most 2 rows name the same one
- col_local: int32 [2048, 6], P(('grp', 'clu')), may hold values from 0 to 7
- ranks: int32 [2048], P(('grp', 'clu')), may hold values from 64 to 128
- parent_group: int32 [2048, 1], P(('grp', 'clu')), may hold values from 0 to 7; in each aligned block of 8 rows (0 to 7, 8 to 15, ...) no two rows name the same one
Outputs:
- reduced_near: bfloat16 [256, 32, 2, 128, 128], P(('grp', 'clu'))
- merged: bfloat16 [1024, 2, 128, 128], P(('grp', 'clu'))
Inputs may be any that keep to these rules, and one draw needn't show every extreme that they name: `col_device`: within the rows of one device, no device of the subtree is named by more than 2 blocks, and the entries of one row are distinct. `parent_group`: the clusters of one device name each subtree exactly 1 times.
All inputs are finite; a program needn't handle non-finite values.
Results may differ from a plain program's by a relative error of at most 0.0076.
Values may be sent and summed in bfloat16 or wider, within the bound.
No kernel may reach another device: no remote copies, remote signals or barrier semaphores. Data moves between devices by JAX's collectives and lax.ppermute only.
A program may use at most 128 MiB of HBM per device.

v0:
```python
import jax
import jax.numpy as jnp
from jax import lax
from jax.sharding import PartitionSpec as P

HIGH = lax.Precision.HIGHEST


def prepare(basis, diagonal, inverse):
    redundant = inverse.shape[0]
    left_product = jnp.dot(basis.T, diagonal, preferred_element_type=jnp.float32).astype(
        jnp.bfloat16
    )
    skel_red = jnp.dot(
        left_product[redundant:], basis[:, :redundant], preferred_element_type=jnp.float32
    )
    red_skel = jnp.dot(
        left_product[:redundant], basis[:, redundant:], preferred_element_type=jnp.float32
    )
    lower_factor = jnp.dot(skel_red, inverse, precision=HIGH)
    upper_factor = jnp.dot(inverse, red_skel, precision=HIGH)
    basis_wide = basis.astype(jnp.float32)
    row_basis = (
        basis_wide[:, redundant:].T
        - jnp.dot(lower_factor, basis_wide[:, :redundant].T, precision=HIGH)
    ).astype(jnp.bfloat16)
    col_basis = (
        basis_wide[:, redundant:] - jnp.dot(basis_wide[:, :redundant], upper_factor, precision=HIGH)
    ).astype(jnp.bfloat16)
    diag_left = jnp.dot(row_basis, diagonal, preferred_element_type=jnp.float32).astype(
        jnp.bfloat16
    )
    return (row_basis, col_basis, diag_left)


def rank_mask(row_ranks, col_ranks, skeleton):
    skeleton_index = jnp.arange(skeleton, dtype=jnp.int32)
    rows_ok = skeleton_index[:, None] < row_ranks[..., None, None]
    cols_ok = skeleton_index[None, :] < col_ranks[..., None, None]
    return (rows_ok & cols_ok).astype(jnp.float32)


def running_slot(targets, buckets):
    onehot = (targets[:, None] == jnp.arange(buckets, dtype=jnp.int32)[None, :]).astype(jnp.int32)
    before = jnp.cumsum(onehot, axis=0) - onehot
    return jnp.sum(before * onehot, axis=1)


def on_device(
    near_blocks, diag_blocks, bases, diag_inverses, col_device, col_local, ranks, parent_group
):
    clu_size = lax.axis_size("clu")
    group_size = lax.axis_size("grp")
    local_count, near_count = col_device.shape
    skeleton = diag_inverses.shape[1]
    skeleton = bases.shape[2] - skeleton
    block_size = bases.shape[1]
    capacity = max(2, -(-(local_count * near_count) // clu_size))
    row_basis, col_basis, diag_left = jax.vmap(prepare)(bases, diag_blocks, diag_inverses)
    rdiag = jnp.einsum("csb,cbt->cst", diag_left, col_basis, preferred_element_type=jnp.float32)
    rdiag = (rdiag * rank_mask(ranks, ranks, skeleton)).astype(jnp.bfloat16)
    per_group = local_count // group_size
    parent_target = parent_group[:, 0]
    merge_slot = running_slot(parent_target, group_size)
    outgoing = jnp.zeros((group_size, per_group, skeleton, skeleton), jnp.bfloat16)
    outgoing = outgoing.at[parent_target, merge_slot].set(rdiag)
    arrived = lax.all_to_all(outgoing, "grp", split_axis=0, concat_axis=0, tiled=True)
    merged = arrived.reshape(local_count // 2, 2, skeleton, skeleton)
    moved = jnp.einsum("csb,ckbd->cksd", row_basis, near_blocks, preferred_element_type=jnp.float32)
    moved = moved.astype(jnp.bfloat16).reshape(local_count * near_count, skeleton, block_size)
    destination = col_device.reshape(-1)
    slot_index = running_slot(destination, clu_size)
    row_ranks = jnp.repeat(ranks, near_count)
    all_bases, all_ranks = (
        lax.all_gather(col_basis, "clu", axis=0, tiled=True),
        lax.all_gather(ranks, "clu", axis=0, tiled=True),
    )
    gather_index = (col_device * local_count + col_local).reshape(-1)
    chosen = all_bases[gather_index]
    reduced = jnp.einsum("esd,edt->est", moved, chosen, preferred_element_type=jnp.float32)
    reduced = (reduced * rank_mask(row_ranks, all_ranks[gather_index], skeleton)).astype(
        jnp.bfloat16
    )
    outgoing_near = jnp.zeros((clu_size, capacity, skeleton, skeleton), jnp.bfloat16)
    outgoing_near = outgoing_near.at[destination, slot_index].set(reduced)
    reduced_near = lax.all_to_all(outgoing_near, "clu", split_axis=0, concat_axis=0, tiled=True)[
        None
    ]
    return (reduced_near, merged)


def solution(mesh):
    in_specs = (
        P(("grp", "clu"), None, None, None),
        P(("grp", "clu"), None, None),
        P(("grp", "clu"), None, None),
        P(("grp", "clu"), None, None),
        P(("grp", "clu"), None),
        P(("grp", "clu"), None),
        P(("grp", "clu")),
        P(("grp", "clu"), None),
    )
    out_specs = (P(("grp", "clu"), None, None, None, None), P(("grp", "clu"), None, None, None))
    return jax.shard_map(
        on_device, mesh=mesh, in_specs=in_specs, out_specs=out_specs, check_vma=False
    )
```

profile of v0, /device:TPU:16, one launch (start us, length us, event | category | flops | bytes accessed | tf_op | source)
XLA Modules:
  0.0 247.2 jit_solution(1545207099458903474)
XLA Ops:
  7.2 0.0 copy-start
  7.2 0.0 copy-start.1
  7.2 0.0 copy-start.3
  7.2 0.0 all-gather.2.cloned.1.call-start
  7.2 2.0 slice.19
  9.3 1.2 copy.35
  10.5 0.0 copy-done
  10.5 1.7 convolution_convert_fusion.1
  12.3 0.0 copy-start.2
  12.3 1.0 copy-done.2
  13.2 0.0 copy-done.1
  13.2 0.0 copy-start.6
  13.2 0.0 copy-start.7
  13.2 0.3 fusion.4
  13.6 0.0 copy-done.3
  13.6 1.2 fusion.20
  14.8 1.4 fusion.1
  16.2 2.0 copy.28
  18.2 0.0 all-gather.2.cloned.1.call-update
  18.3 0.0 copy-done.6
  18.3 0.1 fusion.13
  18.4 0.2 select_reduce_fusion.1
  18.6 0.0 copy-done.7
  18.6 0.1 iota_compare_fusion.3
  18.6 1.3 fusion.6
  20.0 0.6 fusion.19
  20.6 0.0 copy-start.4
  20.6 0.0 copy-start.5
  20.7 0.0 copy-start.8
  20.7 0.6 fusion.2
  21.3 1.5 fusion.3
  22.8 0.7 broadcast.173
  23.5 2.2 scatter_fusion.1
  25.7 5.4 %all-to-all-start.1 = ((bf16[8,1,128,128]{3,2,1,0:T(8,128)(2,1)}), bf16[8,1,128,128]{3,2,1,0:T(8,128)(2,1)S(1)}, u32[]{:S(2)}, u32[]{:S(2)}) async-start(bf16[8,1,128,128]{3,2,1,0:T(8,128)(2,1)} %bitcast.14), calls=%async_computation.1 | async-start | bytes 524288 | tf_op jit(solution)/shard_map/all_to_all | solution.py:67
  31.1 0.0 copy-done.4
  31.1 0.1 eq.30
  31.2 0.1 reshape.193
  31.3 0.0 copy-done.5
  31.3 0.1 reshape.194
  31.4 0.1 broadcast_in_dim.9
  31.4 0.1 lt.116
  31.5 0.1 fusion.12
  31.6 0.1 reduce_window_sum.22
  31.7 0.0 copy-done.8
  31.7 0.6 dynamic-slice
  32.9 0.2 dynamic-update-slice
  33.2 23.1 %all-reduce = s32[256]{0:T(256)S(1)} all-reduce(s32[256]{0:T(256)S(1)} %dynamic-update-slice), channel_id=1, replica_groups=mesh['grp'=8,'clu'=32] {'clu'}, use_global_device_ids=true, to_apply=%add | all-reduce | flops 256 | bytes 2048
  56.3 0.8 gather_fusion
  57.0 0.2 select_reduce_fusion
  57.2 0.1 iota_compare_fusion.1
  57.3 0.1 iota_compare_fusion
  57.4 5.5 %convolution_convert_fusion = bf16[8,128,6,256]{3,1,2,0:T(8,128)(2,1)} fusion(bf16[8,6,256,256]{3,2,1,0:T(8,128)(2,1)} %param.8, bf16[8,128,256]{2,1,0:T(8,128)(2,1)S(1)} %fusion.2), kind=kOutput, calls=%fused_computation.5 | convolution fusion | flops 806879232 | bytes 9961472 | tf_op jit(solution)/shard_map/csb,ckbd->cksd/dot_general | solution.py:69
  62.9 98.8 %all-gather.2.cloned.1.call-done = bf16[256,256,128]{2,1,0:T(8,128)(2,1)} async-done(((bf16[8,256,128]{2,1,0:T(8,128)(2,1)}), bf16[256,256,128]{2,1,0:T(8,128)(2,1)}) %all-gather.2.cloned.1.call-update) | async-done | bytes 16777232 | tf_op jit(solution)/shard_map/all_gather | solution.py:75
  161.8 8.5 %gather_fusion.1 = bf16[48,256,128]{2,1,0:T(8,128)(2,1)} fusion(bf16[256,256,128]{2,1,0:T(8,128)(2,1)} %all-gather.2.cloned.1.call-done, s32[1024]{0:T(1024)S(1)} %pad_clamp_fusion), kind=kCustom, calls=%fused_computation.1 | custom fusion | bytes 6291648 | tf_op jit(solution)/shard_map/gather | solution.py:79
  170.3 3.7 %select_convert_fusion = bf16[48,128,128]{2,1,0:T(8,128)(2,1)S(1)} fusion(bf16[48,128,256]{2,1,0:T(8,128)(2,1)} %bitcast.54, bf16[48,256,128]{2,1,0:T(8,128)(2,1)} %gather_fusion.1, pred[48,128]{1,0:T(8,128)(4,1)S(1)} %iota_compare_fusion, pred[48,128]{1,0:T(8,128)(4,1)S(1)} %iota_compare_fusion.1), kind=kOutput, calls=%fused_computation.4 | convolution fusion | flops 405012480 | bytes 7876608 | tf_op jit(solution)/shard_map/esd,edt->est/dot_general | solution.py:80
  174.0 1.8 broadcast_in_dim.8
  175.8 7.1 %scatter_fusion = bf16[32,2,128,128]{3,2,1,0:T(8,128)(2,1)} fusion(bf16[32,2,128,128]{3,2,1,0:T(8,128)(2,1)} %broadcast_in_dim.8, s32[48]{0:T(128)S(1)} %fusion.16, bf16[48,128,128]{2,1,0:T(8,128)(2,1)S(1)} %select_convert_fusion), kind=kCustom, calls=%fused_computation.2 | custom fusion | bytes 4718976 | tf_op jit(solution)/shard_map/scatter | solution.py:85
  182.9 0.0 all-to-all-done.1
  182.9 5.6 %all-to-all-start = ((bf16[32,2,128,128]{3,2,1,0:T(8,128)(2,1)}), bf16[32,2,128,128]{3,2,1,0:T(8,128)(2,1)S(1)}, u32[]{:S(2)}, u32[]{:S(2)}) async-start(bf16[32,2,128,128]{3,2,1,0:T(8,128)(2,1)} %scatter_fusion), calls=%async_computation | async-start | bytes 4194304 | tf_op jit(solution)/shard_map/all_to_all | solution.py:86
  188.5 49.8 %all-to-all-done = bf16[32,2,128,128]{3,2,1,0:T(8,128)(2,1)S(1)} async-done(((bf16[32,2,128,128]{3,2,1,0:T(8,128)(2,1)}), bf16[32,2,128,128]{3,2,1,0:T(8,128)(2,1)S(1)}, u32[]{:S(2)}, u32[]{:S(2)}) %all-to-all-start) | async-done | bytes 2097184 | tf_op jit(solution)/shard_map/all_to_all | solution.py:86
  238.3 1.3 copy.41
  239.6 0.7 copy.42
  (7 shorter events, 0.1 us)
Async XLA Ops:
  7.2 3.4 %copy-start = (bf16[8,256,256]{2,1,0:T(8,128)(2,1)S(1)}, bf16[8,256,256]{2,1,0:T(8,128)(2,1)}, u32[]{:S(2)}) copy-start(bf16[8,256,256]{2,1,0:T(8,128)(2,1)} %param.9) | copy-start | bytes 3145732
  7.2 6.1 %copy-start.1 = (bf16[8,256,256]{2,1,0:T(8,128)(2,1)S(1)}, bf16[8,256,256]{2,1,0:T(8,128)(2,1)}, u32[]{:S(2)}) copy-start(bf16[8,256,256]{2,1,0:T(8,128)(2,1)} %param.10) | copy-start | bytes 3145732
  7.2 6.4 %copy-start.3 = (f32[8,128,128]{2,1,0:T(8,128)S(1)}, f32[8,128,128]{2,1,0:T(8,128)}, u32[]{:S(2)}) copy-start(f32[8,128,128]{2,1,0:T(8,128)} %param.11) | copy-start | bytes 1572868
  7.2 154.6 %all-gather.2.cloned.1.call-start = ((), (), s32[]{:S(2)}) async-start(), calls=%async_computation.2 | async-start | bytes 17301504 | tf_op jit(solution)/shard_map/all_gather | solution.py:75
  12.3 1.0 copy-start.2
  13.2 5.0 %copy-start.6 = (s32[8,1]{0,1:T(1,128)S(1)}, s32[8,1]{0,1:T(1,128)}, u32[]{:S(2)}) copy-start(s32[8,1]{0,1:T(1,128)} %param.15) | copy-start | bytes 100
  13.2 5.3 %copy-start.7 = (s32[8]{0:T(128)S(1)}, s32[8]{0:T(128)}, u32[]{:S(2)}) copy-start(s32[8]{0:T(128)} %param.14) | copy-start | bytes 100
  20.6 10.5 %copy-start.4 = (s32[8,6]{1,0:T(8,128)S(1)}, s32[8,6]{1,0:T(8,128)}, u32[]{:S(2)}) copy-start(s32[8,6]{1,0:T(8,128)} %param.12) | copy-start | bytes 580
  20.6 10.6 %copy-start.5 = (s32[8,6]{1,0:T(8,128)S(1)}, s32[8,6]{1,0:T(8,128)}, u32[]{:S(2)}) copy-start(s32[8,6]{1,0:T(8,128)} %param.13) | copy-start | bytes 580
  20.7 11.0 %copy-start.8 = (u32[256]{0:T(256)S(1)}, u32[256]{0:T(256)}, u32[]{:S(2)}) copy-start(u32[256]{0:T(256)} %constant.57) | copy-start | bytes 3076
  25.7 157.2 %all-to-all-start.1 = ((bf16[8,1,128,128]{3,2,1,0:T(8,128)(2,1)}), bf16[8,1,128,128]{3,2,1,0:T(8,128)(2,1)S(1)}, u32[]{:S(2)}, u32[]{:S(2)}) async-start(bf16[8,1,128,128]{3,2,1,0:T(8,128)(2,1)} %bitcast.14), calls=%async_computation.1 | async-start | bytes 524288 | tf_op jit(solution)/shard_map/all_to_all | solution.py:67
  182.9 55.4 %all-to-all-start = ((bf16[32,2,128,128]{3,2,1,0:T(8,128)(2,1)}), bf16[32,2,128,128]{3,2,1,0:T(8,128)(2,1)S(1)}, u32[]{:S(2)}, u32[]{:S(2)}) async-start(bf16[32,2,128,128]{3,2,1,0:T(8,128)(2,1)} %scatter_fusion), calls=%async_computation | async-start | bytes 4194304 | tf_op jit(solution)/shard_map/all_to_all | solution.py:86
Sparse Core Ops, SparseCore 0:
  18.4 143.3 all-gather.1
where the time goes:
time: 249 us; the launch traced here: 247 us
  waiting for transfers between devices  149 us (60%)
  local copies, waits for them, and re-layouts  30.7 us (12%)
  blocking collectives  23.1 us (9%)
  matrix products  18 us (7%)
  between operations  14.9 us (6%)
  starting transfers between devices  11.1 us (4%)
    all_gather x1, waiting for transfers between devices, on_device(): lax.all_gather(col_basis, 'clu', axis=0, tiled=True)  98.8 us
    all_to_all x1, waiting for transfers between devices, on_device(): lax.all_to_all(outgoing_near, 'clu', split_axis=0, concat_axis=0, tiled=T...  49.8 us
    unnamed x1, blocking collectives  23.1 us
    gather x1, local copies, waits for them, and re-layouts, on_device(): chosen = all_bases[gather_index]  8.52 us
    unnamed x25, local copies, waits for them, and re-layouts  7.13 us
    scatter x1, local copies, waits for them, and re-layouts, on_device(): outgoing_near = outgoing_near.at[destination, slot_index].set(reduced)  7.12 us
    all_to_all x1, starting transfers between devices, on_device(): lax.all_to_all(outgoing_near, 'clu', split_axis=0, concat_axis=0, tiled=T...  5.63 us
    dot_general x1, matrix products, on_device(): jnp.einsum('csb,ckbd->cksd', row_basis, near_blocks, preferred_element_ty...  5.52 us
  transfers between devices with their start and end apart: 3, of which 2 were waited for; matrix products, arithmetic and copies ran while one was open for 15% of the time, Pallas kernels for 0%

commit v1 on v0

v1 whole, which is shorter than its diff:
```python
import functools

import jax
import jax.numpy as jnp
from jax import lax
from jax.experimental import pallas as pl
from jax.experimental.pallas import tpu as pltpu
from jax.sharding import PartitionSpec as P

BF16 = jnp.bfloat16
F32 = jnp.float32
CAPACITY = 2


def dot(a, b):
    return jnp.dot(a, b, preferred_element_type=F32)


def dot_nt(a, b):
    return lax.dot_general(a, b, (((1,), (1,)), ((), ())), preferred_element_type=F32)


def halves(x):
    high = x.astype(BF16)
    return high, (x - high.astype(F32)).astype(BF16)


def dot_wide(a, b):
    a_high, a_low = halves(a)
    b_high, b_low = halves(b)
    upper = jnp.concatenate([b_high, b_low], 1)
    lower = jnp.concatenate([b_high, jnp.zeros_like(b_low)], 1)
    both = dot(jnp.concatenate([a_high, a_low], 1), jnp.concatenate([upper, lower], 0))
    return both[:, : b.shape[1]] + both[:, b.shape[1] :]


def move_kernel(
    near_count,
    group,
    col_device_hbm,
    col_local_hbm,
    ranks_hbm,
    bases_hbm,
    diag_hbm,
    inverse_hbm,
    near_hbm,
    send_hbm,
    row_hbm,
    meta_hbm,
    col_device,
    col_local,
    ranks,
    bases,
    diag,
    inverse,
    near,
    rows,
    moved,
    count,
    place,
    meta,
    int_sem,
    in_sem,
    near_sem,
    out_sem,
    row_sem,
):
    local_count, block, _ = bases.shape
    redundant = inverse.shape[1]
    skeleton = block - redundant
    groups = local_count // group
    ints = (
        pltpu.make_async_copy(col_device_hbm, col_device, int_sem.at[0]),
        pltpu.make_async_copy(col_local_hbm, col_local, int_sem.at[1]),
        pltpu.make_async_copy(ranks_hbm, ranks, int_sem.at[2]),
    )
    meta_copy = pltpu.make_async_copy(meta, meta_hbm, int_sem.at[3])

    def inputs(g):
        part = pl.ds(g * group, group)
        return (
            pltpu.make_async_copy(bases_hbm.at[part], bases.at[part], in_sem.at[g, 0]),
            pltpu.make_async_copy(diag_hbm.at[part], diag.at[part], in_sem.at[g, 1]),
            pltpu.make_async_copy(inverse_hbm.at[part], inverse.at[part], in_sem.at[g, 2]),
        )

    def near_copy(c):
        return pltpu.make_async_copy(near_hbm.at[c], near.at[c], near_sem.at[c])

    def out_copy(c, k):
        return pltpu.make_async_copy(moved.at[c, k], send_hbm.at[place[c, k]], out_sem.at[c, k])

    def row_copy(g):
        part = pl.ds(g * group, group)
        return pltpu.make_async_copy(rows.at[part], row_hbm.at[part], row_sem.at[g])

    for copy in ints:
        copy.start()
    for g in range(groups):
        for copy in inputs(g):
            copy.start()
        for c in range(g * group, (g + 1) * group):
            near_copy(c).start()

    def clear(d, carry):
        count[d] = 0
        for s in range(CAPACITY):
            meta[d, s] = -1
        return carry

    lax.fori_loop(0, count.shape[0], clear, 0)
    for copy in ints:
        copy.wait()

    def assign(l, carry):
        for k in range(near_count):
            d = col_device[l, k]
            s = count[d]
            count[d] = s + 1
            meta[d, s] = col_local[l, k]
            place[l, k] = d * CAPACITY + s
        return carry

    lax.fori_loop(0, local_count, assign, 0)
    meta_copy.start()

    def prepare(members):
        red = [bases[c][:, :redundant] for c in members]
        skel_t = [bases[c][:, redundant:].T for c in members]
        left = [dot(s, diag[c]).astype(BF16) for s, c in zip(skel_t, members)]
        factor = [dot(l, r) for l, r in zip(left, red)]
        lower = [halves(dot_wide(f, inverse[c])) for f, c in zip(factor, members)]
        taken = [
            dot_nt(jnp.concatenate(pair, 1), jnp.concatenate([r, r], 1))
            for pair, r in zip(lower, red)
        ]
        for c, s, t in zip(members, skel_t, taken):
            rows[c] = (s.astype(F32) - t).astype(BF16)

    rows_at = lax.broadcasted_iota(jnp.int32, (skeleton, block), 0)

    def step(c, carry):
        near_copy(c).wait()
        keep = rows_at < ranks[c]
        row = rows[c]
        for k in range(near_count):
            moved[c, k] = jnp.where(keep, dot(row, near[c, k]), 0.0).astype(BF16)
        for k in range(near_count):
            out_copy(c, k).start()
        return carry

    for g in range(groups):
        for copy in inputs(g):
            copy.wait()
        prepare(range(g * group, (g + 1) * group))
        row_copy(g).start()
        lax.fori_loop(g * group, (g + 1) * group, step, 0)

    for g in range(groups):
        row_copy(g).wait()
    meta_copy.wait()

    def finish(c, carry):
        for k in range(near_count):
            out_copy(c, k).wait()
        return carry

    lax.fori_loop(0, local_count, finish, 0)


def move_blocks(near_blocks, diag_blocks, bases, diag_inverses, col_device, col_local, ranks, buckets):
    local_count, near_count, block, _ = near_blocks.shape
    redundant = diag_inverses.shape[1]
    skeleton = block - redundant
    group = 4
    groups = local_count // group
    hbm = pl.BlockSpec(memory_space=pl.ANY)
    dma = pltpu.SemaphoreType.DMA
    return pl.pallas_call(
        functools.partial(move_kernel, near_count, group),
        out_shape=(
            jax.ShapeDtypeStruct((buckets * CAPACITY, skeleton, block), BF16),
            jax.ShapeDtypeStruct((local_count, skeleton, block), BF16),
            jax.ShapeDtypeStruct((buckets, CAPACITY), jnp.int32),
        ),
        in_specs=[hbm] * 7,
        out_specs=(hbm, hbm, hbm),
        scratch_shapes=[
            pltpu.SMEM((local_count, near_count), jnp.int32),
            pltpu.SMEM((local_count, near_count), jnp.int32),
            pltpu.SMEM((local_count,), jnp.int32),
            pltpu.VMEM((local_count, block, block), BF16),
            pltpu.VMEM((local_count, block, block), BF16),
            pltpu.VMEM((local_count, redundant, redundant), F32),
            pltpu.VMEM((local_count, near_count, block, block), BF16),
            pltpu.VMEM((local_count, skeleton, block), BF16),
            pltpu.VMEM((local_count, near_count, skeleton, block), BF16),
            pltpu.SMEM((buckets,), jnp.int32),
            pltpu.SMEM((local_count, near_count), jnp.int32),
            pltpu.SMEM((buckets, CAPACITY), jnp.int32),
            dma((4,)),
            dma((groups, 3)),
            dma((local_count,)),
            dma((local_count, near_count)),
            dma((groups,)),
        ],
        compiler_params=pltpu.CompilerParams(vmem_limit_bytes=56 * 2**20),
        cost_estimate=pl.CostEstimate(
            flops=2 * 10**9, bytes_accessed=13 * 10**6, transcendentals=0
        ),
        name="move_blocks",
    )(col_device, col_local, ranks, bases, diag_blocks, diag_inverses, near_blocks)


def diagonal_kernel(parent, ranks, basis_ref, diag_ref, inverse_ref, row_ref, out_ref, col_ref):
    c = pl.program_id(0)
    redundant = inverse_ref.shape[1]
    basis = basis_ref[0]
    diagonal = diag_ref[0]
    red = basis[:, :redundant]
    skel = basis[:, redundant:]
    left = dot(red.T, diagonal).astype(BF16)
    upper = dot_wide(inverse_ref[0], dot(left, skel))
    high, low = halves(upper)
    col = (skel.astype(F32) - (dot(red, high) + dot(red, low))).astype(BF16)
    col_ref[0] = col
    reduced = dot(dot(row_ref[0], diagonal).astype(BF16), col)
    rank = ranks[c]
    rows_at = lax.broadcasted_iota(jnp.int32, reduced.shape, 0)
    cols_at = lax.broadcasted_iota(jnp.int32, reduced.shape, 1)
    keep = (rows_at < rank) & (cols_at < rank)
    out_ref[0] = jnp.where(keep, reduced, 0.0).astype(BF16)


def diagonal_part(bases, diag_blocks, diag_inverses, row_basis, ranks, parent_group):
    local_count, block, _ = bases.shape
    redundant = diag_inverses.shape[1]
    skeleton = block - redundant

    def own(*shape):
        return pl.BlockSpec((1,) + shape, lambda c, parent, ranks: (c, 0, 0))

    return pl.pallas_call(
        diagonal_kernel,
        out_shape=(
            jax.ShapeDtypeStruct((local_count, skeleton, skeleton), BF16),
            jax.ShapeDtypeStruct((local_count, block, skeleton), BF16),
        ),
        grid_spec=pltpu.PrefetchScalarGridSpec(
            num_scalar_prefetch=2,
            grid=(local_count,),
            in_specs=[
                own(block, block),
                own(block, block),
                own(redundant, redundant),
                own(skeleton, block),
            ],
            out_specs=[
                pl.BlockSpec(
                    (1, skeleton, skeleton), lambda c, parent, ranks: (parent[c], 0, 0)
                ),
                own(block, skeleton),
            ],
        ),
        compiler_params=pltpu.CompilerParams(vmem_limit_bytes=16 * 2**20),
        cost_estimate=pl.CostEstimate(
            flops=10**9, bytes_accessed=4 * 10**6, transcendentals=0
        ),
        name="diagonal_part",
    )(parent_group[:, 0], ranks, bases, diag_blocks, diag_inverses, row_basis)


def reduce_kernel(
    chunk,
    meta_hbm,
    ranks_hbm,
    moved_hbm,
    col_hbm,
    out_hbm,
    meta,
    ranks,
    moved,
    col,
    out,
    int_sem,
    in_sem,
    out_sem,
):
    steps = moved.shape[0] // chunk
    firsts = (
        pltpu.make_async_copy(meta_hbm, meta, int_sem.at[0]),
        pltpu.make_async_copy(ranks_hbm, ranks, int_sem.at[1]),
        pltpu.make_async_copy(col_hbm, col, int_sem.at[2]),
    )

    def in_copy(i):
        part = pl.ds(i * chunk, chunk)
        return pltpu.make_async_copy(moved_hbm.at[part], moved.at[part], in_sem.at[i])

    def out_copy(i):
        part = pl.ds(i * chunk, chunk)
        return pltpu.make_async_copy(out.at[part], out_hbm.at[part], out_sem.at[i])

    for copy in firsts:
        copy.start()
    for i in range(steps):
        in_copy(i).start()
    for copy in firsts:
        copy.wait()
    cols_at = lax.broadcasted_iota(jnp.int32, out.shape[1:], 1)

    def step(i, carry):
        in_copy(i).wait()
        for j in range(chunk):
            e = i * chunk + j
            local = meta[i * (chunk // CAPACITY) + j // CAPACITY, j % CAPACITY]
            owner = jnp.maximum(local, 0)
            rank = jnp.where(local < 0, 0, ranks[owner])
            out[e] = jnp.where(cols_at < rank, dot(moved[e], col[owner]), 0.0).astype(BF16)
        out_copy(i).start()
        return carry

    lax.fori_loop(0, steps, step, 0)
    for i in range(steps):
        out_copy(i).wait()


def reduce_blocks(moved, meta, col_basis, ranks):
    slots, skeleton, block = moved.shape
    chunk = 16
    hbm = pl.BlockSpec(memory_space=pl.ANY)
    dma = pltpu.SemaphoreType.DMA
    return pl.pallas_call(
        functools.partial(reduce_kernel, chunk),
        out_shape=jax.ShapeDtypeStruct((slots, skeleton, skeleton), BF16),
        in_specs=[hbm] * 4,
        out_specs=hbm,
        scratch_shapes=[
            pltpu.SMEM(meta.shape, jnp.int32),
            pltpu.SMEM(ranks.shape, jnp.int32),
            pltpu.VMEM(moved.shape, BF16),
            pltpu.VMEM(col_basis.shape, BF16),
            pltpu.VMEM((slots, skeleton, skeleton), BF16),
            dma((3,)),
            dma((slots // chunk,)),
            dma((slots // chunk,)),
        ],
        compiler_params=pltpu.CompilerParams(vmem_limit_bytes=56 * 2**20),
        cost_estimate=pl.CostEstimate(
            flops=6 * 10**8, bytes_accessed=7 * 10**6, transcendentals=0
        ),
        name="reduce_blocks",
    )(meta, ranks, moved, col_basis)


def swap_halves(x, axis_name):
    size = lax.axis_size(axis_name)
    me = lax.axis_index(axis_name)
    bit = 1
    while bit < size:
        pairs = x.reshape((size // (2 * bit), 2, bit) + x.shape[1:])
        mine = (me // bit) % 2
        kept = lax.dynamic_index_in_dim(pairs, mine, 1, keepdims=False)
        given = lax.dynamic_index_in_dim(pairs, 1 - mine, 1, keepdims=False)
        got = lax.ppermute(given, axis_name, [(i, i ^ bit) for i in range(size)])
        low, high = jnp.stack([kept, got], 1), jnp.stack([got, kept], 1)
        x = jnp.where(mine == 0, low, high).reshape(x.shape)
        bit *= 2
    return x


def on_device(
    near_blocks, diag_blocks, bases, diag_inverses, col_device, col_local, ranks, parent_group
):
    buckets = lax.axis_size("clu")
    local_count = ranks.shape[0]
    send, row_basis, meta = move_blocks(
        near_blocks, diag_blocks, bases, diag_inverses, col_device, col_local, ranks, buckets
    )
    skeleton, block = send.shape[1:]
    received = lax.all_to_all(
        send.reshape(buckets, CAPACITY, skeleton, block), "clu", 0, 0, tiled=True
    )
    came_meta = swap_halves(meta, "clu")
    outgoing, col_basis = diagonal_part(
        bases, diag_blocks, diag_inverses, row_basis, ranks, parent_group
    )
    arrived = swap_halves(outgoing, "grp")
    merged = arrived.reshape(local_count // 2, 2, skeleton, skeleton)
    reduced = reduce_blocks(
        received.reshape(buckets * CAPACITY, skeleton, block), came_meta, col_basis, ranks
    )
    return reduced.reshape(1, buckets, CAPACITY, skeleton, skeleton), merged


def solution(mesh):
    in_specs = (
        P(("grp", "clu"), None, None, None),
        P(("grp", "clu"), None, None),
        P(("grp", "clu"), None, None),
        P(("grp", "clu"), None, None),
        P(("grp", "clu"), None),
        P(("grp", "clu"), None),
        P(("grp", "clu")),
        P(("grp", "clu"), None),
    )
    out_specs = (P(("grp", "clu"), None, None, None, None), P(("grp", "clu"), None, None, None))
    return jax.shard_map(
        on_device, mesh=mesh, in_specs=in_specs, out_specs=out_specs, check_vma=False
    )
```

time: 249 us -> 135 us (0.54)
  waiting for transfers between devices: 149 us -> 81.6 us
  local copies, waits for them, and re-layouts: 30.7 us -> 2.78 us
  blocking collectives: 23.1 us -> 0 us
  Pallas kernels: 0 us -> 19.2 us
  matrix products: 18 us -> 0 us
  starting transfers between devices: 11.1 us -> 26.8 us
  between operations: 14.9 us -> 1.06 us
    all_gather x1 -> x0, waiting for transfers between devices: 98.8 us -> none  [on_device(): lax.all_gather(col_basis, 'clu', axis=0, tiled=True)]
    ppermute x0 -> x8, waiting for transfers between devices: none -> 81.6 us  [swap_halves(): got = lax.ppermute(given, axis_name, [(i, i ^ bit) for i in range(size)])]
    all_to_all x2 -> x1, waiting for transfers between devices: 49.8 us -> 0.01 us  [on_device(): lax.all_to_all(send.reshape(buckets, CAPACITY, skeleton, block), 'clu', 0...]
    unnamed x1 -> x0, blocking collectives: 23.1 us -> none
    pallas_call x0 -> x3, Pallas kernels: none -> 19.2 us  [the longest x1 7.37 us: diagonal_part(): pl.pallas_call(diagonal_kernel, out_shape=(jax.ShapeDtypeStruct((local_co...]
    dot_general x10 -> x0, matrix products: 18 us -> none  [the longest x1 5.52 us: on_device(): jnp.einsum('csb,ckbd->cksd', row_basis, near_blocks, preferred_element_ty...]
    ppermute x0 -> x8, starting transfers between devices: none -> 15.1 us  [swap_halves(): got = lax.ppermute(given, axis_name, [(i, i ^ bit) for i in range(size)])]
    gather x2 -> x0, local copies, waits for them, and re-layouts: 9.31 us -> none  [the longest x1 8.52 us: on_device(): chosen = all_bases[gather_index]]
  transfers between devices with their start and end apart: 3 -> 9, of which waited for: 2 -> 4; matrix products, arithmetic and copies ran while one was open for 15% -> 2% of each run, Pallas kernels for 0% -> 6%
where the time goes in v1:
time: 135 us; the launch traced here: 132 us
  waiting for transfers between devices  81.6 us (60%)
  starting transfers between devices  26.8 us (20%)
  Pallas kernels  19.2 us (14%)
  local copies, waits for them, and re-layouts  2.78 us (2%)
    ppermute x8, waiting for transfers between devices, swap_halves(): got = lax.ppermute(given, axis_name, [(i, i ^ bit) for i in range(size)])  81.6 us
    ppermute x8, starting transfers between devices, swap_halves(): got = lax.ppermute(given, axis_name, [(i, i ^ bit) for i in range(size)])  15.1 us
    all_to_all x1, starting transfers between devices, on_device(): lax.all_to_all(send.reshape(buckets, CAPACITY, skeleton, block), 'clu', 0...  11.7 us
    pallas_call x1, Pallas kernels, diagonal_part(): pl.pallas_call(diagonal_kernel, out_shape=(jax.ShapeDtypeStruct((local_co...  7.37 us
    pallas_call x1, Pallas kernels, move_blocks(): pl.pallas_call(functools.partial(move_kernel, near_count, group), out_sha...  7.19 us
    pallas_call x1, Pallas kernels, reduce_blocks(): pl.pallas_call(functools.partial(reduce_kernel, chunk), out_shape=jax.Sha...  4.6 us
  transfers between devices with their start and end apart: 9, of which 4 were waited for; matrix products, arithmetic and copies ran while one was open for 2% of the time, Pallas kernels for 6%

profile of v1, /device:TPU:16, one launch (start us, length us, event | category | flops | bytes accessed | tf_op | source)
XLA Modules:
  0.0 132.3 jit_solution(4022558234348544306)
XLA Ops:
  0.6 7.2 %move_blocks.1 = (bf16[64,128,256]{2,1,0:T(8,128)(2,1)}, bf16[8,128,256]{2,1,0:T(8,128)(2,1)}, s32[32,2]{1,0:T(8,128)}) custom-call(s32[8,6]{1,0:T(8,128)} %col_device_hbm.1, s32[8,6]{1,0:T(8,128)} %col_local_hbm.1, s32[8]{0:T(128)} %ranks_hbm.3, bf16[8,256,256]{2,1,0:T(8,128)(2,1)} %basis_ref.1, bf16[8,256,256]{2,1,0:T(8,128)(2,1)} %diag_ref.1, ...), custom_call_target="tpu_custom_call" | custom-call | flops 2000000000 | bytes 13000000 | tf_op jit(solution)/shard_map/move_blocks/pallas_call | solution.py:179
  7.8 0.0 copy-start.7
  7.8 0.0 copy-start
  7.9 0.0 copy-start.1
  7.9 0.0 copy-start.3
  7.9 0.0 copy-start.4
  7.9 0.0 copy-start.5
  7.9 0.0 copy-start.6
  7.9 11.7 %all-to-all-start = ((bf16[32,2,128,256]{3,2,1,0:T(8,128)(2,1)}), bf16[32,2,128,256]{3,2,1,0:T(8,128)(2,1)}, u32[]{:S(2)}, u32[]{:S(2)}) async-start(bf16[32,2,128,256]{3,2,1,0:T(8,128)(2,1)} %bitcast.47), calls=%async_computation | async-start | bytes 8388608 | tf_op jit(solution)/shard_map/all_to_all | solution.py:381
  19.7 0.0 copy-done.7
  19.7 0.1 copy.56
  19.8 1.7 %collective-permute-start = (s32[16,1,2]{0,2,1:T(2,128)S(1)}, s32[16,1,2]{0,2,1:T(2,128)S(1)}, u32[]{:S(2)}, u32[]{:S(2)}) collective-permute-start(s32[16,1,2]{0,2,1:T(2,128)S(1)} %bitcast.63), channel_id=1, source_target_pairs={{0,1},{1,0},{2,3},{3,2},{4,5},{5,4},{6,7},{7,6},{8,9},{9,8},{10,11... | collective-permute-start | bytes 392 | tf_op jit(solution)/shard_map/ppermute | solution.py:365
  21.5 0.0 copy-done
  21.5 0.0 copy-done.1
  21.5 0.0 copy-done.3
  21.5 0.0 copy-done.4
  21.5 0.0 copy-done.5
  21.5 0.0 copy-done.6
  21.6 7.4 %diagonal_part.1 = (bf16[8,128,128]{2,1,0:T(8,128)(2,1)S(1)}, bf16[8,256,128]{2,1,0:T(8,128)(2,1)S(1)}) custom-call(s32[8]{0:T(128)S(1)} %bitcast.46, s32[8]{0:T(128)S(1)} %copy-done.4, bf16[8,256,256]{2,1,0:T(8,128)(2,1)S(1)} %copy-done, bf16[8,256,256]{2,1,0:T(8,128)(2,1)S(1)} %copy-done.1, f32[8,128,128]{2,1,0:T(8,128)S(1)} %copy-done.3, ...), custom_call_target="tpu_custom_call" | custom-call | flops 1000000000 | bytes 4000000 | tf_op jit(solution)/shard_map/diagonal_part/pallas_call | solution.py:243
  28.9 0.0 copy-start.2
  28.9 0.9 copy-done.2
  29.8 0.1 collective-permute-start.5
  30.1 0.1 copy.37
  30.2 0.0 collective-permute-done
  30.2 0.1 stack.101
  30.3 0.1 copy.38
  30.4 4.7 %collective-permute-start.1 = (s32[8,2,2]{0,2,1:T(2,128)S(1)}, s32[8,2,2]{0,2,1:T(2,128)S(1)}, u32[]{:S(2)}, u32[]{:S(2)}) collective-permute-start(s32[8,2,2]{0,2,1:T(2,128)S(1)} %get-tuple-element.25), channel_id=1, source_target_pairs={{0,2},{1,3},{2,0},{3,1},{4,6},{5,7},{6,4},{7,5},{8,10},{9,11},{10,... | collective-permute-start | bytes 392 | tf_op jit(solution)/shard_map/ppermute | solution.py:365
  35.1 1.6 %collective-permute-done.1 = s32[8,2,2]{0,2,1:T(2,128)S(1)} collective-permute-done((s32[8,2,2]{0,2,1:T(2,128)S(1)}, s32[8,2,2]{0,2,1:T(2,128)S(1)}, u32[]{:S(2)}, u32[]{:S(2)}) %collective-permute-start.1) | collective-permute-done | bytes 160 | tf_op jit(solution)/shard_map/ppermute | solution.py:365
  36.7 0.1 select_n.242
  36.8 0.1 constant_dynamic-slice_fusion.8
  36.9 0.1 copy.41
  37.0 1.5 %collective-permute-start.2 = (s32[4,4,2]{1,0,2:T(4,128)S(1)}, s32[4,4,2]{1,0,2:T(4,128)S(1)}, u32[]{:S(2)}, u32[]{:S(2)}) collective-permute-start(s32[4,4,2]{1,0,2:T(4,128)S(1)} %bitcast.59), channel_id=1, source_target_pairs={{0,4},{1,5},{2,6},{3,7},{4,0},{5,1},{6,2},{7,3},{8,12},{9,13},{10,... | collective-permute-start | bytes 392 | tf_op jit(solution)/shard_map/ppermute | solution.py:365
  38.5 73.0 %collective-permute-done.2 = s32[4,4,2]{1,0,2:T(4,128)S(1)} collective-permute-done((s32[4,4,2]{1,0,2:T(4,128)S(1)}, s32[4,4,2]{1,0,2:T(4,128)S(1)}, u32[]{:S(2)}, u32[]{:S(2)}) %collective-permute-start.2) | collective-permute-done | bytes 160 | tf_op jit(solution)/shard_map/ppermute | solution.py:365
  111.5 0.1 copy.42
  111.7 0.1 add_select_fusion
  111.8 0.1 copy.44
  111.9 0.1 select_n.246
  112.0 0.0 collective-permute-done.5
  112.1 1.4 %collective-permute-start.6 = (bf16[2,2,128,128]{3,2,1,0:T(8,128)(2,1)S(1)}, bf16[2,2,128,128]{3,2,1,0:T(8,128)(2,1)S(1)}, u32[]{:S(2)}, u32[]{:S(2)}) collective-permute-start(bf16[2,2,128,128]{3,2,1,0:T(8,128)(2,1)S(1)} %get-tuple-element.15), channel_id=1, source_target_pairs={{0,64},{32,96},{64,0},{96,32},{128,192},{160,224},{192,128},{224,1... | collective-permute-start | bytes 393224 | tf_op jit(solution)/shard_map/ppermute | solution.py:365
  113.4 0.5 collective-permute-start.3
  113.9 4.0 %collective-permute-done.3 = s32[2,8,2]{1,2,0:T(2,128)S(1)} collective-permute-done((s32[2,8,2]{1,2,0:T(2,128)S(1)}, s32[2,8,2]{1,2,0:T(2,128)S(1)}, u32[]{:S(2)}, u32[]{:S(2)}) %collective-permute-start.3) | collective-permute-done | bytes 160 | tf_op jit(solution)/shard_map/ppermute | solution.py:365
  117.9 0.1 select_n.250
  118.0 0.0 collective-permute-done.6
  118.1 0.7 collective-permute-start.7
  118.8 4.5 %collective-permute-start.4 = (s32[1,16,2]{1,2,0:T(2,128)S(1)}, s32[1,16,2]{1,2,0:T(2,128)S(1)}, u32[]{:S(2)}, u32[]{:S(2)}) collective-permute-start(s32[1,16,2]{1,2,0:T(2,128)S(1)} %get-tuple-element.27), channel_id=1, source_target_pairs={{0,16},{1,17},{2,18},{3,19},{4,20},{5,21},{6,22},{7,23},{8,24},{9,... | collective-permute-start | bytes 392 | tf_op jit(solution)/shard_map/ppermute | solution.py:365
  123.3 3.0 %collective-permute-done.4 = s32[1,16,2]{1,2,0:T(2,128)S(1)} collective-permute-done((s32[1,16,2]{1,2,0:T(2,128)S(1)}, s32[1,16,2]{1,2,0:T(2,128)S(1)}, u32[]{:S(2)}, u32[]{:S(2)}) %collective-permute-start.4) | collective-permute-done | bytes 160 | tf_op jit(solution)/shard_map/ppermute | solution.py:365
  126.3 0.7 copy.51
  127.0 0.0 collective-permute-done.7
  127.0 0.7 maximum_select_fusion.2
  127.7 0.0 all-to-all-done
  127.7 4.6 %reduce_blocks.1 = bf16[64,128,128]{2,1,0:T(8,128)(2,1)} custom-call(s32[32,2]{1,0:T(8,128)} %bitcast.55, s32[8]{0:T(128)} %ranks_hbm.3, bf16[64,128,256]{2,1,0:T(8,128)(2,1)} %bitcast.13.moved_hbm, bf16[8,256,128]{2,1,0:T(8,128)(2,1)} %copy-done.2), custom_call_target="tpu_custom_call" | custom-call | flops 600000000 | bytes 7000000 | tf_op jit(solution)/shard_map/reduce_blocks/pallas_call | solution.py:333
  (14 shorter events, 0.2 us)
Async XLA Ops:
  7.8 11.8 %copy-start.7 = (s32[32,2]{1,0:T(8,128)S(1)}, s32[32,2]{1,0:T(8,128)}, u32[]{:S(2)}) copy-start(s32[32,2]{1,0:T(8,128)} %get-tuple-element.7) | copy-start | bytes 772
  7.8 13.7 %copy-start = (bf16[8,256,256]{2,1,0:T(8,128)(2,1)S(1)}, bf16[8,256,256]{2,1,0:T(8,128)(2,1)}, u32[]{:S(2)}) copy-start(bf16[8,256,256]{2,1,0:T(8,128)(2,1)} %basis_ref.1) | copy-start | bytes 3145732
  7.9 13.7 %copy-start.1 = (bf16[8,256,256]{2,1,0:T(8,128)(2,1)S(1)}, bf16[8,256,256]{2,1,0:T(8,128)(2,1)}, u32[]{:S(2)}) copy-start(bf16[8,256,256]{2,1,0:T(8,128)(2,1)} %diag_ref.1) | copy-start | bytes 3145732
  7.9 13.7 %copy-start.3 = (f32[8,128,128]{2,1,0:T(8,128)S(1)}, f32[8,128,128]{2,1,0:T(8,128)}, u32[]{:S(2)}) copy-start(f32[8,128,128]{2,1,0:T(8,128)} %inverse_ref.1) | copy-start | bytes 1572868
  7.9 13.7 %copy-start.4 = (s32[8]{0:T(128)S(1)}, s32[8]{0:T(128)}, u32[]{:S(2)}) copy-start(s32[8]{0:T(128)} %ranks_hbm.3) | copy-start | bytes 100
  7.9 13.6 %copy-start.5 = (bf16[8,128,256]{2,1,0:T(8,128)(2,1)S(1)}, bf16[8,128,256]{2,1,0:T(8,128)(2,1)}, u32[]{:S(2)}) copy-start(bf16[8,128,256]{2,1,0:T(8,128)(2,1)} %get-tuple-element.9.row_ref) | copy-start | bytes 1572868
  7.9 13.6 %copy-start.6 = (s32[8,1]{0,1:T(1,128)S(1)}, s32[8,1]{0,1:T(1,128)}, u32[]{:S(2)}) copy-start(s32[8,1]{0,1:T(1,128)} %param.15) | copy-start | bytes 100
  7.9 119.8 %all-to-all-start = ((bf16[32,2,128,256]{3,2,1,0:T(8,128)(2,1)}), bf16[32,2,128,256]{3,2,1,0:T(8,128)(2,1)}, u32[]{:S(2)}, u32[]{:S(2)}) async-start(bf16[32,2,128,256]{3,2,1,0:T(8,128)(2,1)} %bitcast.47), calls=%async_computation | async-start | bytes 8388608 | tf_op jit(solution)/shard_map/all_to_all | solution.py:381
  19.8 10.4 %collective-permute-start = (s32[16,1,2]{0,2,1:T(2,128)S(1)}, s32[16,1,2]{0,2,1:T(2,128)S(1)}, u32[]{:S(2)}, u32[]{:S(2)}) collective-permute-start(s32[16,1,2]{0,2,1:T(2,128)S(1)} %bitcast.63), channel_id=1, source_target_pairs={{0,1},{1,0},{2,3},{3,2},{4,5},{5,4},{6,7},{7,6},{8,9},{9,8},{10,11... | collective-permute-start | bytes 392 | tf_op jit(solution)/shard_map/ppermute | solution.py:365
  28.9 0.9 copy-start.2
  29.8 82.2 %collective-permute-start.5 = (bf16[4,1,128,128]{3,2,0,1:T(8,128)(2,1)S(1)}, bf16[4,1,128,128]{3,2,0,1:T(8,128)(2,1)S(1)}, u32[]{:S(2)}, u32[]{:S(2)}) collective-permute-start(bf16[4,1,128,128]{3,2,0,1:T(8,128)(2,1)S(1)} %get-tuple-element.17), channel_id=1, source_target_pairs={{0,32},{32,0},{64,96},{96,64},{128,160},{160,128},{192,224},{224,1... | collective-permute-start | bytes 393224 | tf_op jit(solution)/shard_map/ppermute | solution.py:365
  30.4 6.3 %collective-permute-start.1 = (s32[8,2,2]{0,2,1:T(2,128)S(1)}, s32[8,2,2]{0,2,1:T(2,128)S(1)}, u32[]{:S(2)}, u32[]{:S(2)}) collective-permute-start(s32[8,2,2]{0,2,1:T(2,128)S(1)} %get-tuple-element.25), channel_id=1, source_target_pairs={{0,2},{1,3},{2,0},{3,1},{4,6},{5,7},{6,4},{7,5},{8,10},{9,11},{10,... | collective-permute-start | bytes 392 | tf_op jit(solution)/shard_map/ppermute | solution.py:365
  37.0 74.5 %collective-permute-start.2 = (s32[4,4,2]{1,0,2:T(4,128)S(1)}, s32[4,4,2]{1,0,2:T(4,128)S(1)}, u32[]{:S(2)}, u32[]{:S(2)}) collective-permute-start(s32[4,4,2]{1,0,2:T(4,128)S(1)} %bitcast.59), channel_id=1, source_target_pairs={{0,4},{1,5},{2,6},{3,7},{4,0},{5,1},{6,2},{7,3},{8,12},{9,13},{10,... | collective-permute-start | bytes 392 | tf_op jit(solution)/shard_map/ppermute | solution.py:365
  112.1 6.0 %collective-permute-start.6 = (bf16[2,2,128,128]{3,2,1,0:T(8,128)(2,1)S(1)}, bf16[2,2,128,128]{3,2,1,0:T(8,128)(2,1)S(1)}, u32[]{:S(2)}, u32[]{:S(2)}) collective-permute-start(bf16[2,2,128,128]{3,2,1,0:T(8,128)(2,1)S(1)} %get-tuple-element.15), channel_id=1, source_target_pairs={{0,64},{32,96},{64,0},{96,32},{128,192},{160,224},{192,128},{224,1... | collective-permute-start | bytes 393224 | tf_op jit(solution)/shard_map/ppermute | solution.py:365
  113.4 4.5 %collective-permute-start.3 = (s32[2,8,2]{1,2,0:T(2,128)S(1)}, s32[2,8,2]{1,2,0:T(2,128)S(1)}, u32[]{:S(2)}, u32[]{:S(2)}) collective-permute-start(s32[2,8,2]{1,2,0:T(2,128)S(1)} %get-tuple-element.23), channel_id=1, source_target_pairs={{0,8},{1,9},{2,10},{3,11},{4,12},{5,13},{6,14},{7,15},{8,0},{9,1},... | collective-permute-start | bytes 392 | tf_op jit(solution)/shard_map/ppermute | solution.py:365
  118.1 8.9 %collective-permute-start.7 = (bf16[1,4,128,128]{3,2,1,0:T(8,128)(2,1)S(1)}, bf16[1,4,128,128]{3,2,1,0:T(8,128)(2,1)S(1)}, u32[]{:S(2)}, u32[]{:S(2)}) collective-permute-start(bf16[1,4,128,128]{3,2,1,0:T(8,128)(2,1)S(1)} %get-tuple-element.13), channel_id=1, source_target_pairs={{0,128},{32,160},{64,192},{96,224},{128,0},{160,32},{192,64},{224,... | collective-permute-start | bytes 393224 | tf_op jit(solution)/shard_map/ppermute | solution.py:365
  118.8 7.5 %collective-permute-start.4 = (s32[1,16,2]{1,2,0:T(2,128)S(1)}, s32[1,16,2]{1,2,0:T(2,128)S(1)}, u32[]{:S(2)}, u32[]{:S(2)}) collective-permute-start(s32[1,16,2]{1,2,0:T(2,128)S(1)} %get-tuple-element.27), channel_id=1, source_target_pairs={{0,16},{1,17},{2,18},{3,19},{4,20},{5,21},{6,22},{7,23},{8,24},{9,... | collective-permute-start | bytes 392 | tf_op jit(solution)/shard_map/ppermute | solution.py:365

commit v2 on v1

v2 whole, which is shorter than its diff:
```python
import functools

import jax
import jax.numpy as jnp
from jax import lax
from jax.experimental import pallas as pl
from jax.experimental.pallas import tpu as pltpu
from jax.sharding import PartitionSpec as P

BF16 = jnp.bfloat16
F32 = jnp.float32
CAPACITY = 2
NOTE_ROWS = 16


def dot(a, b):
    return jnp.dot(a, b, preferred_element_type=F32)


def dot_nt(a, b):
    return lax.dot_general(a, b, (((1,), (1,)), ((), ())), preferred_element_type=F32)


def halves(x):
    high = x.astype(BF16)
    return high, (x - high.astype(F32)).astype(BF16)


def dot_wide(a, b):
    a_high, a_low = halves(a)
    b_high, b_low = halves(b)
    upper = jnp.concatenate([b_high, b_low], 1)
    lower = jnp.concatenate([b_high, jnp.zeros_like(b_low)], 1)
    both = dot(jnp.concatenate([a_high, a_low], 1), jnp.concatenate([upper, lower], 0))
    return both[:, : b.shape[1]] + both[:, b.shape[1] :]


def move_kernel(
    near_count,
    groups,
    targets_hbm,
    locals_hbm,
    ranks_hbm,
    bases_hbm,
    diag_hbm,
    inverse_hbm,
    near_hbm,
    send_hbm,
    row_hbm,
    targets,
    locals_,
    ranks,
    bases,
    diag,
    inverse,
    near,
    rows,
    moved,
    notes,
    count,
    place,
    codes,
    int_sem,
    in_sem,
    near_sem,
    out_sem,
    row_sem,
):
    local_count, block, _ = bases.shape
    redundant = inverse.shape[1]
    skeleton = block - redundant
    members = []
    for size in groups:
        first = members[-1][-1] + 1 if members else 0
        members.append(range(first, first + size))
    ints = (
        pltpu.make_async_copy(targets_hbm, targets, int_sem.at[0]),
        pltpu.make_async_copy(ranks_hbm, ranks, int_sem.at[1]),
        pltpu.make_async_copy(locals_hbm, locals_, int_sem.at[2]),
    )
    body = CAPACITY * 2 * skeleton
    note_copy = pltpu.make_async_copy(
        notes, send_hbm.at[:, pl.ds(body, NOTE_ROWS)], row_sem.at[1]
    )
    row_copy = pltpu.make_async_copy(rows, row_hbm, row_sem.at[0])

    def part(g):
        return pl.ds(members[g][0], len(members[g]))

    def inputs(g):
        return (
            pltpu.make_async_copy(bases_hbm.at[part(g)], bases.at[part(g)], in_sem.at[g, 0]),
            pltpu.make_async_copy(diag_hbm.at[part(g)], diag.at[part(g)], in_sem.at[g, 1]),
            pltpu.make_async_copy(inverse_hbm.at[part(g)], inverse.at[part(g)], in_sem.at[g, 2]),
        )

    def near_copy(g):
        return pltpu.make_async_copy(near_hbm.at[part(g)], near.at[part(g)], near_sem.at[g])

    def out_copy(c, k):
        row = pl.multiple_of(place[c, k] * 2 * skeleton, 2 * skeleton)
        target = send_hbm.at[targets[c, k], pl.ds(row, 2 * skeleton)]
        return pltpu.make_async_copy(moved.at[c, k], target, out_sem.at[c, k])

    for g in range(len(groups)):
        for copy in inputs(g):
            copy.start()
        if g == 0:
            for copy in ints:
                copy.start()
        near_copy(g).start()

    def clear(d, carry):
        count[d] = 0
        for s in range(CAPACITY):
            codes[d, s] = -1
        return carry

    lax.fori_loop(0, count.shape[0], clear, 0)
    for copy in ints:
        copy.wait()

    def assign(l, carry):
        for k in range(near_count):
            d = targets[l, k]
            s = count[d]
            place[l, k] = s
            count[d] = s + 1
            codes[d, s] = locals_[l, k]
        return carry

    lax.fori_loop(0, local_count, assign, 0)

    lanes = lax.broadcasted_iota(jnp.int32, notes.shape[1:], 1)

    def write_note(d, carry):
        note = jnp.full(notes.shape[1:], -1, jnp.int32)
        for s in range(CAPACITY):
            note = jnp.where(lanes == s, codes[d, s], note)
        notes[d] = note.astype(F32).astype(BF16)
        return carry

    lax.fori_loop(0, count.shape[0], write_note, 0)
    note_copy.start()

    def prepare(g):
        red = [bases[c][:, :redundant] for c in members[g]]
        skel_t = [bases[c][:, redundant:].T for c in members[g]]
        left = [dot(s, diag[c]).astype(BF16) for s, c in zip(skel_t, members[g])]
        factor = [dot(l, r) for l, r in zip(left, red)]
        lower = [halves(dot_wide(f, inverse[c])) for f, c in zip(factor, members[g])]
        taken = [
            dot_nt(jnp.concatenate(pair, 1), jnp.concatenate([r, r], 1))
            for pair, r in zip(lower, red)
        ]
        for c, s, t in zip(members[g], skel_t, taken):
            rows[c] = (s.astype(F32) - t).astype(BF16)

    rows_at = lax.broadcasted_iota(jnp.int32, (skeleton, block), 0)

    def move(g):
        for c in members[g]:
            keep = rows_at < ranks[c]
            row = rows[c]
            for k in range(near_count):
                product = jnp.where(keep, dot(row, near[c, k]), 0.0).astype(BF16)
                moved[c, k, :skeleton] = product[:, :skeleton]
                moved[c, k, skeleton:] = product[:, skeleton:]

    def send_one(c, carry):
        for k in range(near_count):
            out_copy(c, k).start()
        return carry

    def finish_one(c, carry):
        for k in range(near_count):
            out_copy(c, k).wait()
        return carry

    for copy in inputs(0):
        copy.wait()
    prepare(0)
    for g in range(len(groups)):
        near_copy(g).wait()
        if g + 1 < len(groups):
            for copy in inputs(g + 1):
                copy.wait()
        move(g)
        if g + 1 < len(groups):
            prepare(g + 1)
        lax.fori_loop(members[g][0], members[g][-1] + 1, send_one, 0)
        if g + 2 == len(groups):
            row_copy.start()
    row_copy.wait()
    note_copy.wait()
    lax.fori_loop(0, local_count, finish_one, 0)


def move_blocks(near_blocks, diag_blocks, bases, diag_inverses, col_device, col_local, ranks, buckets):
    local_count, near_count, block, _ = near_blocks.shape
    redundant = diag_inverses.shape[1]
    skeleton = block - redundant
    groups = (2, 3, 3)
    hbm = pl.BlockSpec(memory_space=pl.ANY)
    dma = pltpu.SemaphoreType.DMA
    return pl.pallas_call(
        functools.partial(move_kernel, near_count, groups),
        out_shape=(
            jax.ShapeDtypeStruct((buckets, CAPACITY * block + NOTE_ROWS, skeleton), BF16),
            jax.ShapeDtypeStruct((local_count, skeleton, block), BF16),
        ),
        in_specs=[hbm] * 7,
        out_specs=(hbm, hbm),
        scratch_shapes=[
            pltpu.SMEM((local_count, near_count), jnp.int32),
            pltpu.SMEM((local_count, near_count), jnp.int32),
            pltpu.SMEM((local_count,), jnp.int32),
            pltpu.VMEM((local_count, block, block), BF16),
            pltpu.VMEM((local_count, block, block), BF16),
            pltpu.VMEM((local_count, redundant, redundant), F32),
            pltpu.VMEM((local_count, near_count, block, block), BF16),
            pltpu.VMEM((local_count, skeleton, block), BF16),
            pltpu.VMEM((local_count, near_count, 2 * skeleton, skeleton), BF16),
            pltpu.VMEM((buckets, NOTE_ROWS, skeleton), BF16),
            pltpu.SMEM((buckets,), jnp.int32),
            pltpu.SMEM((local_count, near_count), jnp.int32),
            pltpu.SMEM((buckets, CAPACITY), jnp.int32),
            dma((3,)),
            dma((len(groups), 3)),
            dma((len(groups),)),
            dma((local_count, near_count)),
            dma((2,)),
        ],
        compiler_params=pltpu.CompilerParams(vmem_limit_bytes=56 * 2**20),
        cost_estimate=pl.CostEstimate(
            flops=2 * 10**9, bytes_accessed=13 * 10**6, transcendentals=0
        ),
        name="move_blocks",
    )(col_device, col_local, ranks, bases, diag_blocks, diag_inverses, near_blocks)


def diagonal_kernel(parent, ranks, basis_ref, diag_ref, inverse_ref, row_ref, out_ref, col_ref):
    c = pl.program_id(0)
    redundant = inverse_ref.shape[1]
    basis = basis_ref[0]
    diagonal = diag_ref[0]
    red = basis[:, :redundant]
    skel = basis[:, redundant:]
    left = dot(red.T, diagonal).astype(BF16)
    upper = dot_wide(inverse_ref[0], dot(left, skel))
    high, low = halves(upper)
    col = (skel.astype(F32) - (dot(red, high) + dot(red, low))).astype(BF16)
    col_ref[0] = col
    reduced = dot(dot(row_ref[0], diagonal).astype(BF16), col)
    rank = ranks[c]
    rows_at = lax.broadcasted_iota(jnp.int32, reduced.shape, 0)
    cols_at = lax.broadcasted_iota(jnp.int32, reduced.shape, 1)
    keep = (rows_at < rank) & (cols_at < rank)
    out_ref[0] = jnp.where(keep, reduced, 0.0).astype(BF16)


def diagonal_part(bases, diag_blocks, diag_inverses, row_basis, ranks, parent_group):
    local_count, block, _ = bases.shape
    redundant = diag_inverses.shape[1]
    skeleton = block - redundant

    def own(*shape):
        return pl.BlockSpec((1,) + shape, lambda c, parent, ranks: (c, 0, 0))

    return pl.pallas_call(
        diagonal_kernel,
        out_shape=(
            jax.ShapeDtypeStruct((local_count, skeleton, skeleton), BF16),
            jax.ShapeDtypeStruct((local_count, block, skeleton), BF16),
        ),
        grid_spec=pltpu.PrefetchScalarGridSpec(
            num_scalar_prefetch=2,
            grid=(local_count,),
            in_specs=[
                own(block, block),
                own(block, block),
                own(redundant, redundant),
                own(skeleton, block),
            ],
            out_specs=[
                pl.BlockSpec(
                    (1, skeleton, skeleton), lambda c, parent, ranks: (parent[c], 0, 0)
                ),
                own(block, skeleton),
            ],
        ),
        compiler_params=pltpu.CompilerParams(vmem_limit_bytes=16 * 2**20),
        cost_estimate=pl.CostEstimate(
            flops=10**9, bytes_accessed=4 * 10**6, transcendentals=0
        ),
        name="diagonal_part",
    )(parent_group[:, 0], ranks, bases, diag_blocks, diag_inverses, row_basis)


def reduce_kernel(
    chunk,
    ranks_hbm,
    came_hbm,
    col_hbm,
    out_hbm,
    ranks,
    came,
    notes,
    local_rows,
    locals_,
    col,
    out,
    first_sem,
    in_sem,
    out_sem,
):
    sources = came.shape[0]
    skeleton = came.shape[2]
    body = came.shape[1]
    steps = sources // chunk
    ranks_copy = pltpu.make_async_copy(ranks_hbm, ranks, first_sem.at[0])
    col_copy = pltpu.make_async_copy(col_hbm, col, first_sem.at[1])
    note_copy = pltpu.make_async_copy(
        came_hbm.at[:, pl.ds(body, NOTE_ROWS)], notes, first_sem.at[2]
    )
    local_copy = pltpu.make_async_copy(local_rows, locals_, first_sem.at[3])

    def in_copy(i):
        part = pl.ds(i * chunk, chunk)
        return pltpu.make_async_copy(
            came_hbm.at[part, pl.ds(0, body)], came.at[part], in_sem.at[i]
        )

    def out_copy(i):
        part = pl.ds(i * chunk * CAPACITY, chunk * CAPACITY)
        return pltpu.make_async_copy(out.at[part], out_hbm.at[part], out_sem.at[i])

    note_copy.start()
    ranks_copy.start()
    col_copy.start()
    for i in range(steps):
        in_copy(i).start()
    note_copy.wait()
    local_rows[...] = notes[:, 0, :].astype(F32).astype(jnp.int32)
    local_copy.start()
    ranks_copy.wait()
    col_copy.wait()
    local_copy.wait()
    cols_at = lax.broadcasted_iota(jnp.int32, out.shape[1:], 1)

    def step(i, carry):
        in_copy(i).wait()
        for j in range(chunk):
            source = i * chunk + j
            for s in range(CAPACITY):
                local = locals_[source, s]
                owner = jnp.maximum(local, 0)
                rank = jnp.where(local < 0, 0, ranks[owner])
                top = 2 * s * skeleton
                moved = jnp.concatenate(
                    [came[source, pl.ds(top, skeleton)], came[source, pl.ds(top + skeleton, skeleton)]],
                    1,
                )
                product = dot(moved, col[owner])
                out[source * CAPACITY + s] = jnp.where(cols_at < rank, product, 0.0).astype(BF16)
        out_copy(i).start()
        return carry

    lax.fori_loop(0, steps, step, 0)
    for i in range(steps):
        out_copy(i).wait()


def reduce_blocks(received, col_basis, ranks):
    sources, rows, skeleton = received.shape
    body = rows - NOTE_ROWS
    chunk = 16
    hbm = pl.BlockSpec(memory_space=pl.ANY)
    dma = pltpu.SemaphoreType.DMA
    return pl.pallas_call(
        functools.partial(reduce_kernel, chunk),
        out_shape=jax.ShapeDtypeStruct((sources * CAPACITY, skeleton, skeleton), BF16),
        in_specs=[hbm] * 3,
        out_specs=hbm,
        scratch_shapes=[
            pltpu.SMEM(ranks.shape, jnp.int32),
            pltpu.VMEM((sources, body, skeleton), BF16),
            pltpu.VMEM((sources, NOTE_ROWS, skeleton), BF16),
            pltpu.VMEM((sources, skeleton), jnp.int32),
            pltpu.SMEM((sources, skeleton), jnp.int32),
            pltpu.VMEM(col_basis.shape, BF16),
            pltpu.VMEM((sources * CAPACITY, skeleton, skeleton), BF16),
            dma((4,)),
            dma((sources // chunk,)),
            dma((sources // chunk,)),
        ],
        compiler_params=pltpu.CompilerParams(vmem_limit_bytes=56 * 2**20),
        cost_estimate=pl.CostEstimate(
            flops=6 * 10**8, bytes_accessed=7 * 10**6, transcendentals=0
        ),
        name="reduce_blocks",
    )(ranks, received, col_basis)


def swap_halves(x, axis_name):
    size = lax.axis_size(axis_name)
    me = lax.axis_index(axis_name)
    bit = 1
    while bit < size:
        pairs = x.reshape((size // (2 * bit), 2, bit) + x.shape[1:])
        mine = (me // bit) % 2
        kept = lax.dynamic_index_in_dim(pairs, mine, 1, keepdims=False)
        given = lax.dynamic_index_in_dim(pairs, 1 - mine, 1, keepdims=False)
        got = lax.ppermute(given, axis_name, [(i, i ^ bit) for i in range(size)])
        low, high = jnp.stack([kept, got], 1), jnp.stack([got, kept], 1)
        x = jnp.where(mine == 0, low, high).reshape(x.shape)
        bit *= 2
    return x


def on_device(
    near_blocks, diag_blocks, bases, diag_inverses, col_device, col_local, ranks, parent_group
):
    buckets = lax.axis_size("clu")
    local_count = ranks.shape[0]
    send, row_basis = move_blocks(
        near_blocks, diag_blocks, bases, diag_inverses, col_device, col_local, ranks, buckets
    )
    skeleton = send.shape[2]
    received = lax.all_to_all(send, "clu", 0, 0, tiled=True)
    outgoing, col_basis = diagonal_part(
        bases, diag_blocks, diag_inverses, row_basis, ranks, parent_group
    )
    merged = swap_halves(outgoing, "grp").reshape(local_count // 2, 2, skeleton, skeleton)
    reduced = reduce_blocks(received, col_basis, ranks)
    return reduced.reshape(1, buckets, CAPACITY, skeleton, skeleton), merged


def solution(mesh):
    in_specs = (
        P(("grp", "clu"), None, None, None),
        P(("grp", "clu"), None, None),
        P(("grp", "clu"), None, None),
        P(("grp", "clu"), None, None),
        P(("grp", "clu"), None),
        P(("grp", "clu"), None),
        P(("grp", "clu")),
        P(("grp", "clu"), None),
    )
    out_specs = (P(("grp", "clu"), None, None, None, None), P(("grp", "clu"), None, None, None))
    return jax.shard_map(
        on_device, mesh=mesh, in_specs=in_specs, out_specs=out_specs, check_vma=False
    )
```

time: 135 us -> 122 us (0.904)
  starting transfers between devices: 26.8 us -> 13.6 us
  waiting for transfers between devices: 81.6 us -> 85.9 us
  local copies, waits for them, and re-layouts: 2.78 us -> 0.97 us
  Pallas kernels: 19.2 us -> 17.7 us
    all_to_all x1, waiting for transfers between devices: 0.01 us -> 74.2 us  [on_device(): received = lax.all_to_all(send, 'clu', 0, 0, tiled=True)]
    ppermute x8 -> x3, waiting for transfers between devices: 81.6 us -> 11.7 us  [swap_halves(): got = lax.ppermute(given, axis_name, [(i, i ^ bit) for i in range(size)])]
    ppermute x8 -> x3, starting transfers between devices: 15.1 us -> 1.86 us  [swap_halves(): got = lax.ppermute(given, axis_name, [(i, i ^ bit) for i in range(size)])]
  transfers between devices with their start and end apart: 9 -> 4, of which waited for: 4 -> 4; matrix products, arithmetic and copies ran while one was open for 2% -> 1% of each run, Pallas kernels for 6% -> 6%
where the time goes in v2:
time: 122 us; the launch traced here: 120 us
  waiting for transfers between devices  85.9 us (70%)
  Pallas kernels  17.7 us (15%)
  starting transfers between devices  13.6 us (11%)
    all_to_all x1, waiting for transfers between devices, on_device(): received = lax.all_to_all(send, 'clu', 0, 0, tiled=True)  74.2 us
    all_to_all x1, starting transfers between devices, on_device(): received = lax.all_to_all(send, 'clu', 0, 0, tiled=True)  11.7 us
    ppermute x3, waiting for transfers between devices, swap_halves(): got = lax.ppermute(given, axis_name, [(i, i ^ bit) for i in range(size)])  11.7 us
    pallas_call x1, Pallas kernels, diagonal_part(): pl.pallas_call(diagonal_kernel, out_shape=(jax.ShapeDtypeStruct((local_co...  7.38 us
    pallas_call x1, Pallas kernels, move_blocks(): pl.pallas_call(functools.partial(move_kernel, near_count, groups), out_sh...  6.11 us
    pallas_call x1, Pallas kernels, reduce_blocks(): pl.pallas_call(functools.partial(reduce_kernel, chunk), out_shape=jax.Sha...  4.21 us
  transfers between devices with their start and end apart: 4, of which 4 were waited for; matrix products, arithmetic and copies ran while one was open for 1% of the time, Pallas kernels for 6%

profile of v2, /device:TPU:16, one launch (start us, length us, event | category | flops | bytes accessed | tf_op | source)
XLA Modules:
  0.0 119.8 jit_solution(9104247817375450683)
XLA Ops:
  0.6 6.1 %move_blocks.1 = (bf16[32,528,128]{2,1,0:T(8,128)(2,1)}, bf16[8,128,256]{2,1,0:T(8,128)(2,1)}) custom-call(s32[8,6]{1,0:T(8,128)} %targets_hbm.1, s32[8,6]{1,0:T(8,128)} %locals_hbm.1, s32[8]{0:T(128)} %ranks_hbm.3, bf16[8,256,256]{2,1,0:T(8,128)(2,1)} %basis_ref.1, bf16[8,256,256]{2,1,0:T(8,128)(2,1)} %diag_ref.1, f32[8,128,128]{2,1,0:T(8,128)} %inverse_ref.1, ...), custom_call_target="tpu_custom_call" | custom-call | flops 2000000000 | bytes 13000000 | tf_op jit(solution)/shard_map/move_blocks/pallas_call | solution.py:206
  6.7 0.0 copy-start
  6.8 0.0 copy-start.1
  6.8 0.0 copy-start.3
  6.8 0.0 copy-start.4
  6.8 0.0 copy-start.5
  6.8 0.0 copy-start.6
  6.8 11.7 %all-to-all-start = ((bf16[32,528,128]{2,1,0:T(8,128)(2,1)}), bf16[32,528,128]{2,1,0:T(8,128)(2,1)}, u32[]{:S(2)}, u32[]{:S(2)}) async-start(bf16[32,528,128]{2,1,0:T(8,128)(2,1)} %get-tuple-element.6), calls=%async_computation | async-start | bytes 8650752 | tf_op jit(solution)/shard_map/all_to_all | solution.py:430
  18.6 0.0 copy-done
  18.6 0.0 copy-done.1
  18.6 0.0 copy-done.3
  18.6 0.0 copy-done.4
  18.6 0.0 copy-done.5
  18.6 0.0 copy-done.6
  18.6 7.4 %diagonal_part.1 = (bf16[8,128,128]{2,1,0:T(8,128)(2,1)S(1)}, bf16[8,256,128]{2,1,0:T(8,128)(2,1)S(1)}) custom-call(s32[8]{0:T(128)S(1)} %bitcast.16, s32[8]{0:T(128)S(1)} %copy-done.4, bf16[8,256,256]{2,1,0:T(8,128)(2,1)S(1)} %copy-done, bf16[8,256,256]{2,1,0:T(8,128)(2,1)S(1)} %copy-done.1, f32[8,128,128]{2,1,0:T(8,128)S(1)} %copy-done.3, ...), custom_call_target="tpu_custom_call" | custom-call | flops 1000000000 | bytes 4000000 | tf_op jit(solution)/shard_map/diagonal_part/pallas_call | solution.py:270
  26.0 0.0 copy-start.2
  26.0 0.9 copy-done.2
  26.9 0.1 collective-permute-start
  27.1 1.3 %collective-permute-done = bf16[4,1,128,128]{3,2,0,1:T(8,128)(2,1)S(1)} collective-permute-done((bf16[4,1,128,128]{3,2,0,1:T(8,128)(2,1)S(1)}, bf16[4,1,128,128]{3,2,0,1:T(8,128)(2,1)S(1)}, u32[]{:S(2)}, u32[]{:S(2)}) %collective-permute-start) | collective-permute-done | bytes 131104 | tf_op jit(solution)/shard_map/ppermute | solution.py:414
  28.4 1.4 %collective-permute-start.1 = (bf16[2,2,128,128]{3,2,1,0:T(8,128)(2,1)S(1)}, bf16[2,2,128,128]{3,2,1,0:T(8,128)(2,1)S(1)}, u32[]{:S(2)}, u32[]{:S(2)}) collective-permute-start(bf16[2,2,128,128]{3,2,1,0:T(8,128)(2,1)S(1)} %get-tuple-element.13), channel_id=1, source_target_pairs={{0,64},{32,96},{64,0},{96,32},{128,192},{160,224},{192,128},{224,1... | collective-permute-start | bytes 393224 | tf_op jit(solution)/shard_map/ppermute | solution.py:414
  29.8 4.3 %collective-permute-done.1 = bf16[2,2,128,128]{3,2,1,0:T(8,128)(2,1)S(1)} collective-permute-done((bf16[2,2,128,128]{3,2,1,0:T(8,128)(2,1)S(1)}, bf16[2,2,128,128]{3,2,1,0:T(8,128)(2,1)S(1)}, u32[]{:S(2)}, u32[]{:S(2)}) %collective-permute-start.1) | collective-permute-done | bytes 131104 | tf_op jit(solution)/shard_map/ppermute | solution.py:414
  34.1 0.4 collective-permute-start.2
  34.5 6.1 %collective-permute-done.2 = bf16[1,4,128,128]{3,2,1,0:T(8,128)(2,1)S(1)} collective-permute-done((bf16[1,4,128,128]{3,2,1,0:T(8,128)(2,1)S(1)}, bf16[1,4,128,128]{3,2,1,0:T(8,128)(2,1)S(1)}, u32[]{:S(2)}, u32[]{:S(2)}) %collective-permute-start.2) | collective-permute-done | bytes 131104 | tf_op jit(solution)/shard_map/ppermute | solution.py:414
  40.7 0.7 maximum_select_fusion.2
  41.4 74.2 %all-to-all-done.came_hbm = bf16[32,528,128]{2,1,0:T(8,128)(2,1)} async-done(((bf16[32,528,128]{2,1,0:T(8,128)(2,1)}), bf16[32,528,128]{2,1,0:T(8,128)(2,1)}, u32[]{:S(2)}, u32[]{:S(2)}) %all-to-all-start) | async-done | bytes 4325408 | tf_op jit(solution)/shard_map/all_to_all | solution.py:430
  115.6 4.2 %reduce_blocks.1 = bf16[64,128,128]{2,1,0:T(8,128)(2,1)} custom-call(s32[8]{0:T(128)} %ranks_hbm.3, bf16[32,528,128]{2,1,0:T(8,128)(2,1)} %all-to-all-done.came_hbm, bf16[8,256,128]{2,1,0:T(8,128)(2,1)} %copy-done.2), custom_call_target="tpu_custom_call" | custom-call | flops 600000000 | bytes 7000000 | tf_op jit(solution)/shard_map/reduce_blocks/pallas_call | solution.py:380
  (5 shorter events, 0.1 us)
Async XLA Ops:
  6.7 11.8 %copy-start = (bf16[8,256,256]{2,1,0:T(8,128)(2,1)S(1)}, bf16[8,256,256]{2,1,0:T(8,128)(2,1)}, u32[]{:S(2)}) copy-start(bf16[8,256,256]{2,1,0:T(8,128)(2,1)} %basis_ref.1) | copy-start | bytes 3145732
  6.8 11.8 %copy-start.1 = (bf16[8,256,256]{2,1,0:T(8,128)(2,1)S(1)}, bf16[8,256,256]{2,1,0:T(8,128)(2,1)}, u32[]{:S(2)}) copy-start(bf16[8,256,256]{2,1,0:T(8,128)(2,1)} %diag_ref.1) | copy-start | bytes 3145732
  6.8 11.8 %copy-start.3 = (f32[8,128,128]{2,1,0:T(8,128)S(1)}, f32[8,128,128]{2,1,0:T(8,128)}, u32[]{:S(2)}) copy-start(f32[8,128,128]{2,1,0:T(8,128)} %inverse_ref.1) | copy-start | bytes 1572868
  6.8 11.8 %copy-start.4 = (s32[8]{0:T(128)S(1)}, s32[8]{0:T(128)}, u32[]{:S(2)}) copy-start(s32[8]{0:T(128)} %ranks_hbm.3) | copy-start | bytes 100
  6.8 11.8 %copy-start.5 = (bf16[8,128,256]{2,1,0:T(8,128)(2,1)S(1)}, bf16[8,128,256]{2,1,0:T(8,128)(2,1)}, u32[]{:S(2)}) copy-start(bf16[8,128,256]{2,1,0:T(8,128)(2,1)} %get-tuple-element.7.row_ref) | copy-start | bytes 1572868
  6.8 11.8 %copy-start.6 = (s32[8,1]{0,1:T(1,128)S(1)}, s32[8,1]{0,1:T(1,128)}, u32[]{:S(2)}) copy-start(s32[8,1]{0,1:T(1,128)} %param.15) | copy-start | bytes 100
  6.8 108.8 %all-to-all-start = ((bf16[32,528,128]{2,1,0:T(8,128)(2,1)}), bf16[32,528,128]{2,1,0:T(8,128)(2,1)}, u32[]{:S(2)}, u32[]{:S(2)}) async-start(bf16[32,528,128]{2,1,0:T(8,128)(2,1)} %get-tuple-element.6), calls=%async_computation | async-start | bytes 8650752 | tf_op jit(solution)/shard_map/all_to_all | solution.py:430
  26.0 0.9 copy-start.2
  26.9 1.4 %collective-permute-start = (bf16[4,1,128,128]{3,2,0,1:T(8,128)(2,1)S(1)}, bf16[4,1,128,128]{3,2,0,1:T(8,128)(2,1)S(1)}, u32[]{:S(2)}, u32[]{:S(2)}) collective-permute-start(bf16[4,1,128,128]{3,2,0,1:T(8,128)(2,1)S(1)} %get-tuple-element.15), channel_id=1, source_target_pairs={{0,32},{32,0},{64,96},{96,64},{128,160},{160,128},{192,224},{224,1... | collective-permute-start | bytes 393224 | tf_op jit(solution)/shard_map/ppermute | solution.py:414
  28.4 5.6 %collective-permute-start.1 = (bf16[2,2,128,128]{3,2,1,0:T(8,128)(2,1)S(1)}, bf16[2,2,128,128]{3,2,1,0:T(8,128)(2,1)S(1)}, u32[]{:S(2)}, u32[]{:S(2)}) collective-permute-start(bf16[2,2,128,128]{3,2,1,0:T(8,128)(2,1)S(1)} %get-tuple-element.13), channel_id=1, source_target_pairs={{0,64},{32,96},{64,0},{96,32},{128,192},{160,224},{192,128},{224,1... | collective-permute-start | bytes 393224 | tf_op jit(solution)/shard_map/ppermute | solution.py:414
  34.1 6.6 %collective-permute-start.2 = (bf16[1,4,128,128]{3,2,1,0:T(8,128)(2,1)S(1)}, bf16[1,4,128,128]{3,2,1,0:T(8,128)(2,1)S(1)}, u32[]{:S(2)}, u32[]{:S(2)}) collective-permute-start(bf16[1,4,128,128]{3,2,1,0:T(8,128)(2,1)S(1)} %get-tuple-element.11), channel_id=1, source_target_pairs={{0,128},{32,160},{64,192},{96,224},{128,0},{160,32},{192,64},{224,... | collective-permute-start | bytes 393224 | tf_op jit(solution)/shard_map/ppermute | solution.py:414

commit v3 on v2

--- a/solution.py
+++ b/solution.py
@@ -10,7 +10,9 @@
 BF16 = jnp.bfloat16
 F32 = jnp.float32
 CAPACITY = 2
-NOTE_ROWS = 16
+NOTE_ROWS = 8
+GROUPS = (2, 4, 2)
+CHUNKS = (16, 16)
 
 
 def dot(a, b):
@@ -46,7 +48,6 @@
     inverse_hbm,
     near_hbm,
     send_hbm,
-    row_hbm,
     targets,
     locals_,
     ranks,
@@ -64,7 +65,7 @@
     in_sem,
     near_sem,
     out_sem,
-    row_sem,
+    note_sem,
 ):
     local_count, block, _ = bases.shape
     redundant = inverse.shape[1]
@@ -80,9 +81,8 @@
     )
     body = CAPACITY * 2 * skeleton
     note_copy = pltpu.make_async_copy(
-        notes, send_hbm.at[:, pl.ds(body, NOTE_ROWS)], row_sem.at[1]
-    )
-    row_copy = pltpu.make_async_copy(rows, row_hbm, row_sem.at[0])
+        notes, send_hbm.at[:, pl.ds(body, NOTE_ROWS)], note_sem.at[0]
+    )
 
     def part(g):
         return pl.ds(members[g][0], len(members[g]))
@@ -189,9 +189,6 @@
         if g + 1 < len(groups):
             prepare(g + 1)
         lax.fori_loop(members[g][0], members[g][-1] + 1, send_one, 0)
-        if g + 2 == len(groups):
-            row_copy.start()
-    row_copy.wait()
     note_copy.wait()
     lax.fori_loop(0, local_count, finish_one, 0)
 
@@ -200,17 +197,16 @@
     local_count, near_count, block, _ = near_blocks.shape
     redundant = diag_inverses.shape[1]
     skeleton = block - redundant
-    groups = (2, 3, 3)
+    groups = GROUPS
     hbm = pl.BlockSpec(memory_space=pl.ANY)
     dma = pltpu.SemaphoreType.DMA
     return pl.pallas_call(
         functools.partial(move_kernel, near_count, groups),
-        out_shape=(
-            jax.ShapeDtypeStruct((buckets, CAPACITY * block + NOTE_ROWS, skeleton), BF16),
-            jax.ShapeDtypeStruct((local_count, skeleton, block), BF16),
+        out_shape=jax.ShapeDtypeStruct(
+            (buckets, CAPACITY * block + NOTE_ROWS, skeleton), BF16
         ),
         in_specs=[hbm] * 7,
-        out_specs=(hbm, hbm),
+        out_specs=hbm,
         scratch_shapes=[
             pltpu.SMEM((local_count, near_count), jnp.int32),
             pltpu.SMEM((local_count, near_count), jnp.int32),
@@ -229,7 +225,7 @@
             dma((len(groups), 3)),
             dma((len(groups),)),
             dma((local_count, near_count)),
-            dma((2,)),
+            dma((1,)),
         ],
         compiler_params=pltpu.CompilerParams(vmem_limit_bytes=56 * 2**20),
         cost_estimate=pl.CostEstimate(
@@ -239,19 +235,23 @@
     )(col_device, col_local, ranks, bases, diag_blocks, diag_inverses, near_blocks)
 
 
-def diagonal_kernel(parent, ranks, basis_ref, diag_ref, inverse_ref, row_ref, out_ref, col_ref):
+def diagonal_kernel(parent, ranks, basis_ref, diag_ref, inverse_ref, out_ref, col_ref):
     c = pl.program_id(0)
     redundant = inverse_ref.shape[1]
     basis = basis_ref[0]
     diagonal = diag_ref[0]
     red = basis[:, :redundant]
     skel = basis[:, redundant:]
-    left = dot(red.T, diagonal).astype(BF16)
-    upper = dot_wide(inverse_ref[0], dot(left, skel))
+    skel_t = skel.T
+    left = dot(basis.T, diagonal).astype(BF16)
+    upper = dot_wide(inverse_ref[0], dot(left[:redundant], skel))
+    lower = dot_wide(dot(left[redundant:], red), inverse_ref[0])
     high, low = halves(upper)
     col = (skel.astype(F32) - (dot(red, high) + dot(red, low))).astype(BF16)
     col_ref[0] = col
-    reduced = dot(dot(row_ref[0], diagonal).astype(BF16), col)
+    high, low = halves(lower)
+    row = (skel_t.astype(F32) - (dot_nt(high, red) + dot_nt(low, red))).astype(BF16)
+    reduced = dot(dot(row, diagonal).astype(BF16), col)
     rank = ranks[c]
     rows_at = lax.broadcasted_iota(jnp.int32, reduced.shape, 0)
     cols_at = lax.broadcasted_iota(jnp.int32, reduced.shape, 1)
@@ -259,7 +259,7 @@
     out_ref[0] = jnp.where(keep, reduced, 0.0).astype(BF16)
 
 
-def diagonal_part(bases, diag_blocks, diag_inverses, row_basis, ranks, parent_group):
+def diagonal_part(bases, diag_blocks, diag_inverses, ranks, parent_group):
     local_count, block, _ = bases.shape
     redundant = diag_inverses.shape[1]
     skeleton = block - redundant
@@ -280,7 +280,6 @@
                 own(block, block),
                 own(block, block),
                 own(redundant, redundant),
-                own(skeleton, block),
             ],
             out_specs=[
                 pl.BlockSpec(
@@ -294,11 +293,11 @@
             flops=10**9, bytes_accessed=4 * 10**6, transcendentals=0
         ),
         name="diagonal_part",
-    )(parent_group[:, 0], ranks, bases, diag_blocks, diag_inverses, row_basis)
+    )(parent_group[:, 0], ranks, bases, diag_blocks, diag_inverses)
 
 
 def reduce_kernel(
-    chunk,
+    chunks,
     ranks_hbm,
     came_hbm,
     col_hbm,
@@ -314,10 +313,12 @@
     in_sem,
     out_sem,
 ):
-    sources = came.shape[0]
     skeleton = came.shape[2]
     body = came.shape[1]
-    steps = sources // chunk
+    steps = []
+    for size in chunks:
+        first = steps[-1][-1] + 1 if steps else 0
+        steps.append(range(first, first + size))
     ranks_copy = pltpu.make_async_copy(ranks_hbm, ranks, first_sem.at[0])
     col_copy = pltpu.make_async_copy(col_hbm, col, first_sem.at[1])
     note_copy = pltpu.make_async_copy(
@@ -326,19 +327,19 @@
     local_copy = pltpu.make_async_copy(local_rows, locals_, first_sem.at[3])
 
     def in_copy(i):
-        part = pl.ds(i * chunk, chunk)
+        part = pl.ds(steps[i][0], len(steps[i]))
         return pltpu.make_async_copy(
             came_hbm.at[part, pl.ds(0, body)], came.at[part], in_sem.at[i]
         )
 
     def out_copy(i):
-        part = pl.ds(i * chunk * CAPACITY, chunk * CAPACITY)
+        part = pl.ds(steps[i][0] * CAPACITY, len(steps[i]) * CAPACITY)
         return pltpu.make_async_copy(out.at[part], out_hbm.at[part], out_sem.at[i])
 
     note_copy.start()
     ranks_copy.start()
     col_copy.start()
-    for i in range(steps):
+    for i in range(len(steps)):
         in_copy(i).start()
     note_copy.wait()
     local_rows[...] = notes[:, 0, :].astype(F32).astype(jnp.int32)
@@ -348,37 +349,31 @@
     local_copy.wait()
     cols_at = lax.broadcasted_iota(jnp.int32, out.shape[1:], 1)
 
-    def step(i, carry):
+    for i in range(len(steps)):
         in_copy(i).wait()
-        for j in range(chunk):
-            source = i * chunk + j
+        for source in steps[i]:
             for s in range(CAPACITY):
                 local = locals_[source, s]
                 owner = jnp.maximum(local, 0)
                 rank = jnp.where(local < 0, 0, ranks[owner])
                 top = 2 * s * skeleton
-                moved = jnp.concatenate(
-                    [came[source, pl.ds(top, skeleton)], came[source, pl.ds(top + skeleton, skeleton)]],
-                    1,
-                )
-                product = dot(moved, col[owner])
+                left = came[source, pl.ds(top, skeleton)]
+                right = came[source, pl.ds(top + skeleton, skeleton)]
+                product = dot(jnp.concatenate([left, right], 1), col[owner])
                 out[source * CAPACITY + s] = jnp.where(cols_at < rank, product, 0.0).astype(BF16)
         out_copy(i).start()
-        return carry
-
-    lax.fori_loop(0, steps, step, 0)
-    for i in range(steps):
+    for i in range(len(steps)):
         out_copy(i).wait()
 
 
 def reduce_blocks(received, col_basis, ranks):
     sources, rows, skeleton = received.shape
     body = rows - NOTE_ROWS
-    chunk = 16
+    chunks = CHUNKS
     hbm = pl.BlockSpec(memory_space=pl.ANY)
     dma = pltpu.SemaphoreType.DMA
     return pl.pallas_call(
-        functools.partial(reduce_kernel, chunk),
+        functools.partial(reduce_kernel, chunks),
         out_shape=jax.ShapeDtypeStruct((sources * CAPACITY, skeleton, skeleton), BF16),
         in_specs=[hbm] * 3,
         out_specs=hbm,
@@ -391,8 +386,8 @@
             pltpu.VMEM(col_basis.shape, BF16),
             pltpu.VMEM((sources * CAPACITY, skeleton, skeleton), BF16),
             dma((4,)),
-            dma((sources // chunk,)),
-            dma((sources // chunk,)),
+            dma((len(chunks),)),
+            dma((len(chunks),)),
         ],
         compiler_params=pltpu.CompilerParams(vmem_limit_bytes=56 * 2**20),
         cost_estimate=pl.CostEstimate(
@@ -423,13 +418,13 @@
 ):
     buckets = lax.axis_size("clu")
     local_count = ranks.shape[0]
-    send, row_basis = move_blocks(
+    send = move_blocks(
         near_blocks, diag_blocks, bases, diag_inverses, col_device, col_local, ranks, buckets
     )
     skeleton = send.shape[2]
     received = lax.all_to_all(send, "clu", 0, 0, tiled=True)
     outgoing, col_basis = diagonal_part(
-        bases, diag_blocks, diag_inverses, row_basis, ranks, parent_group
+        bases, diag_blocks, diag_inverses, ranks, parent_group
     )
     merged = swap_halves(outgoing, "grp").reshape(local_count // 2, 2, skeleton, skeleton)
     reduced = reduce_blocks(received, col_basis, ranks)

time: 122 us -> 120 us (0.984)
  waiting for transfers between devices: 85.9 us -> 82.9 us
  Pallas kernels: 17.7 us -> 19.3 us
    all_to_all x1, waiting for transfers between devices: 74.2 us -> 71.2 us  [on_device(): received = lax.all_to_all(send, 'clu', 0, 0, tiled=True)]
    pallas_call x1, Pallas kernels: 7.38 us -> 9.06 us  [diagonal_part(): pl.pallas_call(diagonal_kernel, out_shape=(jax.ShapeDtypeStruct((local_co...]
  transfers between devices with their start and end apart: 4 -> 4, of which waited for: 4 -> 4; matrix products, arithmetic and copies ran while one was open for 1% -> 1% of each run, Pallas kernels for 6% -> 8%
where the time goes in v3:
time: 120 us; the launch traced here: 118 us
  waiting for transfers between devices  82.9 us (69%)
  Pallas kernels  19.3 us (16%)
  starting transfers between devices  13.5 us (11%)
    all_to_all x1, waiting for transfers between devices, on_device(): received = lax.all_to_all(send, 'clu', 0, 0, tiled=True)  71.2 us
    ppermute x3, waiting for transfers between devices, swap_halves(): got = lax.ppermute(given, axis_name, [(i, i ^ bit) for i in range(size)])  11.7 us
    all_to_all x1, starting transfers between devices, on_device(): received = lax.all_to_all(send, 'clu', 0, 0, tiled=True)  11.6 us
    pallas_call x1, Pallas kernels, diagonal_part(): pl.pallas_call(diagonal_kernel, out_shape=(jax.ShapeDtypeStruct((local_co...  9.06 us
    pallas_call x1, Pallas kernels, move_blocks(): pl.pallas_call(functools.partial(move_kernel, near_count, groups), out_sh...  6.11 us
    pallas_call x1, Pallas kernels, reduce_blocks(): pl.pallas_call(functools.partial(reduce_kernel, chunks), out_shape=jax.Sh...  4.17 us
  transfers between devices with their start and end apart: 4, of which 4 were waited for; matrix products, arithmetic and copies ran while one was open for 1% of the time, Pallas kernels for 8%

profile of v3, /device:TPU:16, one launch (start us, length us, event | category | flops | bytes accessed | tf_op | source)
XLA Modules:
  0.0 118.3 jit_solution(7623592651145226184)
XLA Ops:
  0.6 6.1 %move_blocks.1 = bf16[32,520,128]{2,1,0:T(8,128)(2,1)} custom-call(s32[8,6]{1,0:T(8,128)} %targets_hbm.1, s32[8,6]{1,0:T(8,128)} %locals_hbm.1, s32[8]{0:T(128)} %ranks_hbm.3, bf16[8,256,256]{2,1,0:T(8,128)(2,1)} %basis_ref.1, bf16[8,256,256]{2,1,0:T(8,128)(2,1)} %diag_ref.1, f32[8,128,128]{2,1,0:T(8,128)} %inverse_ref.1, bf16[8,6,256,256]{3,2,1,0:T(8,128)(2,1)} %near_hbm.1), custom_call_target="tpu_custom_call" | custom-call | flops 2000000000 | bytes 13000000 | tf_op jit(solution)/shard_map/move_blocks/pallas_call | solution.py:203
  6.7 0.0 copy-start
  6.8 0.0 copy-start.1
  6.8 0.0 copy-start.2
  6.8 0.0 copy-start.4
  6.8 0.0 copy-start.5
  6.8 11.6 %all-to-all-start = ((bf16[32,520,128]{2,1,0:T(8,128)(2,1)}), bf16[32,520,128]{2,1,0:T(8,128)(2,1)}, u32[]{:S(2)}, u32[]{:S(2)}) async-start(bf16[32,520,128]{2,1,0:T(8,128)(2,1)} %move_blocks.1), calls=%async_computation | async-start | bytes 8519680 | tf_op jit(solution)/shard_map/all_to_all | solution.py:425
  18.4 0.0 copy-done
  18.4 0.0 copy-done.1
  18.4 0.0 copy-done.2
  18.5 0.0 copy-done.4
  18.5 0.0 copy-done.5
  18.5 9.1 %diagonal_part.1 = (bf16[8,128,128]{2,1,0:T(8,128)(2,1)S(1)}, bf16[8,256,128]{2,1,0:T(8,128)(2,1)S(1)}) custom-call(s32[8]{0:T(128)S(1)} %bitcast.16, s32[8]{0:T(128)S(1)} %copy-done.4, bf16[8,256,256]{2,1,0:T(8,128)(2,1)S(1)} %copy-done, bf16[8,256,256]{2,1,0:T(8,128)(2,1)S(1)} %copy-done.1, f32[8,128,128]{2,1,0:T(8,128)S(1)} %copy-done.2), custom_call_target="tpu_custom_call" | custom-call | flops 1000000000 | bytes 4000000 | tf_op jit(solution)/shard_map/diagonal_part/pallas_call | solution.py:270
  27.5 0.0 copy-start.3
  27.6 0.8 copy-done.3
  28.4 0.1 collective-permute-start
  28.6 1.3 %collective-permute-done = bf16[4,1,128,128]{3,2,0,1:T(8,128)(2,1)S(1)} collective-permute-done((bf16[4,1,128,128]{3,2,0,1:T(8,128)(2,1)S(1)}, bf16[4,1,128,128]{3,2,0,1:T(8,128)(2,1)S(1)}, u32[]{:S(2)}, u32[]{:S(2)}) %collective-permute-start) | collective-permute-done | bytes 131104 | tf_op jit(solution)/shard_map/ppermute | solution.py:409
  29.9 1.4 %collective-permute-start.1 = (bf16[2,2,128,128]{3,2,1,0:T(8,128)(2,1)S(1)}, bf16[2,2,128,128]{3,2,1,0:T(8,128)(2,1)S(1)}, u32[]{:S(2)}, u32[]{:S(2)}) collective-permute-start(bf16[2,2,128,128]{3,2,1,0:T(8,128)(2,1)S(1)} %get-tuple-element.9), channel_id=1, source_target_pairs={{0,64},{32,96},{64,0},{96,32},{128,192},{160,224},{192,128},{224,1... | collective-permute-start | bytes 393224 | tf_op jit(solution)/shard_map/ppermute | solution.py:409
  31.3 4.3 %collective-permute-done.1 = bf16[2,2,128,128]{3,2,1,0:T(8,128)(2,1)S(1)} collective-permute-done((bf16[2,2,128,128]{3,2,1,0:T(8,128)(2,1)S(1)}, bf16[2,2,128,128]{3,2,1,0:T(8,128)(2,1)S(1)}, u32[]{:S(2)}, u32[]{:S(2)}) %collective-permute-start.1) | collective-permute-done | bytes 131104 | tf_op jit(solution)/shard_map/ppermute | solution.py:409
  35.6 0.4 collective-permute-start.2
  36.0 6.1 %collective-permute-done.2 = bf16[1,4,128,128]{3,2,1,0:T(8,128)(2,1)S(1)} collective-permute-done((bf16[1,4,128,128]{3,2,1,0:T(8,128)(2,1)S(1)}, bf16[1,4,128,128]{3,2,1,0:T(8,128)(2,1)S(1)}, u32[]{:S(2)}, u32[]{:S(2)}) %collective-permute-start.2) | collective-permute-done | bytes 131104 | tf_op jit(solution)/shard_map/ppermute | solution.py:409
  42.2 0.7 maximum_select_fusion.2
  42.9 71.2 %all-to-all-done.came_hbm = bf16[32,520,128]{2,1,0:T(8,128)(2,1)} async-done(((bf16[32,520,128]{2,1,0:T(8,128)(2,1)}), bf16[32,520,128]{2,1,0:T(8,128)(2,1)}, u32[]{:S(2)}, u32[]{:S(2)}) %all-to-all-start) | async-done | bytes 4259872 | tf_op jit(solution)/shard_map/all_to_all | solution.py:425
  114.1 4.2 %reduce_blocks.1 = bf16[64,128,128]{2,1,0:T(8,128)(2,1)} custom-call(s32[8]{0:T(128)} %ranks_hbm.3, bf16[32,520,128]{2,1,0:T(8,128)(2,1)} %all-to-all-done.came_hbm, bf16[8,256,128]{2,1,0:T(8,128)(2,1)} %copy-done.3), custom_call_target="tpu_custom_call" | custom-call | flops 600000000 | bytes 7000000 | tf_op jit(solution)/shard_map/reduce_blocks/pallas_call | solution.py:375
  (5 shorter events, 0.1 us)
Async XLA Ops:
  6.7 11.7 %copy-start = (bf16[8,256,256]{2,1,0:T(8,128)(2,1)S(1)}, bf16[8,256,256]{2,1,0:T(8,128)(2,1)}, u32[]{:S(2)}) copy-start(bf16[8,256,256]{2,1,0:T(8,128)(2,1)} %basis_ref.1) | copy-start | bytes 3145732
  6.8 11.7 %copy-start.1 = (bf16[8,256,256]{2,1,0:T(8,128)(2,1)S(1)}, bf16[8,256,256]{2,1,0:T(8,128)(2,1)}, u32[]{:S(2)}) copy-start(bf16[8,256,256]{2,1,0:T(8,128)(2,1)} %diag_ref.1) | copy-start | bytes 3145732
  6.8 11.7 %copy-start.2 = (f32[8,128,128]{2,1,0:T(8,128)S(1)}, f32[8,128,128]{2,1,0:T(8,128)}, u32[]{:S(2)}) copy-start(f32[8,128,128]{2,1,0:T(8,128)} %inverse_ref.1) | copy-start | bytes 1572868
  6.8 11.7 %copy-start.4 = (s32[8]{0:T(128)S(1)}, s32[8]{0:T(128)}, u32[]{:S(2)}) copy-start(s32[8]{0:T(128)} %ranks_hbm.3) | copy-start | bytes 100
  6.8 11.7 %copy-start.5 = (s32[8,1]{0,1:T(1,128)S(1)}, s32[8,1]{0,1:T(1,128)}, u32[]{:S(2)}) copy-start(s32[8,1]{0,1:T(1,128)} %param.15) | copy-start | bytes 100
  6.8 107.3 %all-to-all-start = ((bf16[32,520,128]{2,1,0:T(8,128)(2,1)}), bf16[32,520,128]{2,1,0:T(8,128)(2,1)}, u32[]{:S(2)}, u32[]{:S(2)}) async-start(bf16[32,520,128]{2,1,0:T(8,128)(2,1)} %move_blocks.1), calls=%async_computation | async-start | bytes 8519680 | tf_op jit(solution)/shard_map/all_to_all | solution.py:425
  27.5 0.9 copy-start.3
  28.4 1.4 %collective-permute-start = (bf16[4,1,128,128]{3,2,0,1:T(8,128)(2,1)S(1)}, bf16[4,1,128,128]{3,2,0,1:T(8,128)(2,1)S(1)}, u32[]{:S(2)}, u32[]{:S(2)}) collective-permute-start(bf16[4,1,128,128]{3,2,0,1:T(8,128)(2,1)S(1)} %get-tuple-element.11), channel_id=1, source_target_pairs={{0,32},{32,0},{64,96},{96,64},{128,160},{160,128},{192,224},{224,1... | collective-permute-start | bytes 393224 | tf_op jit(solution)/shard_map/ppermute | solution.py:409
  29.9 5.6 %collective-permute-start.1 = (bf16[2,2,128,128]{3,2,1,0:T(8,128)(2,1)S(1)}, bf16[2,2,128,128]{3,2,1,0:T(8,128)(2,1)S(1)}, u32[]{:S(2)}, u32[]{:S(2)}) collective-permute-start(bf16[2,2,128,128]{3,2,1,0:T(8,128)(2,1)S(1)} %get-tuple-element.9), channel_id=1, source_target_pairs={{0,64},{32,96},{64,0},{96,32},{128,192},{160,224},{192,128},{224,1... | collective-permute-start | bytes 393224 | tf_op jit(solution)/shard_map/ppermute | solution.py:409
  35.6 6.6 %collective-permute-start.2 = (bf16[1,4,128,128]{3,2,1,0:T(8,128)(2,1)S(1)}, bf16[1,4,128,128]{3,2,1,0:T(8,128)(2,1)S(1)}, u32[]{:S(2)}, u32[]{:S(2)}) collective-permute-start(bf16[1,4,128,128]{3,2,1,0:T(8,128)(2,1)S(1)} %get-tuple-element.7), channel_id=1, source_target_pairs={{0,128},{32,160},{64,192},{96,224},{128,0},{160,32},{192,64},{224,... | collective-permute-start | bytes 393224 | tf_op jit(solution)/shard_map/ppermute | solution.py:409

commit v4 on v3

v4 whole, which is shorter than its diff:
```python
import functools

import jax
import jax.numpy as jnp
from jax import lax
from jax.experimental import pallas as pl
from jax.experimental.pallas import tpu as pltpu
from jax.sharding import PartitionSpec as P

BF16 = jnp.bfloat16
F32 = jnp.float32
CAPACITY = 2
NEAR_LINKS = 4
HALF_Z = 4


def dot(a, b):
    return jnp.dot(a, b, preferred_element_type=F32)


def dot_nt(a, b):
    return lax.dot_general(a, b, (((1,), (1,)), ((), ())), preferred_element_type=F32)


def halves(x):
    high = x.astype(BF16)
    return high, (x - high.astype(F32)).astype(BF16)


def dot_wide(a, b):
    a_high, a_low = halves(a)
    b_high, b_low = halves(b)
    upper = jnp.concatenate([b_high, b_low], 1)
    lower = jnp.concatenate([b_high, jnp.zeros_like(b_low)], 1)
    both = dot(jnp.concatenate([a_high, a_low], 1), jnp.concatenate([upper, lower], 0))
    return both[:, : b.shape[1]] + both[:, b.shape[1] :]


def move_kernel(
    near_count,
    groups,
    targets_hbm,
    ranks_hbm,
    bases_hbm,
    diag_hbm,
    inverse_hbm,
    near_hbm,
    send_hbm,
    targets,
    ranks,
    bases,
    diag,
    inverse,
    near,
    rows,
    moved,
    count,
    place,
    int_sem,
    in_sem,
    near_sem,
    out_sem,
):
    local_count, block, _ = bases.shape
    redundant = inverse.shape[1]
    skeleton = block - redundant
    members = []
    for size in groups:
        first = members[-1][-1] + 1 if members else 0
        members.append(range(first, first + size))
    ints = (
        pltpu.make_async_copy(targets_hbm, targets, int_sem.at[0]),
        pltpu.make_async_copy(ranks_hbm, ranks, int_sem.at[1]),
    )

    def part(g):
        return pl.ds(members[g][0], len(members[g]))

    def inputs(g):
        return (
            pltpu.make_async_copy(bases_hbm.at[part(g)], bases.at[part(g)], in_sem.at[g, 0]),
            pltpu.make_async_copy(diag_hbm.at[part(g)], diag.at[part(g)], in_sem.at[g, 1]),
            pltpu.make_async_copy(inverse_hbm.at[part(g)], inverse.at[part(g)], in_sem.at[g, 2]),
        )

    def near_copy(g):
        return pltpu.make_async_copy(near_hbm.at[part(g)], near.at[part(g)], near_sem.at[g])

    def out_copy(c, k):
        return pltpu.make_async_copy(moved.at[c, k], send_hbm.at[place[c, k]], out_sem.at[c, k])

    for g in range(len(groups)):
        for copy in inputs(g):
            copy.start()
        if g == 0:
            for copy in ints:
                copy.start()
        near_copy(g).start()

    def clear(d, carry):
        count[d] = 0
        return carry

    lax.fori_loop(0, count.shape[0], clear, 0)
    for copy in ints:
        copy.wait()

    def assign(l, carry):
        for k in range(near_count):
            d = targets[l, k]
            place[l, k] = d * CAPACITY + count[d]
            count[d] = count[d] + 1
        return carry

    lax.fori_loop(0, local_count, assign, 0)

    def prepare(g):
        red = [bases[c][:, :redundant] for c in members[g]]
        skel_t = [bases[c][:, redundant:].T for c in members[g]]
        left = [dot(s, diag[c]).astype(BF16) for s, c in zip(skel_t, members[g])]
        factor = [dot(l, r) for l, r in zip(left, red)]
        lower = [halves(dot_wide(f, inverse[c])) for f, c in zip(factor, members[g])]
        taken = [
            dot_nt(jnp.concatenate(pair, 1), jnp.concatenate([r, r], 1))
            for pair, r in zip(lower, red)
        ]
        for c, s, t in zip(members[g], skel_t, taken):
            rows[c] = (s.astype(F32) - t).astype(BF16)

    rows_at = lax.broadcasted_iota(jnp.int32, (skeleton, block), 0)

    def move(g):
        for c in members[g]:
            keep = rows_at < ranks[c]
            row = rows[c]
            for k in range(near_count):
                moved[c, k] = jnp.where(keep, dot(row, near[c, k]), 0.0).astype(BF16)

    def send_one(c, carry):
        for k in range(near_count):
            out_copy(c, k).start()
        return carry

    def finish_one(c, carry):
        for k in range(near_count):
            out_copy(c, k).wait()
        return carry

    for copy in inputs(0):
        copy.wait()
    prepare(0)
    for g in range(len(groups)):
        near_copy(g).wait()
        if g + 1 < len(groups):
            for copy in inputs(g + 1):
                copy.wait()
        move(g)
        if g + 1 < len(groups):
            prepare(g + 1)
        lax.fori_loop(members[g][0], members[g][-1] + 1, send_one, 0)
    lax.fori_loop(0, local_count, finish_one, 0)


def move_blocks(near_blocks, diag_blocks, bases, diag_inverses, col_device, ranks, buckets):
    local_count, near_count, block, _ = near_blocks.shape
    redundant = diag_inverses.shape[1]
    skeleton = block - redundant
    groups = (2, 4, 2)
    hbm = pl.BlockSpec(memory_space=pl.ANY)
    dma = pltpu.SemaphoreType.DMA
    return pl.pallas_call(
        functools.partial(move_kernel, near_count, groups),
        out_shape=jax.ShapeDtypeStruct((buckets * CAPACITY, skeleton, block), BF16),
        in_specs=[hbm] * 6,
        out_specs=hbm,
        scratch_shapes=[
            pltpu.SMEM((local_count, near_count), jnp.int32),
            pltpu.SMEM((local_count,), jnp.int32),
            pltpu.VMEM((local_count, block, block), BF16),
            pltpu.VMEM((local_count, block, block), BF16),
            pltpu.VMEM((local_count, redundant, redundant), F32),
            pltpu.VMEM((local_count, near_count, block, block), BF16),
            pltpu.VMEM((local_count, skeleton, block), BF16),
            pltpu.VMEM((local_count, near_count, skeleton, block), BF16),
            pltpu.SMEM((buckets,), jnp.int32),
            pltpu.SMEM((local_count, near_count), jnp.int32),
            dma((2,)),
            dma((len(groups), 3)),
            dma((len(groups),)),
            dma((local_count, near_count)),
        ],
        compiler_params=pltpu.CompilerParams(vmem_limit_bytes=56 * 2**20),
        cost_estimate=pl.CostEstimate(
            flops=2 * 10**9, bytes_accessed=13 * 10**6, transcendentals=0
        ),
        name="move_blocks",
    )(col_device, ranks, bases, diag_blocks, diag_inverses, near_blocks)


def table_kernel(me, *refs):
    inputs, table, held, count, sem = refs[:4], refs[4], refs[5:9], refs[9], refs[10]
    copies = [
        pltpu.make_async_copy(ref, place, sem.at[i])
        for i, (ref, place) in enumerate(zip(inputs, held))
    ]
    for copy in copies:
        copy.start()
    device, local, far_device, far_local = held
    local_count, near_count = device.shape
    half = HALF_Z * CAPACITY * 2
    my_side = (me[0] // NEAR_LINKS) % 2

    def blank(x, carry):
        for j in range(2 * half):
            table[x, j] = -1
        return carry

    lax.fori_loop(0, NEAR_LINKS, blank, 0)
    for copy in copies:
        copy.wait()
    for whose, (devices, locals_) in enumerate(((device, local), (far_device, far_local))):

        def clear(d, carry):
            count[d] = 0
            return carry

        def assign(l, carry):
            for k in range(near_count):
                d = devices[l, k]
                z = d // NEAR_LINKS
                away = jnp.where(z % 2 == my_side, 0, half)
                slot = count[d]
                count[d] = slot + 1
                column = (whose * HALF_Z + z // 2) * CAPACITY + slot + away
                table[d % NEAR_LINKS, column] = locals_[l, k]
            return carry

        lax.fori_loop(0, count.shape[0], clear, 0)
        lax.fori_loop(0, local_count, assign, 0)


def make_table(me, device, local, far_device, far_local, buckets):
    smem = pl.BlockSpec(memory_space=pltpu.SMEM)
    hbm = pl.BlockSpec(memory_space=pl.ANY)
    return pl.pallas_call(
        table_kernel,
        out_shape=jax.ShapeDtypeStruct((NEAR_LINKS, HALF_Z * CAPACITY * 4), jnp.int32),
        in_specs=[smem] + [hbm] * 4,
        out_specs=smem,
        scratch_shapes=[pltpu.SMEM(device.shape, jnp.int32)] * 4
        + [pltpu.SMEM((buckets,), jnp.int32), pltpu.SemaphoreType.DMA((4,))],
        compiler_params=pltpu.CompilerParams(vmem_limit_bytes=16 * 2**20),
        name="make_table",
    )(me.reshape(1), device, local, far_device, far_local)


def diagonal_kernel(parent, ranks, basis_ref, diag_ref, inverse_ref, out_ref, col_ref):
    c = pl.program_id(0)
    redundant = inverse_ref.shape[1]
    basis = basis_ref[0]
    diagonal = diag_ref[0]
    red = basis[:, :redundant]
    skel = basis[:, redundant:]
    skel_t = skel.T
    left = dot(basis.T, diagonal).astype(BF16)
    upper = dot_wide(inverse_ref[0], dot(left[:redundant], skel))
    lower = dot_wide(dot(left[redundant:], red), inverse_ref[0])
    high, low = halves(upper)
    col = (skel.astype(F32) - (dot(red, high) + dot(red, low))).astype(BF16)
    col_ref[0] = col
    high, low = halves(lower)
    row = (skel_t.astype(F32) - (dot_nt(high, red) + dot_nt(low, red))).astype(BF16)
    reduced = dot(dot(row, diagonal).astype(BF16), col)
    rank = ranks[c]
    rows_at = lax.broadcasted_iota(jnp.int32, reduced.shape, 0)
    cols_at = lax.broadcasted_iota(jnp.int32, reduced.shape, 1)
    keep = (rows_at < rank) & (cols_at < rank)
    out_ref[0] = jnp.where(keep, reduced, 0.0).astype(BF16)


def diagonal_part(bases, diag_blocks, diag_inverses, ranks, parent_group):
    local_count, block, _ = bases.shape
    redundant = diag_inverses.shape[1]
    skeleton = block - redundant

    def own(*shape):
        return pl.BlockSpec((1,) + shape, lambda c, parent, ranks: (c, 0, 0))

    return pl.pallas_call(
        diagonal_kernel,
        out_shape=(
            jax.ShapeDtypeStruct((local_count, skeleton, skeleton), BF16),
            jax.ShapeDtypeStruct((local_count, block, skeleton), BF16),
        ),
        grid_spec=pltpu.PrefetchScalarGridSpec(
            num_scalar_prefetch=2,
            grid=(local_count,),
            in_specs=[
                own(block, block),
                own(block, block),
                own(redundant, redundant),
            ],
            out_specs=[
                pl.BlockSpec(
                    (1, skeleton, skeleton), lambda c, parent, ranks: (parent[c], 0, 0)
                ),
                own(block, skeleton),
            ],
        ),
        compiler_params=pltpu.CompilerParams(vmem_limit_bytes=16 * 2**20),
        cost_estimate=pl.CostEstimate(
            flops=10**9, bytes_accessed=4 * 10**6, transcendentals=0
        ),
        name="diagonal_part",
    )(parent_group[:, 0], ranks, bases, diag_blocks, diag_inverses)


def reduce_kernel(chunk, far, *refs):
    tables_hbm = refs[:far]
    (
        me_hbm,
        ranks_hbm,
        moved_hbm,
        col_hbm,
        out_hbm,
        tables,
        me,
        ranks,
        moved,
        col,
        out,
        table_sem,
        int_sem,
        in_sem,
        out_sem,
    ) = refs[far:]
    steps = moved.shape[0] // chunk
    firsts = (
        pltpu.make_async_copy(me_hbm, me, int_sem.at[0]),
        pltpu.make_async_copy(ranks_hbm, ranks, int_sem.at[1]),
        pltpu.make_async_copy(col_hbm, col, int_sem.at[2]),
    ) + tuple(
        pltpu.make_async_copy(tables_hbm[t], tables.at[t], table_sem.at[t]) for t in range(far)
    )

    def in_copy(i):
        part = pl.ds(i * chunk, chunk)
        return pltpu.make_async_copy(moved_hbm.at[part], moved.at[part], in_sem.at[i])

    def out_copy(i):
        part = pl.ds(i * chunk, chunk)
        return pltpu.make_async_copy(out.at[part], out_hbm.at[part], out_sem.at[i])

    for copy in firsts:
        copy.start()
    for i in range(steps):
        in_copy(i).start()
    for copy in firsts:
        copy.wait()
    cols_at = lax.broadcasted_iota(jnp.int32, out.shape[1:], 1)
    my_z = me[0] // NEAR_LINKS

    for i in range(steps):
        in_copy(i).wait()
        for e in range(i * chunk, (i + 1) * chunk):
            source = e // CAPACITY
            apart = (source // NEAR_LINKS) ^ my_z
            column = (apart % 2) * CAPACITY + e % CAPACITY
            local = tables[apart // 2, source % NEAR_LINKS, column]
            owner = jnp.maximum(local, 0)
            rank = jnp.where(local < 0, 0, ranks[owner])
            out[e] = jnp.where(cols_at < rank, dot(moved[e], col[owner]), 0.0).astype(BF16)
        out_copy(i).start()
    for i in range(steps):
        out_copy(i).wait()


def reduce_blocks(moved, tables, me, col_basis, ranks):
    slots, skeleton, block = moved.shape
    far = len(tables)
    chunk = 32
    hbm = pl.BlockSpec(memory_space=pl.ANY)
    dma = pltpu.SemaphoreType.DMA
    return pl.pallas_call(
        functools.partial(reduce_kernel, chunk, far),
        out_shape=jax.ShapeDtypeStruct((slots, skeleton, skeleton), BF16),
        in_specs=[hbm] * (far + 4),
        out_specs=hbm,
        scratch_shapes=[
            pltpu.SMEM((far,) + tables[0].shape, jnp.int32),
            pltpu.SMEM((1,), jnp.int32),
            pltpu.SMEM(ranks.shape, jnp.int32),
            pltpu.VMEM(moved.shape, BF16),
            pltpu.VMEM(col_basis.shape, BF16),
            pltpu.VMEM((slots, skeleton, skeleton), BF16),
            dma((far,)),
            dma((3,)),
            dma((slots // chunk,)),
            dma((slots // chunk,)),
        ],
        compiler_params=pltpu.CompilerParams(vmem_limit_bytes=12 * 2**20),
        cost_estimate=pl.CostEstimate(
            flops=6 * 10**8, bytes_accessed=7 * 10**6, transcendentals=0
        ),
        name="reduce_blocks",
    )(*tables, me.reshape(1), ranks, moved, col_basis)


def swap_halves(x, axis_name, size):
    whole = lax.axis_size(axis_name)
    me = lax.axis_index(axis_name)
    bit = 1
    while bit < size:
        pairs = x.reshape((size // (2 * bit), 2, bit) + x.shape[1:])
        mine = (me // bit) % 2
        kept = lax.dynamic_index_in_dim(pairs, mine, 1, keepdims=False)
        given = lax.dynamic_index_in_dim(pairs, 1 - mine, 1, keepdims=False)
        got = lax.ppermute(given, axis_name, [(i, i ^ bit) for i in range(whole)])
        low, high = jnp.stack([kept, got], 1), jnp.stack([got, kept], 1)
        x = jnp.where(mine == 0, low, high).reshape(x.shape)
        bit *= 2
    return x


def on_device(
    near_blocks, diag_blocks, bases, diag_inverses, col_device, col_local, ranks, parent_group
):
    buckets = lax.axis_size("clu")
    local_count = ranks.shape[0]
    me = lax.axis_index("clu")
    across = [(i, i ^ NEAR_LINKS) for i in range(buckets)]
    far_device = lax.ppermute(col_device, "clu", across)
    far_local = lax.ppermute(col_local, "clu", across)
    send = move_blocks(
        near_blocks, diag_blocks, bases, diag_inverses, col_device, ranks, buckets
    )
    send, far_device, far_local = lax.optimization_barrier((send, far_device, far_local))
    skeleton, block = send.shape[1:]
    received = lax.all_to_all(
        send.reshape(buckets, CAPACITY, skeleton, block), "clu", 0, 0, tiled=True
    )
    outgoing, col_basis = diagonal_part(
        bases, diag_blocks, diag_inverses, ranks, parent_group
    )
    arrived = swap_halves(outgoing, "grp", lax.axis_size("grp"))
    merged = arrived.reshape(local_count // 2, 2, skeleton, skeleton)

    table = make_table(me, col_device, col_local, far_device, far_local, buckets)
    table = swap_halves(table, "clu", NEAR_LINKS)
    table, merged = lax.optimization_barrier((table, merged))
    table = table[:, : 2 * HALF_Z * CAPACITY].reshape(NEAR_LINKS, 2, HALF_Z, CAPACITY)
    my_place = me // (2 * NEAR_LINKS)
    tables = []
    for apart in range(HALF_Z):
        given = lax.dynamic_index_in_dim(table, my_place ^ apart, 2, keepdims=False)
        given = given.reshape(NEAR_LINKS, 2 * CAPACITY)
        if apart:
            pairs = [(i, i ^ (2 * apart * NEAR_LINKS)) for i in range(buckets)]
            given = lax.ppermute(given, "clu", pairs)
        tables.append(given)
    reduced = reduce_blocks(
        received.reshape(buckets * CAPACITY, skeleton, block), tables, me, col_basis, ranks
    )
    return reduced.reshape(1, buckets, CAPACITY, skeleton, skeleton), merged


def solution(mesh):
    in_specs = (
        P(("grp", "clu"), None, None, None),
        P(("grp", "clu"), None, None),
        P(("grp", "clu"), None, None),
        P(("grp", "clu"), None, None),
        P(("grp", "clu"), None),
        P(("grp", "clu"), None),
        P(("grp", "clu")),
        P(("grp", "clu"), None),
    )
    out_specs = (P(("grp", "clu"), None, None, None, None), P(("grp", "clu"), None, None, None))
    return jax.shard_map(
        on_device, mesh=mesh, in_specs=in_specs, out_specs=out_specs, check_vma=False
    )
```

time: 120 us -> 120 us (level); the launches traced: 118 us -> 120 us
  waiting for transfers between devices: 82.9 us -> 67.8 us
  starting transfers between devices: 13.5 us -> 27 us
  Pallas kernels: 19.3 us -> 22.6 us
    all_to_all x1, waiting for transfers between devices: 71.2 us -> 0.01 us  [on_device(): lax.all_to_all(send.reshape(buckets, CAPACITY, skeleton, block), 'clu', 0...]
    ppermute x3 -> x10, waiting for transfers between devices: 11.7 us -> 67.8 us  [the longest x3 62.1 us: on_device(): given = lax.ppermute(given, 'clu', pairs)]
    ppermute x3 -> x10, starting transfers between devices: 1.87 us -> 15.4 us  [the longest x5 6.8 us: swap_halves(): got = lax.ppermute(given, axis_name, [(i, i ^ bit) for i in range(whole)])]
    pallas_call x1 -> x2, Pallas kernels: 4.17 us -> 7.54 us  [the longest x1 4.15 us: reduce_blocks(): pl.pallas_call(functools.partial(reduce_kernel, chunk, far), out_shape=ja...]
  transfers between devices with their start and end apart: 4 -> 11, of which waited for: 4 -> 6; matrix products, arithmetic and copies ran while one was open for 1% -> 1% of each run, Pallas kernels for 8% -> 15%
where the time goes in v4:
time: 120 us
  waiting for transfers between devices  67.8 us (56%)
  starting transfers between devices  27 us (22%)
  Pallas kernels  22.6 us (19%)
    ppermute x3, waiting for transfers between devices, on_device(): given = lax.ppermute(given, 'clu', pairs)  62.1 us
    all_to_all x1, starting transfers between devices, on_device(): lax.all_to_all(send.reshape(buckets, CAPACITY, skeleton, block), 'clu', 0...  11.6 us
    pallas_call x1, Pallas kernels, diagonal_part(): pl.pallas_call(diagonal_kernel, out_shape=(jax.ShapeDtypeStruct((local_co...  9.06 us
    ppermute x5, starting transfers between devices, swap_halves(): got = lax.ppermute(given, axis_name, [(i, i ^ bit) for i in range(whole)])  6.8 us
    ppermute x3, starting transfers between devices, on_device(): given = lax.ppermute(given, 'clu', pairs)  6.5 us
    pallas_call x1, Pallas kernels, move_blocks(): pl.pallas_call(functools.partial(move_kernel, near_count, groups), out_sh...  6.01 us
    ppermute x5, waiting for transfers between devices, swap_halves(): got = lax.ppermute(given, axis_name, [(i, i ^ bit) for i in range(whole)])  5.71 us
    pallas_call x1, Pallas kernels, reduce_blocks(): pl.pallas_call(functools.partial(reduce_kernel, chunk, far), out_shape=ja...  4.15 us
  transfers between devices with their start and end apart: 11, of which 6 were waited for; matrix products, arithmetic and copies ran while one was open for 1% of the time, Pallas kernels for 15%

profile of v4, /device:TPU:16, one launch (start us, length us, event | category | flops | bytes accessed | tf_op | source)
XLA Modules:
  0.0 119.9 jit_solution(14794128900894276757)
XLA Ops:
  0.6 2.0 %collective-permute-start.1 = (s32[8,6]{1,0:T(8,128)}, s32[8,6]{1,0:T(8,128)S(1)}, u32[]{:S(2)}, u32[]{:S(2)}) collective-permute-start(s32[8,6]{1,0:T(8,128)} %refs_1_.1), channel_id=1, source_target_pairs={{0,4},{1,5},{2,6},{3,7},{4,0},{5,1},{6,2},{7,3},{8,12},{9,13},{10,... | collective-permute-start | bytes 584 | tf_op jit(solution)/shard_map/ppermute | solution.py:433
  2.6 0.1 collective-permute-start
  2.7 6.0 %move_blocks.1 = bf16[64,128,256]{2,1,0:T(8,128)(2,1)} custom-call(s32[8,6]{1,0:T(8,128)} %refs_0_.1, s32[8]{0:T(128)} %refs_5_.1, bf16[8,256,256]{2,1,0:T(8,128)(2,1)} %basis_ref.1, bf16[8,256,256]{2,1,0:T(8,128)(2,1)} %diag_ref.1, f32[8,128,128]{2,1,0:T(8,128)} %inverse_ref.1, bf16[8,6,256,256]{3,2,1,0:T(8,128)(2,1)} %near_hbm.1), custom_call_target="tpu_custom_call" | custom-call | flops 2000000000 | bytes 13000000 | tf_op jit(solution)/shard_map/move_blocks/pallas_call | solution.py:171
  8.8 0.0 collective-permute-done.1.refs_3_
  8.8 0.0 collective-permute-done.refs_2_
  8.8 0.0 copy-start
  8.8 0.0 copy-start.1
  8.8 0.0 copy-start.2
  8.8 0.0 copy-start.5
  8.8 0.0 copy-start.6
  8.8 11.6 %all-to-all-start = ((bf16[32,2,128,256]{3,2,1,0:T(8,128)(2,1)}), bf16[32,2,128,256]{3,2,1,0:T(8,128)(2,1)}, u32[]{:S(2)}, u32[]{:S(2)}) async-start(bf16[32,2,128,256]{3,2,1,0:T(8,128)(2,1)} %bitcast.38), calls=%async_computation | async-start | bytes 8388608 | tf_op jit(solution)/shard_map/all_to_all | solution.py:439
  20.5 0.0 copy-start.3
  20.5 0.0 copy-start.4
  20.5 0.0 copy-done
  20.5 0.0 copy-done.1
  20.5 0.0 copy-done.2
  20.5 0.0 copy-done.5
  20.5 0.0 copy-done.6
  20.6 9.1 %diagonal_part.1 = (bf16[8,128,128]{2,1,0:T(8,128)(2,1)S(1)}, bf16[8,256,128]{2,1,0:T(8,128)(2,1)S(1)}) custom-call(s32[8]{0:T(128)S(1)} %bitcast.37, s32[8]{0:T(128)S(1)} %copy-done.5, bf16[8,256,256]{2,1,0:T(8,128)(2,1)S(1)} %copy-done, bf16[8,256,256]{2,1,0:T(8,128)(2,1)S(1)} %copy-done.1, f32[8,128,128]{2,1,0:T(8,128)S(1)} %copy-done.2), custom_call_target="tpu_custom_call" | custom-call | flops 1000000000 | bytes 4000000 | tf_op jit(solution)/shard_map/diagonal_part/pallas_call | solution.py:289
  29.7 0.1 collective-permute-start.4
  29.9 0.0 copy-done.3
  29.9 0.0 copy-done.4
  29.9 3.4 %make_table.1 = s32[4,32]{1,0:T(4,128)S(1)} custom-call(s32[1]{0:T(128)} %bitcast.me.refs_4_, s32[8,6]{1,0:T(8,128)S(1)} %copy-done.3, s32[8,6]{1,0:T(8,128)S(1)} %copy-done.4, s32[8,6]{1,0:T(8,128)S(1)} %collective-permute-done.refs_2_, s32[8,6]{1,0:T(8,128)S(1)} %collective-permute-done.1.refs_3_), custom_call_target="tpu_custom_call" | custom-call | tf_op jit(solution)/shard_map/make_table/pallas_call | solution.py:245
  33.3 0.0 collective-permute-done.4
  33.4 1.4 %collective-permute-start.5 = (bf16[2,2,128,128]{3,2,1,0:T(8,128)(2,1)S(1)}, bf16[2,2,128,128]{3,2,1,0:T(8,128)(2,1)S(1)}, u32[]{:S(2)}, u32[]{:S(2)}) collective-permute-start(bf16[2,2,128,128]{3,2,1,0:T(8,128)(2,1)S(1)} %get-tuple-element.19), channel_id=1, source_target_pairs={{0,64},{32,96},{64,0},{96,32},{128,192},{160,224},{192,128},{224,1... | collective-permute-start | bytes 393224 | tf_op jit(solution)/shard_map/ppermute | solution.py:418
  34.8 1.7 %collective-permute-start.2 = (s32[2,1,32]{2,0,1:T(2,128)S(1)}, s32[2,1,32]{2,0,1:T(2,128)S(1)}, u32[]{:S(2)}, u32[]{:S(2)}) collective-permute-start(s32[2,1,32]{2,0,1:T(2,128)S(1)} %bitcast.52), channel_id=1, source_target_pairs={{0,1},{1,0},{2,3},{3,2},{4,5},{5,4},{6,7},{7,6},{8,9},{9,8},{10,11... | collective-permute-start | bytes 776 | tf_op jit(solution)/shard_map/ppermute | solution.py:418
  36.5 1.9 %collective-permute-done.2 = s32[2,1,32]{2,0,1:T(2,128)S(1)} collective-permute-done((s32[2,1,32]{2,0,1:T(2,128)S(1)}, s32[2,1,32]{2,0,1:T(2,128)S(1)}, u32[]{:S(2)}, u32[]{:S(2)}) %collective-permute-start.2) | collective-permute-done | bytes 288 | tf_op jit(solution)/shard_map/ppermute | solution.py:418
  38.4 0.8 collective-permute-done.5
  39.3 0.4 collective-permute-start.6
  39.7 3.2 %collective-permute-start.3 = (s32[1,2,32]{2,1,0:T(2,128)S(1)}, s32[1,2,32]{2,1,0:T(2,128)S(1)}, u32[]{:S(2)}, u32[]{:S(2)}) collective-permute-start(s32[1,2,32]{2,1,0:T(2,128)S(1)} %get-tuple-element.27), channel_id=1, source_target_pairs={{0,2},{1,3},{2,0},{3,1},{4,6},{5,7},{6,4},{7,5},{8,10},{9,11},{10,... | collective-permute-start | bytes 776 | tf_op jit(solution)/shard_map/ppermute | solution.py:418
  42.9 2.0 %collective-permute-done.3 = s32[1,2,32]{2,1,0:T(2,128)S(1)} collective-permute-done((s32[1,2,32]{2,1,0:T(2,128)S(1)}, s32[1,2,32]{2,1,0:T(2,128)S(1)}, u32[]{:S(2)}, u32[]{:S(2)}) %collective-permute-start.3) | collective-permute-done | bytes 288 | tf_op jit(solution)/shard_map/ppermute | solution.py:418
  44.9 1.0 collective-permute-done.6
  45.9 0.7 maximum_select_fusion.2
  46.7 0.1 copy.12
  46.7 0.1 copy.15
  46.8 0.1 copy.14
  46.9 0.1 copy.13
  47.0 0.1 copy.16.refs_0_
  47.1 2.6 %collective-permute-start.7 = (s32[4,4]{1,0:T(4,128)S(1)}, s32[4,4]{1,0:T(4,128)S(1)}, u32[]{:S(2)}, u32[]{:S(2)}) collective-permute-start(s32[4,4]{1,0:T(4,128)S(1)} %copy.13), channel_id=1, source_target_pairs={{0,8},{1,9},{2,10},{3,11},{4,12},{5,13},{6,14},{7,15},{8,0},{9,1},... | collective-permute-start | bytes 200 | tf_op jit(solution)/shard_map/ppermute | solution.py:459
  49.7 3.6 %collective-permute-start.8 = (s32[4,4]{1,0:T(4,128)S(1)}, s32[4,4]{1,0:T(4,128)S(1)}, u32[]{:S(2)}, u32[]{:S(2)}) collective-permute-start(s32[4,4]{1,0:T(4,128)S(1)} %copy.14), channel_id=1, source_target_pairs={{0,16},{1,17},{2,18},{3,19},{4,20},{5,21},{6,22},{7,23},{8,24},{9,... | collective-permute-start | bytes 200 | tf_op jit(solution)/shard_map/ppermute | solution.py:459
  53.3 0.3 collective-permute-start.9
  53.6 54.2 %collective-permute-done.7.refs_1_ = s32[4,4]{1,0:T(4,128)S(1)} collective-permute-done((s32[4,4]{1,0:T(4,128)S(1)}, s32[4,4]{1,0:T(4,128)S(1)}, u32[]{:S(2)}, u32[]{:S(2)}) %collective-permute-start.7) | collective-permute-done | bytes 96 | tf_op jit(solution)/shard_map/ppermute | solution.py:459
  107.8 7.9 %collective-permute-done.8.refs_2_ = s32[4,4]{1,0:T(4,128)S(1)} collective-permute-done((s32[4,4]{1,0:T(4,128)S(1)}, s32[4,4]{1,0:T(4,128)S(1)}, u32[]{:S(2)}, u32[]{:S(2)}) %collective-permute-start.8) | collective-permute-done | bytes 96 | tf_op jit(solution)/shard_map/ppermute | solution.py:459
  115.7 0.0 collective-permute-done.9.refs_3_
  115.7 0.0 all-to-all-done
  115.7 4.1 %reduce_blocks.1 = bf16[64,128,128]{2,1,0:T(8,128)(2,1)} custom-call(s32[4,4]{1,0:T(4,128)S(1)} %copy.16.refs_0_, s32[4,4]{1,0:T(4,128)S(1)} %collective-permute-done.7.refs_1_, s32[4,4]{1,0:T(4,128)S(1)} %collective-permute-done.8.refs_2_, s32[4,4]{1,0:T(4,128)S(1)} %collective-permute-done.9.refs_3_, s32[1]{0:T(128)} %bitcast.me.refs_4_, s32[8]{0:T(128)S(1)} %copy-done.5, ...), custom_call_target="tpu_custom_call" | custom-call | flops 600000000 | bytes 7000000 | tf_op jit(solution)/shard_map/reduce_blocks/pallas_call | solution.py:384
  (10 shorter events, 0.2 us)
Async XLA Ops:
  0.6 8.1 %collective-permute-start.1 = (s32[8,6]{1,0:T(8,128)}, s32[8,6]{1,0:T(8,128)S(1)}, u32[]{:S(2)}, u32[]{:S(2)}) collective-permute-start(s32[8,6]{1,0:T(8,128)} %refs_1_.1), channel_id=1, source_target_pairs={{0,4},{1,5},{2,6},{3,7},{4,0},{5,1},{6,2},{7,3},{8,12},{9,13},{10,... | collective-permute-start | bytes 584 | tf_op jit(solution)/shard_map/ppermute | solution.py:433
  2.6 6.1 %collective-permute-start = (s32[8,6]{1,0:T(8,128)}, s32[8,6]{1,0:T(8,128)S(1)}, u32[]{:S(2)}, u32[]{:S(2)}) collective-permute-start(s32[8,6]{1,0:T(8,128)} %refs_0_.1), channel_id=1, source_target_pairs={{0,4},{1,5},{2,6},{3,7},{4,0},{5,1},{6,2},{7,3},{8,12},{9,13},{10,... | collective-permute-start | bytes 584 | tf_op jit(solution)/shard_map/ppermute | solution.py:432
  8.8 11.7 %copy-start = (bf16[8,256,256]{2,1,0:T(8,128)(2,1)S(1)}, bf16[8,256,256]{2,1,0:T(8,128)(2,1)}, u32[]{:S(2)}) copy-start(bf16[8,256,256]{2,1,0:T(8,128)(2,1)} %basis_ref.1) | copy-start | bytes 3145732
  8.8 11.7 %copy-start.1 = (bf16[8,256,256]{2,1,0:T(8,128)(2,1)S(1)}, bf16[8,256,256]{2,1,0:T(8,128)(2,1)}, u32[]{:S(2)}) copy-start(bf16[8,256,256]{2,1,0:T(8,128)(2,1)} %diag_ref.1) | copy-start | bytes 3145732
  8.8 11.7 %copy-start.2 = (f32[8,128,128]{2,1,0:T(8,128)S(1)}, f32[8,128,128]{2,1,0:T(8,128)}, u32[]{:S(2)}) copy-start(f32[8,128,128]{2,1,0:T(8,128)} %inverse_ref.1) | copy-start | bytes 1572868
  8.8 11.7 %copy-start.5 = (s32[8]{0:T(128)S(1)}, s32[8]{0:T(128)}, u32[]{:S(2)}) copy-start(s32[8]{0:T(128)} %refs_5_.1) | copy-start | bytes 100
  8.8 11.7 %copy-start.6 = (s32[8,1]{0,1:T(1,128)S(1)}, s32[8,1]{0,1:T(1,128)}, u32[]{:S(2)}) copy-start(s32[8,1]{0,1:T(1,128)} %param.15) | copy-start | bytes 100
  8.8 106.9 %all-to-all-start = ((bf16[32,2,128,256]{3,2,1,0:T(8,128)(2,1)}), bf16[32,2,128,256]{3,2,1,0:T(8,128)(2,1)}, u32[]{:S(2)}, u32[]{:S(2)}) async-start(bf16[32,2,128,256]{3,2,1,0:T(8,128)(2,1)} %bitcast.38), calls=%async_computation | async-start | bytes 8388608 | tf_op jit(solution)/shard_map/all_to_all | solution.py:439
  20.5 9.5 %copy-start.3 = (s32[8,6]{1,0:T(8,128)S(1)}, s32[8,6]{1,0:T(8,128)}, u32[]{:S(2)}) copy-start(s32[8,6]{1,0:T(8,128)} %refs_0_.1) | copy-start | bytes 580
  20.5 9.4 %copy-start.4 = (s32[8,6]{1,0:T(8,128)S(1)}, s32[8,6]{1,0:T(8,128)}, u32[]{:S(2)}) copy-start(s32[8,6]{1,0:T(8,128)} %refs_1_.1) | copy-start | bytes 580
  29.7 3.7 %collective-permute-start.4 = (bf16[4,1,128,128]{3,2,0,1:T(8,128)(2,1)S(1)}, bf16[4,1,128,128]{3,2,0,1:T(8,128)(2,1)S(1)}, u32[]{:S(2)}, u32[]{:S(2)}) collective-permute-start(bf16[4,1,128,128]{3,2,0,1:T(8,128)(2,1)S(1)} %get-tuple-element.21), channel_id=1, source_target_pairs={{0,32},{32,0},{64,96},{96,64},{128,160},{160,128},{192,224},{224,1... | collective-permute-start | bytes 393224 | tf_op jit(solution)/shard_map/ppermute | solution.py:418
  33.4 5.8 %collective-permute-start.5 = (bf16[2,2,128,128]{3,2,1,0:T(8,128)(2,1)S(1)}, bf16[2,2,128,128]{3,2,1,0:T(8,128)(2,1)S(1)}, u32[]{:S(2)}, u32[]{:S(2)}) collective-permute-start(bf16[2,2,128,128]{3,2,1,0:T(8,128)(2,1)S(1)} %get-tuple-element.19), channel_id=1, source_target_pairs={{0,64},{32,96},{64,0},{96,32},{128,192},{160,224},{192,128},{224,1... | collective-permute-start | bytes 393224 | tf_op jit(solution)/shard_map/ppermute | solution.py:418
  34.8 3.6 %collective-permute-start.2 = (s32[2,1,32]{2,0,1:T(2,128)S(1)}, s32[2,1,32]{2,0,1:T(2,128)S(1)}, u32[]{:S(2)}, u32[]{:S(2)}) collective-permute-start(s32[2,1,32]{2,0,1:T(2,128)S(1)} %bitcast.52), channel_id=1, source_target_pairs={{0,1},{1,0},{2,3},{3,2},{4,5},{5,4},{6,7},{7,6},{8,9},{9,8},{10,11... | collective-permute-start | bytes 776 | tf_op jit(solution)/shard_map/ppermute | solution.py:418
  39.3 6.6 %collective-permute-start.6 = (bf16[1,4,128,128]{3,2,1,0:T(8,128)(2,1)S(1)}, bf16[1,4,128,128]{3,2,1,0:T(8,128)(2,1)S(1)}, u32[]{:S(2)}, u32[]{:S(2)}) collective-permute-start(bf16[1,4,128,128]{3,2,1,0:T(8,128)(2,1)S(1)} %get-tuple-element.17), channel_id=1, source_target_pairs={{0,128},{32,160},{64,192},{96,224},{128,0},{160,32},{192,64},{224,... | collective-permute-start | bytes 393224 | tf_op jit(solution)/shard_map/ppermute | solution.py:418
  39.7 5.2 %collective-permute-start.3 = (s32[1,2,32]{2,1,0:T(2,128)S(1)}, s32[1,2,32]{2,1,0:T(2,128)S(1)}, u32[]{:S(2)}, u32[]{:S(2)}) collective-permute-start(s32[1,2,32]{2,1,0:T(2,128)S(1)} %get-tuple-element.27), channel_id=1, source_target_pairs={{0,2},{1,3},{2,0},{3,1},{4,6},{5,7},{6,4},{7,5},{8,10},{9,11},{10,... | collective-permute-start | bytes 776 | tf_op jit(solution)/shard_map/ppermute | solution.py:418
  47.1 60.7 %collective-permute-start.7 = (s32[4,4]{1,0:T(4,128)S(1)}, s32[4,4]{1,0:T(4,128)S(1)}, u32[]{:S(2)}, u32[]{:S(2)}) collective-permute-start(s32[4,4]{1,0:T(4,128)S(1)} %copy.13), channel_id=1, source_target_pairs={{0,8},{1,9},{2,10},{3,11},{4,12},{5,13},{6,14},{7,15},{8,0},{9,1},... | collective-permute-start | bytes 200 | tf_op jit(solution)/shard_map/ppermute | solution.py:459
  49.7 66.0 %collective-permute-start.8 = (s32[4,4]{1,0:T(4,128)S(1)}, s32[4,4]{1,0:T(4,128)S(1)}, u32[]{:S(2)}, u32[]{:S(2)}) collective-permute-start(s32[4,4]{1,0:T(4,128)S(1)} %copy.14), channel_id=1, source_target_pairs={{0,16},{1,17},{2,18},{3,19},{4,20},{5,21},{6,22},{7,23},{8,24},{9,... | collective-permute-start | bytes 200 | tf_op jit(solution)/shard_map/ppermute | solution.py:459
  53.3 62.4 %collective-permute-start.9 = (s32[4,4]{1,0:T(4,128)S(1)}, s32[4,4]{1,0:T(4,128)S(1)}, u32[]{:S(2)}, u32[]{:S(2)}) collective-permute-start(s32[4,4]{1,0:T(4,128)S(1)} %copy.15), channel_id=1, source_target_pairs={{0,24},{1,25},{2,26},{3,27},{4,28},{5,29},{6,30},{7,31},{8,16},{9,... | collective-permute-start | bytes 200 | tf_op jit(solution)/shard_map/ppermute | solution.py:459

commit v5 on v4

--- a/solution.py
+++ b/solution.py
@@ -10,6 +10,7 @@
 BF16 = jnp.bfloat16
 F32 = jnp.float32
 CAPACITY = 2
+PIECE = 8
 NEAR_LINKS = 4
 HALF_Z = 4
 
@@ -135,11 +136,8 @@
             row = rows[c]
             for k in range(near_count):
                 moved[c, k] = jnp.where(keep, dot(row, near[c, k]), 0.0).astype(BF16)
-
-    def send_one(c, carry):
-        for k in range(near_count):
-            out_copy(c, k).start()
-        return carry
+            for k in range(near_count):
+                out_copy(c, k).start()
 
     def finish_one(c, carry):
         for k in range(near_count):
@@ -157,7 +155,6 @@
         move(g)
         if g + 1 < len(groups):
             prepare(g + 1)
-        lax.fori_loop(members[g][0], members[g][-1] + 1, send_one, 0)
     lax.fori_loop(0, local_count, finish_one, 0)
 
 
@@ -165,7 +162,7 @@
     local_count, near_count, block, _ = near_blocks.shape
     redundant = diag_inverses.shape[1]
     skeleton = block - redundant
-    groups = (2, 4, 2)
+    groups = (4, 4)
     hbm = pl.BlockSpec(memory_space=pl.ANY)
     dma = pltpu.SemaphoreType.DMA
     return pl.pallas_call(
@@ -348,7 +345,7 @@
         return pltpu.make_async_copy(moved_hbm.at[part], moved.at[part], in_sem.at[i])
 
     def out_copy(i):
-        part = pl.ds(i * chunk, chunk)
+        part = pl.ds(i * PIECE, PIECE)
         return pltpu.make_async_copy(out.at[part], out_hbm.at[part], out_sem.at[i])
 
     for copy in firsts:
@@ -370,8 +367,9 @@
             owner = jnp.maximum(local, 0)
             rank = jnp.where(local < 0, 0, ranks[owner])
             out[e] = jnp.where(cols_at < rank, dot(moved[e], col[owner]), 0.0).astype(BF16)
-        out_copy(i).start()
-    for i in range(steps):
+            if e % PIECE == PIECE - 1:
+                out_copy(e // PIECE).start()
+    for i in range(moved.shape[0] // PIECE):
         out_copy(i).wait()
 
 
@@ -396,7 +394,7 @@
             dma((far,)),
             dma((3,)),
             dma((slots // chunk,)),
-            dma((slots // chunk,)),
+            dma((slots // PIECE,)),
         ],
         compiler_params=pltpu.CompilerParams(vmem_limit_bytes=12 * 2**20),
         cost_estimate=pl.CostEstimate(

time: 120 us -> 119 us (level)
  no operation moved by 1% of the time
where the time goes in v5:
time: 119 us
  waiting for transfers between devices  67.8 us (57%)
  starting transfers between devices  27.1 us (23%)
  Pallas kernels  22.1 us (19%)
    ppermute x3, waiting for transfers between devices, on_device(): given = lax.ppermute(given, 'clu', pairs)  62.1 us
    all_to_all x1, starting transfers between devices, on_device(): lax.all_to_all(send.reshape(buckets, CAPACITY, skeleton, block), 'clu', 0...  11.6 us
    pallas_call x1, Pallas kernels, diagonal_part(): pl.pallas_call(diagonal_kernel, out_shape=(jax.ShapeDtypeStruct((local_co...  9.05 us
    ppermute x5, starting transfers between devices, swap_halves(): got = lax.ppermute(given, axis_name, [(i, i ^ bit) for i in range(whole)])  6.88 us
    ppermute x3, starting transfers between devices, on_device(): given = lax.ppermute(given, 'clu', pairs)  6.5 us
    pallas_call x1, Pallas kernels, move_blocks(): pl.pallas_call(functools.partial(move_kernel, near_count, groups), out_sh...  5.68 us
    ppermute x5, waiting for transfers between devices, swap_halves(): got = lax.ppermute(given, axis_name, [(i, i ^ bit) for i in range(whole)])  5.63 us
    pallas_call x1, Pallas kernels, reduce_blocks(): pl.pallas_call(functools.partial(reduce_kernel, chunk, far), out_shape=ja...  3.93 us
  transfers between devices with their start and end apart: 11, of which 6 were waited for; matrix products, arithmetic and copies ran while one was open for 1% of the time, Pallas kernels for 15%

profile of v5, /device:TPU:16, one launch (start us, length us, event | category | flops | bytes accessed | tf_op | source)
XLA Modules:
  0.0 119.3 jit_solution(15259837962638187076)
XLA Ops:
  0.6 2.0 %collective-permute-start.1 = (s32[8,6]{1,0:T(8,128)}, s32[8,6]{1,0:T(8,128)S(1)}, u32[]{:S(2)}, u32[]{:S(2)}) collective-permute-start(s32[8,6]{1,0:T(8,128)} %refs_1_.1), channel_id=1, source_target_pairs={{0,4},{1,5},{2,6},{3,7},{4,0},{5,1},{6,2},{7,3},{8,12},{9,13},{10,... | collective-permute-start | bytes 584 | tf_op jit(solution)/shard_map/ppermute | solution.py:431
  2.6 0.1 collective-permute-start
  2.7 5.7 %move_blocks.1 = bf16[64,128,256]{2,1,0:T(8,128)(2,1)} custom-call(s32[8,6]{1,0:T(8,128)} %refs_0_.1, s32[8]{0:T(128)} %refs_5_.1, bf16[8,256,256]{2,1,0:T(8,128)(2,1)} %basis_ref.1, bf16[8,256,256]{2,1,0:T(8,128)(2,1)} %diag_ref.1, f32[8,128,128]{2,1,0:T(8,128)} %inverse_ref.1, bf16[8,6,256,256]{3,2,1,0:T(8,128)(2,1)} %near_hbm.1), custom_call_target="tpu_custom_call" | custom-call | flops 2000000000 | bytes 13000000 | tf_op jit(solution)/shard_map/move_blocks/pallas_call | solution.py:168
  8.4 0.0 collective-permute-done.1.refs_3_
  8.4 0.0 collective-permute-done.refs_2_
  8.5 0.0 copy-start
  8.5 0.0 copy-start.1
  8.5 0.0 copy-start.2
  8.5 0.0 copy-start.5
  8.5 0.0 copy-start.6
  8.5 11.6 %all-to-all-start = ((bf16[32,2,128,256]{3,2,1,0:T(8,128)(2,1)}), bf16[32,2,128,256]{3,2,1,0:T(8,128)(2,1)}, u32[]{:S(2)}, u32[]{:S(2)}) async-start(bf16[32,2,128,256]{3,2,1,0:T(8,128)(2,1)} %bitcast.38), calls=%async_computation | async-start | bytes 8388608 | tf_op jit(solution)/shard_map/all_to_all | solution.py:437
  20.1 0.0 copy-start.3
  20.1 0.0 copy-start.4
  20.1 0.0 copy-done
  20.2 0.0 copy-done.1
  20.2 0.0 copy-done.2
  20.2 0.0 copy-done.5
  20.2 0.0 copy-done.6
  20.2 9.1 %diagonal_part.1 = (bf16[8,128,128]{2,1,0:T(8,128)(2,1)S(1)}, bf16[8,256,128]{2,1,0:T(8,128)(2,1)S(1)}) custom-call(s32[8]{0:T(128)S(1)} %bitcast.37, s32[8]{0:T(128)S(1)} %copy-done.5, bf16[8,256,256]{2,1,0:T(8,128)(2,1)S(1)} %copy-done, bf16[8,256,256]{2,1,0:T(8,128)(2,1)S(1)} %copy-done.1, f32[8,128,128]{2,1,0:T(8,128)S(1)} %copy-done.2), custom_call_target="tpu_custom_call" | custom-call | flops 1000000000 | bytes 4000000 | tf_op jit(solution)/shard_map/diagonal_part/pallas_call | solution.py:286
  29.3 0.1 collective-permute-start.4
  29.5 0.0 copy-done.3
  29.6 0.0 copy-done.4
  29.6 3.4 %make_table.1 = s32[4,32]{1,0:T(4,128)S(1)} custom-call(s32[1]{0:T(128)} %bitcast.me.refs_4_, s32[8,6]{1,0:T(8,128)S(1)} %copy-done.3, s32[8,6]{1,0:T(8,128)S(1)} %copy-done.4, s32[8,6]{1,0:T(8,128)S(1)} %collective-permute-done.refs_2_, s32[8,6]{1,0:T(8,128)S(1)} %collective-permute-done.1.refs_3_), custom_call_target="tpu_custom_call" | custom-call | tf_op jit(solution)/shard_map/make_table/pallas_call | solution.py:242
  33.0 0.0 collective-permute-done.4
  33.0 1.4 %collective-permute-start.5 = (bf16[2,2,128,128]{3,2,1,0:T(8,128)(2,1)S(1)}, bf16[2,2,128,128]{3,2,1,0:T(8,128)(2,1)S(1)}, u32[]{:S(2)}, u32[]{:S(2)}) collective-permute-start(bf16[2,2,128,128]{3,2,1,0:T(8,128)(2,1)S(1)} %get-tuple-element.19), channel_id=1, source_target_pairs={{0,64},{32,96},{64,0},{96,32},{128,192},{160,224},{192,128},{224,1... | collective-permute-start | bytes 393224 | tf_op jit(solution)/shard_map/ppermute | solution.py:416
  34.4 1.7 %collective-permute-start.2 = (s32[2,1,32]{2,0,1:T(2,128)S(1)}, s32[2,1,32]{2,0,1:T(2,128)S(1)}, u32[]{:S(2)}, u32[]{:S(2)}) collective-permute-start(s32[2,1,32]{2,0,1:T(2,128)S(1)} %bitcast.52), channel_id=1, source_target_pairs={{0,1},{1,0},{2,3},{3,2},{4,5},{5,4},{6,7},{7,6},{8,9},{9,8},{10,11... | collective-permute-start | bytes 776 | tf_op jit(solution)/shard_map/ppermute | solution.py:416
  36.1 1.9 %collective-permute-done.2 = s32[2,1,32]{2,0,1:T(2,128)S(1)} collective-permute-done((s32[2,1,32]{2,0,1:T(2,128)S(1)}, s32[2,1,32]{2,0,1:T(2,128)S(1)}, u32[]{:S(2)}, u32[]{:S(2)}) %collective-permute-start.2) | collective-permute-done | bytes 288 | tf_op jit(solution)/shard_map/ppermute | solution.py:416
  38.0 0.8 collective-permute-done.5
  38.9 0.5 collective-permute-start.6
  39.4 3.2 %collective-permute-start.3 = (s32[1,2,32]{2,1,0:T(2,128)S(1)}, s32[1,2,32]{2,1,0:T(2,128)S(1)}, u32[]{:S(2)}, u32[]{:S(2)}) collective-permute-start(s32[1,2,32]{2,1,0:T(2,128)S(1)} %get-tuple-element.27), channel_id=1, source_target_pairs={{0,2},{1,3},{2,0},{3,1},{4,6},{5,7},{6,4},{7,5},{8,10},{9,11},{10,... | collective-permute-start | bytes 776 | tf_op jit(solution)/shard_map/ppermute | solution.py:416
  42.6 1.9 %collective-permute-done.3 = s32[1,2,32]{2,1,0:T(2,128)S(1)} collective-permute-done((s32[1,2,32]{2,1,0:T(2,128)S(1)}, s32[1,2,32]{2,1,0:T(2,128)S(1)}, u32[]{:S(2)}, u32[]{:S(2)}) %collective-permute-start.3) | collective-permute-done | bytes 288 | tf_op jit(solution)/shard_map/ppermute | solution.py:416
  44.6 1.0 collective-permute-done.6
  45.6 0.7 maximum_select_fusion.2
  46.3 0.1 copy.12
  46.4 0.1 copy.15
  46.5 0.1 copy.14
  46.6 0.1 copy.13
  46.7 0.1 copy.16.refs_0_
  46.8 2.6 %collective-permute-start.7 = (s32[4,4]{1,0:T(4,128)S(1)}, s32[4,4]{1,0:T(4,128)S(1)}, u32[]{:S(2)}, u32[]{:S(2)}) collective-permute-start(s32[4,4]{1,0:T(4,128)S(1)} %copy.13), channel_id=1, source_target_pairs={{0,8},{1,9},{2,10},{3,11},{4,12},{5,13},{6,14},{7,15},{8,0},{9,1},... | collective-permute-start | bytes 200 | tf_op jit(solution)/shard_map/ppermute | solution.py:457
  49.4 3.6 %collective-permute-start.8 = (s32[4,4]{1,0:T(4,128)S(1)}, s32[4,4]{1,0:T(4,128)S(1)}, u32[]{:S(2)}, u32[]{:S(2)}) collective-permute-start(s32[4,4]{1,0:T(4,128)S(1)} %copy.14), channel_id=1, source_target_pairs={{0,16},{1,17},{2,18},{3,19},{4,20},{5,21},{6,22},{7,23},{8,24},{9,... | collective-permute-start | bytes 200 | tf_op jit(solution)/shard_map/ppermute | solution.py:457
  53.0 0.3 collective-permute-start.9
  53.2 54.2 %collective-permute-done.7.refs_1_ = s32[4,4]{1,0:T(4,128)S(1)} collective-permute-done((s32[4,4]{1,0:T(4,128)S(1)}, s32[4,4]{1,0:T(4,128)S(1)}, u32[]{:S(2)}, u32[]{:S(2)}) %collective-permute-start.7) | collective-permute-done | bytes 96 | tf_op jit(solution)/shard_map/ppermute | solution.py:457
  107.5 7.9 %collective-permute-done.8.refs_2_ = s32[4,4]{1,0:T(4,128)S(1)} collective-permute-done((s32[4,4]{1,0:T(4,128)S(1)}, s32[4,4]{1,0:T(4,128)S(1)}, u32[]{:S(2)}, u32[]{:S(2)}) %collective-permute-start.8) | collective-permute-done | bytes 96 | tf_op jit(solution)/shard_map/ppermute | solution.py:457
  115.4 0.0 collective-permute-done.9.refs_3_
  115.4 0.0 all-to-all-done
  115.4 3.9 %reduce_blocks.1 = bf16[64,128,128]{2,1,0:T(8,128)(2,1)} custom-call(s32[4,4]{1,0:T(4,128)S(1)} %copy.16.refs_0_, s32[4,4]{1,0:T(4,128)S(1)} %collective-permute-done.7.refs_1_, s32[4,4]{1,0:T(4,128)S(1)} %collective-permute-done.8.refs_2_, s32[4,4]{1,0:T(4,128)S(1)} %collective-permute-done.9.refs_3_, s32[1]{0:T(128)} %bitcast.me.refs_4_, s32[8]{0:T(128)S(1)} %copy-done.5, ...), custom_call_target="tpu_custom_call" | custom-call | flops 600000000 | bytes 7000000 | tf_op jit(solution)/shard_map/reduce_blocks/pallas_call | solution.py:382
  (10 shorter events, 0.2 us)
Async XLA Ops:
  0.6 7.8 %collective-permute-start.1 = (s32[8,6]{1,0:T(8,128)}, s32[8,6]{1,0:T(8,128)S(1)}, u32[]{:S(2)}, u32[]{:S(2)}) collective-permute-start(s32[8,6]{1,0:T(8,128)} %refs_1_.1), channel_id=1, source_target_pairs={{0,4},{1,5},{2,6},{3,7},{4,0},{5,1},{6,2},{7,3},{8,12},{9,13},{10,... | collective-permute-start | bytes 584 | tf_op jit(solution)/shard_map/ppermute | solution.py:431
  2.6 5.8 %collective-permute-start = (s32[8,6]{1,0:T(8,128)}, s32[8,6]{1,0:T(8,128)S(1)}, u32[]{:S(2)}, u32[]{:S(2)}) collective-permute-start(s32[8,6]{1,0:T(8,128)} %refs_0_.1), channel_id=1, source_target_pairs={{0,4},{1,5},{2,6},{3,7},{4,0},{5,1},{6,2},{7,3},{8,12},{9,13},{10,... | collective-permute-start | bytes 584 | tf_op jit(solution)/shard_map/ppermute | solution.py:430
  8.5 11.7 %copy-start = (bf16[8,256,256]{2,1,0:T(8,128)(2,1)S(1)}, bf16[8,256,256]{2,1,0:T(8,128)(2,1)}, u32[]{:S(2)}) copy-start(bf16[8,256,256]{2,1,0:T(8,128)(2,1)} %basis_ref.1) | copy-start | bytes 3145732
  8.5 11.7 %copy-start.1 = (bf16[8,256,256]{2,1,0:T(8,128)(2,1)S(1)}, bf16[8,256,256]{2,1,0:T(8,128)(2,1)}, u32[]{:S(2)}) copy-start(bf16[8,256,256]{2,1,0:T(8,128)(2,1)} %diag_ref.1) | copy-start | bytes 3145732
  8.5 11.7 %copy-start.2 = (f32[8,128,128]{2,1,0:T(8,128)S(1)}, f32[8,128,128]{2,1,0:T(8,128)}, u32[]{:S(2)}) copy-start(f32[8,128,128]{2,1,0:T(8,128)} %inverse_ref.1) | copy-start | bytes 1572868
  8.5 11.7 %copy-start.5 = (s32[8]{0:T(128)S(1)}, s32[8]{0:T(128)}, u32[]{:S(2)}) copy-start(s32[8]{0:T(128)} %refs_5_.1) | copy-start | bytes 100
  8.5 11.7 %copy-start.6 = (s32[8,1]{0,1:T(1,128)S(1)}, s32[8,1]{0,1:T(1,128)}, u32[]{:S(2)}) copy-start(s32[8,1]{0,1:T(1,128)} %param.15) | copy-start | bytes 100
  8.5 106.9 %all-to-all-start = ((bf16[32,2,128,256]{3,2,1,0:T(8,128)(2,1)}), bf16[32,2,128,256]{3,2,1,0:T(8,128)(2,1)}, u32[]{:S(2)}, u32[]{:S(2)}) async-start(bf16[32,2,128,256]{3,2,1,0:T(8,128)(2,1)} %bitcast.38), calls=%async_computation | async-start | bytes 8388608 | tf_op jit(solution)/shard_map/all_to_all | solution.py:437
  20.1 9.4 %copy-start.3 = (s32[8,6]{1,0:T(8,128)S(1)}, s32[8,6]{1,0:T(8,128)}, u32[]{:S(2)}) copy-start(s32[8,6]{1,0:T(8,128)} %refs_0_.1) | copy-start | bytes 580
  20.1 9.4 %copy-start.4 = (s32[8,6]{1,0:T(8,128)S(1)}, s32[8,6]{1,0:T(8,128)}, u32[]{:S(2)}) copy-start(s32[8,6]{1,0:T(8,128)} %refs_1_.1) | copy-start | bytes 580
  29.3 3.7 %collective-permute-start.4 = (bf16[4,1,128,128]{3,2,0,1:T(8,128)(2,1)S(1)}, bf16[4,1,128,128]{3,2,0,1:T(8,128)(2,1)S(1)}, u32[]{:S(2)}, u32[]{:S(2)}) collective-permute-start(bf16[4,1,128,128]{3,2,0,1:T(8,128)(2,1)S(1)} %get-tuple-element.21), channel_id=1, source_target_pairs={{0,32},{32,0},{64,96},{96,64},{128,160},{160,128},{192,224},{224,1... | collective-permute-start | bytes 393224 | tf_op jit(solution)/shard_map/ppermute | solution.py:416
  33.0 5.8 %collective-permute-start.5 = (bf16[2,2,128,128]{3,2,1,0:T(8,128)(2,1)S(1)}, bf16[2,2,128,128]{3,2,1,0:T(8,128)(2,1)S(1)}, u32[]{:S(2)}, u32[]{:S(2)}) collective-permute-start(bf16[2,2,128,128]{3,2,1,0:T(8,128)(2,1)S(1)} %get-tuple-element.19), channel_id=1, source_target_pairs={{0,64},{32,96},{64,0},{96,32},{128,192},{160,224},{192,128},{224,1... | collective-permute-start | bytes 393224 | tf_op jit(solution)/shard_map/ppermute | solution.py:416
  34.4 3.6 %collective-permute-start.2 = (s32[2,1,32]{2,0,1:T(2,128)S(1)}, s32[2,1,32]{2,0,1:T(2,128)S(1)}, u32[]{:S(2)}, u32[]{:S(2)}) collective-permute-start(s32[2,1,32]{2,0,1:T(2,128)S(1)} %bitcast.52), channel_id=1, source_target_pairs={{0,1},{1,0},{2,3},{3,2},{4,5},{5,4},{6,7},{7,6},{8,9},{9,8},{10,11... | collective-permute-start | bytes 776 | tf_op jit(solution)/shard_map/ppermute | solution.py:416
  38.9 6.6 %collective-permute-start.6 = (bf16[1,4,128,128]{3,2,1,0:T(8,128)(2,1)S(1)}, bf16[1,4,128,128]{3,2,1,0:T(8,128)(2,1)S(1)}, u32[]{:S(2)}, u32[]{:S(2)}) collective-permute-start(bf16[1,4,128,128]{3,2,1,0:T(8,128)(2,1)S(1)} %get-tuple-element.17), channel_id=1, source_target_pairs={{0,128},{32,160},{64,192},{96,224},{128,0},{160,32},{192,64},{224,... | collective-permute-start | bytes 393224 | tf_op jit(solution)/shard_map/ppermute | solution.py:416
  39.4 5.1 %collective-permute-start.3 = (s32[1,2,32]{2,1,0:T(2,128)S(1)}, s32[1,2,32]{2,1,0:T(2,128)S(1)}, u32[]{:S(2)}, u32[]{:S(2)}) collective-permute-start(s32[1,2,32]{2,1,0:T(2,128)S(1)} %get-tuple-element.27), channel_id=1, source_target_pairs={{0,2},{1,3},{2,0},{3,1},{4,6},{5,7},{6,4},{7,5},{8,10},{9,11},{10,... | collective-permute-start | bytes 776 | tf_op jit(solution)/shard_map/ppermute | solution.py:416
  46.8 60.7 %collective-permute-start.7 = (s32[4,4]{1,0:T(4,128)S(1)}, s32[4,4]{1,0:T(4,128)S(1)}, u32[]{:S(2)}, u32[]{:S(2)}) collective-permute-start(s32[4,4]{1,0:T(4,128)S(1)} %copy.13), channel_id=1, source_target_pairs={{0,8},{1,9},{2,10},{3,11},{4,12},{5,13},{6,14},{7,15},{8,0},{9,1},... | collective-permute-start | bytes 200 | tf_op jit(solution)/shard_map/ppermute | solution.py:457
  49.4 66.0 %collective-permute-start.8 = (s32[4,4]{1,0:T(4,128)S(1)}, s32[4,4]{1,0:T(4,128)S(1)}, u32[]{:S(2)}, u32[]{:S(2)}) collective-permute-start(s32[4,4]{1,0:T(4,128)S(1)} %copy.14), channel_id=1, source_target_pairs={{0,16},{1,17},{2,18},{3,19},{4,20},{5,21},{6,22},{7,23},{8,24},{9,... | collective-permute-start | bytes 200 | tf_op jit(solution)/shard_map/ppermute | solution.py:457
  53.0 62.4 %collective-permute-start.9 = (s32[4,4]{1,0:T(4,128)S(1)}, s32[4,4]{1,0:T(4,128)S(1)}, u32[]{:S(2)}, u32[]{:S(2)}) collective-permute-start(s32[4,4]{1,0:T(4,128)S(1)} %copy.15), channel_id=1, source_target_pairs={{0,24},{1,25},{2,26},{3,27},{4,28},{5,29},{6,30},{7,31},{8,16},{9,... | collective-permute-start | bytes 200 | tf_op jit(solution)/shard_map/ppermute | solution.py:457

commit v6 on v5

--- a/solution.py
+++ b/solution.py
@@ -318,13 +318,12 @@
         me_hbm,
         ranks_hbm,
         moved_hbm,
-        col_hbm,
+        col,
         out_hbm,
         tables,
         me,
         ranks,
         moved,
-        col,
         out,
         table_sem,
         int_sem,
@@ -335,7 +334,6 @@
     firsts = (
         pltpu.make_async_copy(me_hbm, me, int_sem.at[0]),
         pltpu.make_async_copy(ranks_hbm, ranks, int_sem.at[1]),
-        pltpu.make_async_copy(col_hbm, col, int_sem.at[2]),
     ) + tuple(
         pltpu.make_async_copy(tables_hbm[t], tables.at[t], table_sem.at[t]) for t in range(far)
     )
@@ -382,17 +380,16 @@
     return pl.pallas_call(
         functools.partial(reduce_kernel, chunk, far),
         out_shape=jax.ShapeDtypeStruct((slots, skeleton, skeleton), BF16),
-        in_specs=[hbm] * (far + 4),
+        in_specs=[hbm] * (far + 3) + [pl.BlockSpec(memory_space=pltpu.VMEM)],
         out_specs=hbm,
         scratch_shapes=[
             pltpu.SMEM((far,) + tables[0].shape, jnp.int32),
             pltpu.SMEM((1,), jnp.int32),
             pltpu.SMEM(ranks.shape, jnp.int32),
             pltpu.VMEM(moved.shape, BF16),
-            pltpu.VMEM(col_basis.shape, BF16),
             pltpu.VMEM((slots, skeleton, skeleton), BF16),
             dma((far,)),
-            dma((3,)),
+            dma((2,)),
             dma((slots // chunk,)),
             dma((slots // PIECE,)),
         ],

time: 119 us -> 119 us (level)
  no operation moved by 1% of the time
where the time goes in v6:
time: 119 us
  waiting for transfers between devices  67.9 us (57%)
  starting transfers between devices  27 us (23%)
  Pallas kernels  22 us (18%)
    ppermute x3, waiting for transfers between devices, on_device(): given = lax.ppermute(given, 'clu', pairs)  62.2 us
    all_to_all x1, starting transfers between devices, on_device(): lax.all_to_all(send.reshape(buckets, CAPACITY, skeleton, block), 'clu', 0...  11.6 us
    pallas_call x1, Pallas kernels, diagonal_part(): pl.pallas_call(diagonal_kernel, out_shape=(jax.ShapeDtypeStruct((local_co...  9.06 us
    ppermute x5, starting transfers between devices, swap_halves(): got = lax.ppermute(given, axis_name, [(i, i ^ bit) for i in range(whole)])  6.79 us
    ppermute x3, starting transfers between devices, on_device(): given = lax.ppermute(given, 'clu', pairs)  6.5 us
    ppermute x5, waiting for transfers between devices, swap_halves(): got = lax.ppermute(given, axis_name, [(i, i ^ bit) for i in range(whole)])  5.73 us
    pallas_call x1, Pallas kernels, move_blocks(): pl.pallas_call(functools.partial(move_kernel, near_count, groups), out_sh...  5.71 us
    pallas_call x1, Pallas kernels, reduce_blocks(): pl.pallas_call(functools.partial(reduce_kernel, chunk, far), out_shape=ja...  3.88 us
  transfers between devices with their start and end apart: 11, of which 6 were waited for; matrix products, arithmetic and copies ran while one was open for 1% of the time, Pallas kernels for 15%

profile of v6, /device:TPU:16, one launch (start us, length us, event | category | flops | bytes accessed | tf_op | source)
XLA Modules:
  0.0 119.3 jit_solution(8248835134972204227)
XLA Ops:
  0.6 2.0 %collective-permute-start.1 = (s32[8,6]{1,0:T(8,128)}, s32[8,6]{1,0:T(8,128)S(1)}, u32[]{:S(2)}, u32[]{:S(2)}) collective-permute-start(s32[8,6]{1,0:T(8,128)} %refs_1_.1), channel_id=1, source_target_pairs={{0,4},{1,5},{2,6},{3,7},{4,0},{5,1},{6,2},{7,3},{8,12},{9,13},{10,... | collective-permute-start | bytes 584 | tf_op jit(solution)/shard_map/ppermute | solution.py:428
  2.6 0.1 collective-permute-start
  2.7 5.7 %move_blocks.1 = bf16[64,128,256]{2,1,0:T(8,128)(2,1)} custom-call(s32[8,6]{1,0:T(8,128)} %refs_0_.1, s32[8]{0:T(128)} %refs_5_.1, bf16[8,256,256]{2,1,0:T(8,128)(2,1)} %basis_ref.1, bf16[8,256,256]{2,1,0:T(8,128)(2,1)} %diag_ref.1, f32[8,128,128]{2,1,0:T(8,128)} %inverse_ref.1, bf16[8,6,256,256]{3,2,1,0:T(8,128)(2,1)} %near_hbm.1), custom_call_target="tpu_custom_call" | custom-call | flops 2000000000 | bytes 13000000 | tf_op jit(solution)/shard_map/move_blocks/pallas_call | solution.py:168
  8.5 0.0 collective-permute-done.1.refs_3_
  8.5 0.0 collective-permute-done.refs_2_
  8.5 0.0 copy-start
  8.5 0.0 copy-start.1
  8.5 0.0 copy-start.2
  8.5 0.0 copy-start.5
  8.5 0.0 copy-start.6
  8.5 11.6 %all-to-all-start = ((bf16[32,2,128,256]{3,2,1,0:T(8,128)(2,1)}), bf16[32,2,128,256]{3,2,1,0:T(8,128)(2,1)}, u32[]{:S(2)}, u32[]{:S(2)}) async-start(bf16[32,2,128,256]{3,2,1,0:T(8,128)(2,1)} %bitcast.38), calls=%async_computation | async-start | bytes 8388608 | tf_op jit(solution)/shard_map/all_to_all | solution.py:434
  20.1 0.0 copy-start.3
  20.1 0.0 copy-start.4
  20.2 0.0 copy-done
  20.2 0.0 copy-done.1
  20.2 0.0 copy-done.2
  20.2 0.0 copy-done.5
  20.2 0.0 copy-done.6
  20.2 9.1 %diagonal_part.1 = (bf16[8,128,128]{2,1,0:T(8,128)(2,1)S(1)}, bf16[8,256,128]{2,1,0:T(8,128)(2,1)S(1)}) custom-call(s32[8]{0:T(128)S(1)} %bitcast.37, s32[8]{0:T(128)S(1)} %copy-done.5, bf16[8,256,256]{2,1,0:T(8,128)(2,1)S(1)} %copy-done, bf16[8,256,256]{2,1,0:T(8,128)(2,1)S(1)} %copy-done.1, f32[8,128,128]{2,1,0:T(8,128)S(1)} %copy-done.2), custom_call_target="tpu_custom_call" | custom-call | flops 1000000000 | bytes 4000000 | tf_op jit(solution)/shard_map/diagonal_part/pallas_call | solution.py:286
  29.3 0.1 collective-permute-start.4
  29.6 0.0 copy-done.3
  29.6 0.0 copy-done.4
  29.6 3.4 %make_table.1 = s32[4,32]{1,0:T(4,128)S(1)} custom-call(s32[1]{0:T(128)} %bitcast.me.refs_4_, s32[8,6]{1,0:T(8,128)S(1)} %copy-done.3, s32[8,6]{1,0:T(8,128)S(1)} %copy-done.4, s32[8,6]{1,0:T(8,128)S(1)} %collective-permute-done.refs_2_, s32[8,6]{1,0:T(8,128)S(1)} %collective-permute-done.1.refs_3_), custom_call_target="tpu_custom_call" | custom-call | tf_op jit(solution)/shard_map/make_table/pallas_call | solution.py:242
  33.0 0.0 collective-permute-done.4
  33.1 1.3 %collective-permute-start.5 = (bf16[2,2,128,128]{3,2,1,0:T(8,128)(2,1)S(1)}, bf16[2,2,128,128]{3,2,1,0:T(8,128)(2,1)S(1)}, u32[]{:S(2)}, u32[]{:S(2)}) collective-permute-start(bf16[2,2,128,128]{3,2,1,0:T(8,128)(2,1)S(1)} %get-tuple-element.19), channel_id=1, source_target_pairs={{0,64},{32,96},{64,0},{96,32},{128,192},{160,224},{192,128},{224,1... | collective-permute-start | bytes 393224 | tf_op jit(solution)/shard_map/ppermute | solution.py:413
  34.4 1.7 %collective-permute-start.2 = (s32[2,1,32]{2,0,1:T(2,128)S(1)}, s32[2,1,32]{2,0,1:T(2,128)S(1)}, u32[]{:S(2)}, u32[]{:S(2)}) collective-permute-start(s32[2,1,32]{2,0,1:T(2,128)S(1)} %bitcast.52), channel_id=1, source_target_pairs={{0,1},{1,0},{2,3},{3,2},{4,5},{5,4},{6,7},{7,6},{8,9},{9,8},{10,11... | collective-permute-start | bytes 776 | tf_op jit(solution)/shard_map/ppermute | solution.py:413
  36.1 1.9 %collective-permute-done.2 = s32[2,1,32]{2,0,1:T(2,128)S(1)} collective-permute-done((s32[2,1,32]{2,0,1:T(2,128)S(1)}, s32[2,1,32]{2,0,1:T(2,128)S(1)}, u32[]{:S(2)}, u32[]{:S(2)}) %collective-permute-start.2) | collective-permute-done | bytes 288 | tf_op jit(solution)/shard_map/ppermute | solution.py:413
  38.0 0.9 collective-permute-done.5
  39.0 0.4 collective-permute-start.6
  39.4 3.2 %collective-permute-start.3 = (s32[1,2,32]{2,1,0:T(2,128)S(1)}, s32[1,2,32]{2,1,0:T(2,128)S(1)}, u32[]{:S(2)}, u32[]{:S(2)}) collective-permute-start(s32[1,2,32]{2,1,0:T(2,128)S(1)} %get-tuple-element.27), channel_id=1, source_target_pairs={{0,2},{1,3},{2,0},{3,1},{4,6},{5,7},{6,4},{7,5},{8,10},{9,11},{10,... | collective-permute-start | bytes 776 | tf_op jit(solution)/shard_map/ppermute | solution.py:413
  42.6 1.9 %collective-permute-done.3 = s32[1,2,32]{2,1,0:T(2,128)S(1)} collective-permute-done((s32[1,2,32]{2,1,0:T(2,128)S(1)}, s32[1,2,32]{2,1,0:T(2,128)S(1)}, u32[]{:S(2)}, u32[]{:S(2)}) %collective-permute-start.3) | collective-permute-done | bytes 288 | tf_op jit(solution)/shard_map/ppermute | solution.py:413
  44.5 1.1 collective-permute-done.6
  45.6 0.7 maximum_select_fusion.2
  46.3 0.1 copy.12
  46.4 0.1 copy.15
  46.5 0.1 copy.14
  46.6 0.1 copy.13
  46.7 0.1 copy.16.refs_0_
  46.8 2.6 %collective-permute-start.7 = (s32[4,4]{1,0:T(4,128)S(1)}, s32[4,4]{1,0:T(4,128)S(1)}, u32[]{:S(2)}, u32[]{:S(2)}) collective-permute-start(s32[4,4]{1,0:T(4,128)S(1)} %copy.13), channel_id=1, source_target_pairs={{0,8},{1,9},{2,10},{3,11},{4,12},{5,13},{6,14},{7,15},{8,0},{9,1},... | collective-permute-start | bytes 200 | tf_op jit(solution)/shard_map/ppermute | solution.py:454
  49.4 3.6 %collective-permute-start.8 = (s32[4,4]{1,0:T(4,128)S(1)}, s32[4,4]{1,0:T(4,128)S(1)}, u32[]{:S(2)}, u32[]{:S(2)}) collective-permute-start(s32[4,4]{1,0:T(4,128)S(1)} %copy.14), channel_id=1, source_target_pairs={{0,16},{1,17},{2,18},{3,19},{4,20},{5,21},{6,22},{7,23},{8,24},{9,... | collective-permute-start | bytes 200 | tf_op jit(solution)/shard_map/ppermute | solution.py:454
  53.0 0.3 collective-permute-start.9
  53.3 54.2 %collective-permute-done.7.refs_1_ = s32[4,4]{1,0:T(4,128)S(1)} collective-permute-done((s32[4,4]{1,0:T(4,128)S(1)}, s32[4,4]{1,0:T(4,128)S(1)}, u32[]{:S(2)}, u32[]{:S(2)}) %collective-permute-start.7) | collective-permute-done | bytes 96 | tf_op jit(solution)/shard_map/ppermute | solution.py:454
  107.5 8.0 %collective-permute-done.8.refs_2_ = s32[4,4]{1,0:T(4,128)S(1)} collective-permute-done((s32[4,4]{1,0:T(4,128)S(1)}, s32[4,4]{1,0:T(4,128)S(1)}, u32[]{:S(2)}, u32[]{:S(2)}) %collective-permute-start.8) | collective-permute-done | bytes 96 | tf_op jit(solution)/shard_map/ppermute | solution.py:454
  115.5 0.0 collective-permute-done.9.refs_3_
  115.5 0.0 all-to-all-done
  115.5 3.9 %reduce_blocks.1 = bf16[64,128,128]{2,1,0:T(8,128)(2,1)} custom-call(s32[4,4]{1,0:T(4,128)S(1)} %copy.16.refs_0_, s32[4,4]{1,0:T(4,128)S(1)} %collective-permute-done.7.refs_1_, s32[4,4]{1,0:T(4,128)S(1)} %collective-permute-done.8.refs_2_, s32[4,4]{1,0:T(4,128)S(1)} %collective-permute-done.9.refs_3_, s32[1]{0:T(128)} %bitcast.me.refs_4_, s32[8]{0:T(128)S(1)} %copy-done.5, ...), custom_call_target="tpu_custom_call" | custom-call | flops 600000000 | bytes 7000000 | tf_op jit(solution)/shard_map/reduce_blocks/pallas_call | solution.py:380
  (10 shorter events, 0.2 us)
Async XLA Ops:
  0.6 7.8 %collective-permute-start.1 = (s32[8,6]{1,0:T(8,128)}, s32[8,6]{1,0:T(8,128)S(1)}, u32[]{:S(2)}, u32[]{:S(2)}) collective-permute-start(s32[8,6]{1,0:T(8,128)} %refs_1_.1), channel_id=1, source_target_pairs={{0,4},{1,5},{2,6},{3,7},{4,0},{5,1},{6,2},{7,3},{8,12},{9,13},{10,... | collective-permute-start | bytes 584 | tf_op jit(solution)/shard_map/ppermute | solution.py:428
  2.6 5.8 %collective-permute-start = (s32[8,6]{1,0:T(8,128)}, s32[8,6]{1,0:T(8,128)S(1)}, u32[]{:S(2)}, u32[]{:S(2)}) collective-permute-start(s32[8,6]{1,0:T(8,128)} %refs_0_.1), channel_id=1, source_target_pairs={{0,4},{1,5},{2,6},{3,7},{4,0},{5,1},{6,2},{7,3},{8,12},{9,13},{10,... | collective-permute-start | bytes 584 | tf_op jit(solution)/shard_map/ppermute | solution.py:427
  8.5 11.7 %copy-start = (bf16[8,256,256]{2,1,0:T(8,128)(2,1)S(1)}, bf16[8,256,256]{2,1,0:T(8,128)(2,1)}, u32[]{:S(2)}) copy-start(bf16[8,256,256]{2,1,0:T(8,128)(2,1)} %basis_ref.1) | copy-start | bytes 3145732
  8.5 11.7 %copy-start.1 = (bf16[8,256,256]{2,1,0:T(8,128)(2,1)S(1)}, bf16[8,256,256]{2,1,0:T(8,128)(2,1)}, u32[]{:S(2)}) copy-start(bf16[8,256,256]{2,1,0:T(8,128)(2,1)} %diag_ref.1) | copy-start | bytes 3145732
  8.5 11.7 %copy-start.2 = (f32[8,128,128]{2,1,0:T(8,128)S(1)}, f32[8,128,128]{2,1,0:T(8,128)}, u32[]{:S(2)}) copy-start(f32[8,128,128]{2,1,0:T(8,128)} %inverse_ref.1) | copy-start | bytes 1572868
  8.5 11.7 %copy-start.5 = (s32[8]{0:T(128)S(1)}, s32[8]{0:T(128)}, u32[]{:S(2)}) copy-start(s32[8]{0:T(128)} %refs_5_.1) | copy-start | bytes 100
  8.5 11.7 %copy-start.6 = (s32[8,1]{0,1:T(1,128)S(1)}, s32[8,1]{0,1:T(1,128)}, u32[]{:S(2)}) copy-start(s32[8,1]{0,1:T(1,128)} %param.15) | copy-start | bytes 100
  8.5 106.9 %all-to-all-start = ((bf16[32,2,128,256]{3,2,1,0:T(8,128)(2,1)}), bf16[32,2,128,256]{3,2,1,0:T(8,128)(2,1)}, u32[]{:S(2)}, u32[]{:S(2)}) async-start(bf16[32,2,128,256]{3,2,1,0:T(8,128)(2,1)} %bitcast.38), calls=%async_computation | async-start | bytes 8388608 | tf_op jit(solution)/shard_map/all_to_all | solution.py:434
  20.1 9.4 %copy-start.3 = (s32[8,6]{1,0:T(8,128)S(1)}, s32[8,6]{1,0:T(8,128)}, u32[]{:S(2)}) copy-start(s32[8,6]{1,0:T(8,128)} %refs_0_.1) | copy-start | bytes 580
  20.1 9.4 %copy-start.4 = (s32[8,6]{1,0:T(8,128)S(1)}, s32[8,6]{1,0:T(8,128)}, u32[]{:S(2)}) copy-start(s32[8,6]{1,0:T(8,128)} %refs_1_.1) | copy-start | bytes 580
  29.3 3.7 %collective-permute-start.4 = (bf16[4,1,128,128]{3,2,0,1:T(8,128)(2,1)S(1)}, bf16[4,1,128,128]{3,2,0,1:T(8,128)(2,1)S(1)}, u32[]{:S(2)}, u32[]{:S(2)}) collective-permute-start(bf16[4,1,128,128]{3,2,0,1:T(8,128)(2,1)S(1)} %get-tuple-element.21), channel_id=1, source_target_pairs={{0,32},{32,0},{64,96},{96,64},{128,160},{160,128},{192,224},{224,1... | collective-permute-start | bytes 393224 | tf_op jit(solution)/shard_map/ppermute | solution.py:413
  33.1 5.8 %collective-permute-start.5 = (bf16[2,2,128,128]{3,2,1,0:T(8,128)(2,1)S(1)}, bf16[2,2,128,128]{3,2,1,0:T(8,128)(2,1)S(1)}, u32[]{:S(2)}, u32[]{:S(2)}) collective-permute-start(bf16[2,2,128,128]{3,2,1,0:T(8,128)(2,1)S(1)} %get-tuple-element.19), channel_id=1, source_target_pairs={{0,64},{32,96},{64,0},{96,32},{128,192},{160,224},{192,128},{224,1... | collective-permute-start | bytes 393224 | tf_op jit(solution)/shard_map/ppermute | solution.py:413
  34.4 3.6 %collective-permute-start.2 = (s32[2,1,32]{2,0,1:T(2,128)S(1)}, s32[2,1,32]{2,0,1:T(2,128)S(1)}, u32[]{:S(2)}, u32[]{:S(2)}) collective-permute-start(s32[2,1,32]{2,0,1:T(2,128)S(1)} %bitcast.52), channel_id=1, source_target_pairs={{0,1},{1,0},{2,3},{3,2},{4,5},{5,4},{6,7},{7,6},{8,9},{9,8},{10,11... | collective-permute-start | bytes 776 | tf_op jit(solution)/shard_map/ppermute | solution.py:413
  39.0 6.6 %collective-permute-start.6 = (bf16[1,4,128,128]{3,2,1,0:T(8,128)(2,1)S(1)}, bf16[1,4,128,128]{3,2,1,0:T(8,128)(2,1)S(1)}, u32[]{:S(2)}, u32[]{:S(2)}) collective-permute-start(bf16[1,4,128,128]{3,2,1,0:T(8,128)(2,1)S(1)} %get-tuple-element.17), channel_id=1, source_target_pairs={{0,128},{32,160},{64,192},{96,224},{128,0},{160,32},{192,64},{224,... | collective-permute-start | bytes 393224 | tf_op jit(solution)/shard_map/ppermute | solution.py:413
  39.4 5.1 %collective-permute-start.3 = (s32[1,2,32]{2,1,0:T(2,128)S(1)}, s32[1,2,32]{2,1,0:T(2,128)S(1)}, u32[]{:S(2)}, u32[]{:S(2)}) collective-permute-start(s32[1,2,32]{2,1,0:T(2,128)S(1)} %get-tuple-element.27), channel_id=1, source_target_pairs={{0,2},{1,3},{2,0},{3,1},{4,6},{5,7},{6,4},{7,5},{8,10},{9,11},{10,... | collective-permute-start | bytes 776 | tf_op jit(solution)/shard_map/ppermute | solution.py:413
  46.8 60.7 %collective-permute-start.7 = (s32[4,4]{1,0:T(4,128)S(1)}, s32[4,4]{1,0:T(4,128)S(1)}, u32[]{:S(2)}, u32[]{:S(2)}) collective-permute-start(s32[4,4]{1,0:T(4,128)S(1)} %copy.13), channel_id=1, source_target_pairs={{0,8},{1,9},{2,10},{3,11},{4,12},{5,13},{6,14},{7,15},{8,0},{9,1},... | collective-permute-start | bytes 200 | tf_op jit(solution)/shard_map/ppermute | solution.py:454
  49.4 66.0 %collective-permute-start.8 = (s32[4,4]{1,0:T(4,128)S(1)}, s32[4,4]{1,0:T(4,128)S(1)}, u32[]{:S(2)}, u32[]{:S(2)}) collective-permute-start(s32[4,4]{1,0:T(4,128)S(1)} %copy.14), channel_id=1, source_target_pairs={{0,16},{1,17},{2,18},{3,19},{4,20},{5,21},{6,22},{7,23},{8,24},{9,... | collective-permute-start | bytes 200 | tf_op jit(solution)/shard_map/ppermute | solution.py:454
  53.0 62.4 %collective-permute-start.9 = (s32[4,4]{1,0:T(4,128)S(1)}, s32[4,4]{1,0:T(4,128)S(1)}, u32[]{:S(2)}, u32[]{:S(2)}) collective-permute-start(s32[4,4]{1,0:T(4,128)S(1)} %copy.15), channel_id=1, source_target_pairs={{0,24},{1,25},{2,26},{3,27},{4,28},{5,29},{6,30},{7,31},{8,16},{9,... | collective-permute-start | bytes 200 | tf_op jit(solution)/shard_map/ppermute | solution.py:454

commit v7 on v5

--- a/solution.py
+++ b/solution.py
@@ -448,14 +448,14 @@
     table, merged = lax.optimization_barrier((table, merged))
     table = table[:, : 2 * HALF_Z * CAPACITY].reshape(NEAR_LINKS, 2, HALF_Z, CAPACITY)
     my_place = me // (2 * NEAR_LINKS)
-    tables = []
-    for apart in range(HALF_Z):
+    tables = [None] * HALF_Z
+    for apart in (2, 3, 1, 0):
         given = lax.dynamic_index_in_dim(table, my_place ^ apart, 2, keepdims=False)
         given = given.reshape(NEAR_LINKS, 2 * CAPACITY)
         if apart:
             pairs = [(i, i ^ (2 * apart * NEAR_LINKS)) for i in range(buckets)]
             given = lax.ppermute(given, "clu", pairs)
-        tables.append(given)
+        tables[apart] = given
     reduced = reduce_blocks(
         received.reshape(buckets * CAPACITY, skeleton, block), tables, me, col_basis, ranks
     )

time: 119 us -> 119 us (level)
  no operation moved by 1% of the time
where the time goes in v7:
time: 119 us
  waiting for transfers between devices  67.8 us (57%)
  starting transfers between devices  27 us (23%)
  Pallas kernels  22.1 us (19%)
    ppermute x3, waiting for transfers between devices, on_device(): given = lax.ppermute(given, 'clu', pairs)  62.2 us
    all_to_all x1, starting transfers between devices, on_device(): lax.all_to_all(send.reshape(buckets, CAPACITY, skeleton, block), 'clu', 0...  11.5 us
    pallas_call x1, Pallas kernels, diagonal_part(): pl.pallas_call(diagonal_kernel, out_shape=(jax.ShapeDtypeStruct((local_co...  9.06 us
    ppermute x5, starting transfers between devices, swap_halves(): got = lax.ppermute(given, axis_name, [(i, i ^ bit) for i in range(whole)])  6.89 us
    ppermute x3, starting transfers between devices, on_device(): given = lax.ppermute(given, 'clu', pairs)  6.5 us
    pallas_call x1, Pallas kernels, move_blocks(): pl.pallas_call(functools.partial(move_kernel, near_count, groups), out_sh...  5.76 us
    ppermute x5, waiting for transfers between devices, swap_halves(): got = lax.ppermute(given, axis_name, [(i, i ^ bit) for i in range(whole)])  5.63 us
    pallas_call x1, Pallas kernels, reduce_blocks(): pl.pallas_call(functools.partial(reduce_kernel, chunk, far), out_shape=ja...  3.93 us
  transfers between devices with their start and end apart: 11, of which 6 were waited for; matrix products, arithmetic and copies ran while one was open for 1% of the time, Pallas kernels for 15%

profile of v7, /device:TPU:16, one launch (start us, length us, event | category | flops | bytes accessed | tf_op | source)
XLA Modules:
  0.0 119.3 jit_solution(15259837962638187076)
XLA Ops:
  0.6 2.0 %collective-permute-start.1 = (s32[8,6]{1,0:T(8,128)}, s32[8,6]{1,0:T(8,128)S(1)}, u32[]{:S(2)}, u32[]{:S(2)}) collective-permute-start(s32[8,6]{1,0:T(8,128)} %refs_1_.1), channel_id=1, source_target_pairs={{0,4},{1,5},{2,6},{3,7},{4,0},{5,1},{6,2},{7,3},{8,12},{9,13},{10,... | collective-permute-start | bytes 584 | tf_op jit(solution)/shard_map/ppermute | solution.py:431
  2.6 0.1 collective-permute-start
  2.7 5.8 %move_blocks.1 = bf16[64,128,256]{2,1,0:T(8,128)(2,1)} custom-call(s32[8,6]{1,0:T(8,128)} %refs_0_.1, s32[8]{0:T(128)} %refs_5_.1, bf16[8,256,256]{2,1,0:T(8,128)(2,1)} %basis_ref.1, bf16[8,256,256]{2,1,0:T(8,128)(2,1)} %diag_ref.1, f32[8,128,128]{2,1,0:T(8,128)} %inverse_ref.1, bf16[8,6,256,256]{3,2,1,0:T(8,128)(2,1)} %near_hbm.1), custom_call_target="tpu_custom_call" | custom-call | flops 2000000000 | bytes 13000000 | tf_op jit(solution)/shard_map/move_blocks/pallas_call | solution.py:168
  8.5 0.0 collective-permute-done.1.refs_3_
  8.5 0.0 collective-permute-done.refs_2_
  8.5 0.0 copy-start
  8.5 0.0 copy-start.1
  8.6 0.0 copy-start.2
  8.6 0.0 copy-start.5
  8.6 0.0 copy-start.6
  8.6 11.5 %all-to-all-start = ((bf16[32,2,128,256]{3,2,1,0:T(8,128)(2,1)}), bf16[32,2,128,256]{3,2,1,0:T(8,128)(2,1)}, u32[]{:S(2)}, u32[]{:S(2)}) async-start(bf16[32,2,128,256]{3,2,1,0:T(8,128)(2,1)} %bitcast.38), calls=%async_computation | async-start | bytes 8388608 | tf_op jit(solution)/shard_map/all_to_all | solution.py:437
  20.1 0.0 copy-start.3
  20.1 0.0 copy-start.4
  20.1 0.0 copy-done
  20.1 0.0 copy-done.1
  20.1 0.0 copy-done.2
  20.2 0.0 copy-done.5
  20.2 0.0 copy-done.6
  20.2 9.1 %diagonal_part.1 = (bf16[8,128,128]{2,1,0:T(8,128)(2,1)S(1)}, bf16[8,256,128]{2,1,0:T(8,128)(2,1)S(1)}) custom-call(s32[8]{0:T(128)S(1)} %bitcast.37, s32[8]{0:T(128)S(1)} %copy-done.5, bf16[8,256,256]{2,1,0:T(8,128)(2,1)S(1)} %copy-done, bf16[8,256,256]{2,1,0:T(8,128)(2,1)S(1)} %copy-done.1, f32[8,128,128]{2,1,0:T(8,128)S(1)} %copy-done.2), custom_call_target="tpu_custom_call" | custom-call | flops 1000000000 | bytes 4000000 | tf_op jit(solution)/shard_map/diagonal_part/pallas_call | solution.py:286
  29.3 0.1 collective-permute-start.4
  29.5 0.0 copy-done.3
  29.5 0.0 copy-done.4
  29.5 3.4 %make_table.1 = s32[4,32]{1,0:T(4,128)S(1)} custom-call(s32[1]{0:T(128)} %bitcast.me.refs_4_, s32[8,6]{1,0:T(8,128)S(1)} %copy-done.3, s32[8,6]{1,0:T(8,128)S(1)} %copy-done.4, s32[8,6]{1,0:T(8,128)S(1)} %collective-permute-done.refs_2_, s32[8,6]{1,0:T(8,128)S(1)} %collective-permute-done.1.refs_3_), custom_call_target="tpu_custom_call" | custom-call | tf_op jit(solution)/shard_map/make_table/pallas_call | solution.py:242
  32.9 0.0 collective-permute-done.4
  33.0 1.4 %collective-permute-start.5 = (bf16[2,2,128,128]{3,2,1,0:T(8,128)(2,1)S(1)}, bf16[2,2,128,128]{3,2,1,0:T(8,128)(2,1)S(1)}, u32[]{:S(2)}, u32[]{:S(2)}) collective-permute-start(bf16[2,2,128,128]{3,2,1,0:T(8,128)(2,1)S(1)} %get-tuple-element.19), channel_id=1, source_target_pairs={{0,64},{32,96},{64,0},{96,32},{128,192},{160,224},{192,128},{224,1... | collective-permute-start | bytes 393224 | tf_op jit(solution)/shard_map/ppermute | solution.py:416
  34.4 1.7 %collective-permute-start.2 = (s32[2,1,32]{2,0,1:T(2,128)S(1)}, s32[2,1,32]{2,0,1:T(2,128)S(1)}, u32[]{:S(2)}, u32[]{:S(2)}) collective-permute-start(s32[2,1,32]{2,0,1:T(2,128)S(1)} %bitcast.52), channel_id=1, source_target_pairs={{0,1},{1,0},{2,3},{3,2},{4,5},{5,4},{6,7},{7,6},{8,9},{9,8},{10,11... | collective-permute-start | bytes 776 | tf_op jit(solution)/shard_map/ppermute | solution.py:416
  36.1 1.9 %collective-permute-done.2 = s32[2,1,32]{2,0,1:T(2,128)S(1)} collective-permute-done((s32[2,1,32]{2,0,1:T(2,128)S(1)}, s32[2,1,32]{2,0,1:T(2,128)S(1)}, u32[]{:S(2)}, u32[]{:S(2)}) %collective-permute-start.2) | collective-permute-done | bytes 288 | tf_op jit(solution)/shard_map/ppermute | solution.py:416
  38.0 0.8 collective-permute-done.5
  38.9 0.5 collective-permute-start.6
  39.4 3.2 %collective-permute-start.3 = (s32[1,2,32]{2,1,0:T(2,128)S(1)}, s32[1,2,32]{2,1,0:T(2,128)S(1)}, u32[]{:S(2)}, u32[]{:S(2)}) collective-permute-start(s32[1,2,32]{2,1,0:T(2,128)S(1)} %get-tuple-element.27), channel_id=1, source_target_pairs={{0,2},{1,3},{2,0},{3,1},{4,6},{5,7},{6,4},{7,5},{8,10},{9,11},{10,... | collective-permute-start | bytes 776 | tf_op jit(solution)/shard_map/ppermute | solution.py:416
  42.6 1.9 %collective-permute-done.3 = s32[1,2,32]{2,1,0:T(2,128)S(1)} collective-permute-done((s32[1,2,32]{2,1,0:T(2,128)S(1)}, s32[1,2,32]{2,1,0:T(2,128)S(1)}, u32[]{:S(2)}, u32[]{:S(2)}) %collective-permute-start.3) | collective-permute-done | bytes 288 | tf_op jit(solution)/shard_map/ppermute | solution.py:416
  44.5 1.0 collective-permute-done.6
  45.5 0.7 maximum_select_fusion.2
  46.3 0.1 copy.12
  46.4 0.1 copy.15
  46.5 0.1 copy.14
  46.5 0.1 copy.13
  46.6 0.1 copy.16.refs_0_
  46.7 2.6 %collective-permute-start.7 = (s32[4,4]{1,0:T(4,128)S(1)}, s32[4,4]{1,0:T(4,128)S(1)}, u32[]{:S(2)}, u32[]{:S(2)}) collective-permute-start(s32[4,4]{1,0:T(4,128)S(1)} %copy.13), channel_id=1, source_target_pairs={{0,8},{1,9},{2,10},{3,11},{4,12},{5,13},{6,14},{7,15},{8,0},{9,1},... | collective-permute-start | bytes 200 | tf_op jit(solution)/shard_map/ppermute | solution.py:457
  49.4 3.6 %collective-permute-start.8 = (s32[4,4]{1,0:T(4,128)S(1)}, s32[4,4]{1,0:T(4,128)S(1)}, u32[]{:S(2)}, u32[]{:S(2)}) collective-permute-start(s32[4,4]{1,0:T(4,128)S(1)} %copy.14), channel_id=1, source_target_pairs={{0,16},{1,17},{2,18},{3,19},{4,20},{5,21},{6,22},{7,23},{8,24},{9,... | collective-permute-start | bytes 200 | tf_op jit(solution)/shard_map/ppermute | solution.py:457
  53.0 0.3 collective-permute-start.9
  53.2 54.2 %collective-permute-done.7.refs_1_ = s32[4,4]{1,0:T(4,128)S(1)} collective-permute-done((s32[4,4]{1,0:T(4,128)S(1)}, s32[4,4]{1,0:T(4,128)S(1)}, u32[]{:S(2)}, u32[]{:S(2)}) %collective-permute-start.7) | collective-permute-done | bytes 96 | tf_op jit(solution)/shard_map/ppermute | solution.py:457
  107.4 8.0 %collective-permute-done.8.refs_2_ = s32[4,4]{1,0:T(4,128)S(1)} collective-permute-done((s32[4,4]{1,0:T(4,128)S(1)}, s32[4,4]{1,0:T(4,128)S(1)}, u32[]{:S(2)}, u32[]{:S(2)}) %collective-permute-start.8) | collective-permute-done | bytes 96 | tf_op jit(solution)/shard_map/ppermute | solution.py:457
  115.4 0.0 collective-permute-done.9.refs_3_
  115.4 0.0 all-to-all-done
  115.4 3.9 %reduce_blocks.1 = bf16[64,128,128]{2,1,0:T(8,128)(2,1)} custom-call(s32[4,4]{1,0:T(4,128)S(1)} %copy.16.refs_0_, s32[4,4]{1,0:T(4,128)S(1)} %collective-permute-done.7.refs_1_, s32[4,4]{1,0:T(4,128)S(1)} %collective-permute-done.8.refs_2_, s32[4,4]{1,0:T(4,128)S(1)} %collective-permute-done.9.refs_3_, s32[1]{0:T(128)} %bitcast.me.refs_4_, s32[8]{0:T(128)S(1)} %copy-done.5, ...), custom_call_target="tpu_custom_call" | custom-call | flops 600000000 | bytes 7000000 | tf_op jit(solution)/shard_map/reduce_blocks/pallas_call | solution.py:382
  (10 shorter events, 0.2 us)
Async XLA Ops:
  0.6 7.9 %collective-permute-start.1 = (s32[8,6]{1,0:T(8,128)}, s32[8,6]{1,0:T(8,128)S(1)}, u32[]{:S(2)}, u32[]{:S(2)}) collective-permute-start(s32[8,6]{1,0:T(8,128)} %refs_1_.1), channel_id=1, source_target_pairs={{0,4},{1,5},{2,6},{3,7},{4,0},{5,1},{6,2},{7,3},{8,12},{9,13},{10,... | collective-permute-start | bytes 584 | tf_op jit(solution)/shard_map/ppermute | solution.py:431
  2.6 5.9 %collective-permute-start = (s32[8,6]{1,0:T(8,128)}, s32[8,6]{1,0:T(8,128)S(1)}, u32[]{:S(2)}, u32[]{:S(2)}) collective-permute-start(s32[8,6]{1,0:T(8,128)} %refs_0_.1), channel_id=1, source_target_pairs={{0,4},{1,5},{2,6},{3,7},{4,0},{5,1},{6,2},{7,3},{8,12},{9,13},{10,... | collective-permute-start | bytes 584 | tf_op jit(solution)/shard_map/ppermute | solution.py:430
  8.5 11.6 %copy-start = (bf16[8,256,256]{2,1,0:T(8,128)(2,1)S(1)}, bf16[8,256,256]{2,1,0:T(8,128)(2,1)}, u32[]{:S(2)}) copy-start(bf16[8,256,256]{2,1,0:T(8,128)(2,1)} %basis_ref.1) | copy-start | bytes 3145732
  8.5 11.6 %copy-start.1 = (bf16[8,256,256]{2,1,0:T(8,128)(2,1)S(1)}, bf16[8,256,256]{2,1,0:T(8,128)(2,1)}, u32[]{:S(2)}) copy-start(bf16[8,256,256]{2,1,0:T(8,128)(2,1)} %diag_ref.1) | copy-start | bytes 3145732
  8.6 11.6 %copy-start.2 = (f32[8,128,128]{2,1,0:T(8,128)S(1)}, f32[8,128,128]{2,1,0:T(8,128)}, u32[]{:S(2)}) copy-start(f32[8,128,128]{2,1,0:T(8,128)} %inverse_ref.1) | copy-start | bytes 1572868
  8.6 11.6 %copy-start.5 = (s32[8]{0:T(128)S(1)}, s32[8]{0:T(128)}, u32[]{:S(2)}) copy-start(s32[8]{0:T(128)} %refs_5_.1) | copy-start | bytes 100
  8.6 11.6 %copy-start.6 = (s32[8,1]{0,1:T(1,128)S(1)}, s32[8,1]{0,1:T(1,128)}, u32[]{:S(2)}) copy-start(s32[8,1]{0,1:T(1,128)} %param.15) | copy-start | bytes 100
  8.6 106.8 %all-to-all-start = ((bf16[32,2,128,256]{3,2,1,0:T(8,128)(2,1)}), bf16[32,2,128,256]{3,2,1,0:T(8,128)(2,1)}, u32[]{:S(2)}, u32[]{:S(2)}) async-start(bf16[32,2,128,256]{3,2,1,0:T(8,128)(2,1)} %bitcast.38), calls=%async_computation | async-start | bytes 8388608 | tf_op jit(solution)/shard_map/all_to_all | solution.py:437
  20.1 9.5 %copy-start.3 = (s32[8,6]{1,0:T(8,128)S(1)}, s32[8,6]{1,0:T(8,128)}, u32[]{:S(2)}) copy-start(s32[8,6]{1,0:T(8,128)} %refs_0_.1) | copy-start | bytes 580
  20.1 9.5 %copy-start.4 = (s32[8,6]{1,0:T(8,128)S(1)}, s32[8,6]{1,0:T(8,128)}, u32[]{:S(2)}) copy-start(s32[8,6]{1,0:T(8,128)} %refs_1_.1) | copy-start | bytes 580
  29.3 3.7 %collective-permute-start.4 = (bf16[4,1,128,128]{3,2,0,1:T(8,128)(2,1)S(1)}, bf16[4,1,128,128]{3,2,0,1:T(8,128)(2,1)S(1)}, u32[]{:S(2)}, u32[]{:S(2)}) collective-permute-start(bf16[4,1,128,128]{3,2,0,1:T(8,128)(2,1)S(1)} %get-tuple-element.21), channel_id=1, source_target_pairs={{0,32},{32,0},{64,96},{96,64},{128,160},{160,128},{192,224},{224,1... | collective-permute-start | bytes 393224 | tf_op jit(solution)/shard_map/ppermute | solution.py:416
  33.0 5.8 %collective-permute-start.5 = (bf16[2,2,128,128]{3,2,1,0:T(8,128)(2,1)S(1)}, bf16[2,2,128,128]{3,2,1,0:T(8,128)(2,1)S(1)}, u32[]{:S(2)}, u32[]{:S(2)}) collective-permute-start(bf16[2,2,128,128]{3,2,1,0:T(8,128)(2,1)S(1)} %get-tuple-element.19), channel_id=1, source_target_pairs={{0,64},{32,96},{64,0},{96,32},{128,192},{160,224},{192,128},{224,1... | collective-permute-start | bytes 393224 | tf_op jit(solution)/shard_map/ppermute | solution.py:416
  34.4 3.6 %collective-permute-start.2 = (s32[2,1,32]{2,0,1:T(2,128)S(1)}, s32[2,1,32]{2,0,1:T(2,128)S(1)}, u32[]{:S(2)}, u32[]{:S(2)}) collective-permute-start(s32[2,1,32]{2,0,1:T(2,128)S(1)} %bitcast.52), channel_id=1, source_target_pairs={{0,1},{1,0},{2,3},{3,2},{4,5},{5,4},{6,7},{7,6},{8,9},{9,8},{10,11... | collective-permute-start | bytes 776 | tf_op jit(solution)/shard_map/ppermute | solution.py:416
  38.9 6.6 %collective-permute-start.6 = (bf16[1,4,128,128]{3,2,1,0:T(8,128)(2,1)S(1)}, bf16[1,4,128,128]{3,2,1,0:T(8,128)(2,1)S(1)}, u32[]{:S(2)}, u32[]{:S(2)}) collective-permute-start(bf16[1,4,128,128]{3,2,1,0:T(8,128)(2,1)S(1)} %get-tuple-element.17), channel_id=1, source_target_pairs={{0,128},{32,160},{64,192},{96,224},{128,0},{160,32},{192,64},{224,... | collective-permute-start | bytes 393224 | tf_op jit(solution)/shard_map/ppermute | solution.py:416
  39.4 5.1 %collective-permute-start.3 = (s32[1,2,32]{2,1,0:T(2,128)S(1)}, s32[1,2,32]{2,1,0:T(2,128)S(1)}, u32[]{:S(2)}, u32[]{:S(2)}) collective-permute-start(s32[1,2,32]{2,1,0:T(2,128)S(1)} %get-tuple-element.27), channel_id=1, source_target_pairs={{0,2},{1,3},{2,0},{3,1},{4,6},{5,7},{6,4},{7,5},{8,10},{9,11},{10,... | collective-permute-start | bytes 776 | tf_op jit(solution)/shard_map/ppermute | solution.py:416
  46.7 60.7 %collective-permute-start.7 = (s32[4,4]{1,0:T(4,128)S(1)}, s32[4,4]{1,0:T(4,128)S(1)}, u32[]{:S(2)}, u32[]{:S(2)}) collective-permute-start(s32[4,4]{1,0:T(4,128)S(1)} %copy.13), channel_id=1, source_target_pairs={{0,8},{1,9},{2,10},{3,11},{4,12},{5,13},{6,14},{7,15},{8,0},{9,1},... | collective-permute-start | bytes 200 | tf_op jit(solution)/shard_map/ppermute | solution.py:457
  49.4 66.1 %collective-permute-start.8 = (s32[4,4]{1,0:T(4,128)S(1)}, s32[4,4]{1,0:T(4,128)S(1)}, u32[]{:S(2)}, u32[]{:S(2)}) collective-permute-start(s32[4,4]{1,0:T(4,128)S(1)} %copy.14), channel_id=1, source_target_pairs={{0,16},{1,17},{2,18},{3,19},{4,20},{5,21},{6,22},{7,23},{8,24},{9,... | collective-permute-start | bytes 200 | tf_op jit(solution)/shard_map/ppermute | solution.py:457
  53.0 62.4 %collective-permute-start.9 = (s32[4,4]{1,0:T(4,128)S(1)}, s32[4,4]{1,0:T(4,128)S(1)}, u32[]{:S(2)}, u32[]{:S(2)}) collective-permute-start(s32[4,4]{1,0:T(4,128)S(1)} %copy.15), channel_id=1, source_target_pairs={{0,24},{1,25},{2,26},{3,27},{4,28},{5,29},{6,30},{7,31},{8,16},{9,... | collective-permute-start | bytes 200 | tf_op jit(solution)/shard_map/ppermute | solution.py:457
